TPU v7x, 32 devices: a whole 2x2x4 slice. The times are simulated.
32 devices in a mesh: parts: 2 (over y), lat: 4 (over z), fsdp: 2 (over x), sub: 2 (over core).
Axes of the slice: x: 2, y: 2, z: 4, core: 2. Of those that a mesh axis runs over, the one named last changes fastest.
Arguments:
- grid_input_channels: bfloat16 [8, 2, 227, 4096], P(('parts', 'lat'), 'sub', None, 'fsdp'), parts along dimension 0, may hold values from -6 to 6
- cotangent: bfloat16 [8, 2, 512, 4096], P(('parts', 'lat'), 'sub', 'fsdp'), parts along dimension 0
- frozen_input_weight: bfloat16 [227, 512], replicated, may hold values from -0.375 to 0.375
- frozen_output_weight: bfloat16 [512, 512], replicated, may hold values from -0.25 to 0.25
- adapter_down_weight: bfloat16 [454, 16], P('parts'), parts along dimension 0, may hold values from -0.375 to 0.375
- adapter_up_weight: bfloat16 [32, 512], P('parts'), parts along dimension 0, may hold values from -1.5 to 1.5
- interp: bfloat16 [4, 2, 96, 128, 128], P('lat', 'sub'), may hold values from -0.1875 to 0.1875
- nonzero_block_rows: int32 [4, 2, 96], P('lat', 'sub'), may hold values from 0 to 11, as said below
- nonzero_block_columns: int32 [4, 2, 96], P('lat', 'sub'), may hold values from 0 to 255, as said below
- grid_block_storage: int32 [256], replicated, may hold values from 0 to 255, as said below
Outputs:
- decoded: bfloat16 [8, 2, 512, 4096], P(('parts', 'lat'), 'sub', 'fsdp'), parts along dimension 0
- grad_down: float32 [454, 16], P('parts'), parts along dimension 0
- up_gradient: float32 [32, 512], P('parts'), parts along dimension 0
There are 2 independent parts, one for each index of `parts`. A program takes and returns all parts, laid end to end along the dimension named above; an argument that names none is the same for every part. Nothing has to cross between parts.
Inputs may be any that keep to these rules, and one draw needn't show every extreme that they name: Each number once; grid block b is stored as block grid_block_storage[b] % 32 of tile half grid_block_storage[b] // 32. `nonzero_block_columns`: within each tile half, at most 16 slots read grid blocks stored by any one tile half; in every draw exactly 16 slots of every tile half read grid blocks stored by one and the same tile half. `nonzero_block_rows`: within each tile half every mesh block has exactly 8 slots.
All inputs are finite; a program needn't handle non-finite values.
Results may differ from a plain program's by a relative error of at most 0.0083.
Values may be sent and summed in bfloat16 or wider, within the bound.
No kernel may reach another device: no remote copies, remote signals or barrier semaphores. Data moves between devices by JAX's collectives and lax.ppermute only.
A program may use at most 192 MiB of HBM per device.

v0:
```python
import jax
import jax.numpy as jnp
from jax import lax
from jax.sharding import PartitionSpec as P

MBLK = 12


def contract_leading_axes(left, right):
    return lax.dot_general(
        left, right, (((0,), (0,)), ((), ())), preferred_element_type=jnp.float32
    )


def contract_trailing_axes(left, right):
    return lax.dot_general(
        left, right, (((1,), (1,)), ((), ())), preferred_element_type=jnp.float32
    )


def bucket_slots(places, grid_count, pair_count, capacity):
    owner = places // grid_count
    local = places % grid_count
    owner_marks = (owner[..., None] == jnp.arange(pair_count, dtype=jnp.int32)).astype(jnp.int32)
    before = jnp.cumsum(owner_marks, axis=-2) - owner_marks
    rank = jnp.sum(before * owner_marks, axis=-1)
    return (owner, local, owner * capacity + rank)


def move_panels(first, second):
    return (
        lax.all_to_all(first, ("lat", "sub"), split_axis=1, concat_axis=1, tiled=True),
        lax.all_to_all(second, ("lat", "sub"), split_axis=1, concat_axis=1, tiled=True),
    )


def move_sums(first, second):
    return (
        lax.all_to_all(first, ("lat", "sub"), split_axis=1, concat_axis=1, tiled=True),
        lax.all_to_all(second, ("lat", "sub"), split_axis=1, concat_axis=1, tiled=True),
    )


def body(
    grid_input_channels,
    cotangent,
    frozen_input_weight,
    frozen_output_weight,
    adapter_down_weight,
    adapter_up_weight,
    interp,
    nonzero_block_rows,
    nonzero_block_columns,
    grid_block_storage,
):
    in_width, rows_dev = (grid_input_channels.shape[2], grid_input_channels.shape[3])
    feature_rows = grid_input_channels.reshape(in_width, rows_dev)
    adapter_middle_state = contract_leading_axes(adapter_down_weight, feature_rows).astype(
        jnp.bfloat16
    )
    preactivation_values = contract_leading_axes(
        frozen_input_weight, feature_rows
    ) + contract_leading_axes(adapter_up_weight, adapter_middle_state)
    hidden = jax.nn.silu(preactivation_values).astype(jnp.bfloat16)
    raw_out = contract_leading_axes(frozen_output_weight, hidden)
    center = raw_out - jnp.mean(raw_out, axis=0, keepdims=True)
    inv_std = lax.rsqrt(jnp.mean(center * center, axis=0, keepdims=True) + 1e-05)
    normed = center * inv_std
    embedded = normed.astype(jnp.bfloat16)
    grid_chan = lax.all_to_all(embedded, "fsdp", split_axis=0, concat_axis=1, tiled=True)
    channels, grid_rows = grid_chan.shape
    slot_count, block = (interp.shape[2], interp.shape[3])
    values = interp.reshape(slot_count, block, block)
    grid_count = grid_rows // block
    pair_count = lax.axis_size("lat") * lax.axis_size("sub")
    capacity = max(2, (4 * slot_count + 3 * pair_count - 1) // (3 * pair_count))
    places = jnp.take(grid_block_storage, nonzero_block_columns.reshape(slot_count))
    owner, local, flat = bucket_slots(places, grid_count, pair_count, capacity)
    wanted = jnp.full((pair_count * capacity,), grid_count, jnp.int32).at[flat].set(local)
    requests = lax.all_to_all(
        wanted.reshape(pair_count, capacity),
        ("lat", "sub"),
        split_axis=0,
        concat_axis=0,
        tiled=True,
    )
    wanted_flat = requests.reshape(pair_count * capacity)
    present = wanted_flat < grid_count
    picks = jnp.minimum(wanted_flat, grid_count - 1)
    grid_blocks = grid_chan.reshape(channels, grid_count, block)
    cot_blocks = cotangent.reshape(channels, grid_count, block)
    send_embed = jnp.where(present[None, :, None], jnp.take(grid_blocks, picks, axis=1), 0)
    send_cot = jnp.where(present[None, :, None], jnp.take(cot_blocks, picks, axis=1), 0)
    fetched_embed, fetched_cot = move_panels(send_embed, send_cot)
    mesh_rows = nonzero_block_rows.reshape(slot_count)
    row_marks = (mesh_rows[:, None] == jnp.arange(MBLK, dtype=jnp.int32)[None, :]).astype(
        jnp.float32
    )

    def mesh_of(fetched):
        panels = jnp.take(fetched, flat, axis=1)
        products = jnp.einsum("cki,kmi->ckm", panels, values, preferred_element_type=jnp.float32)
        summed = jnp.einsum("ckm,kr->crm", products, row_marks, precision=lax.Precision.HIGHEST)
        return summed.astype(jnp.bfloat16)

    def contributions(mesh_blocks):
        picked = jnp.take(mesh_blocks, mesh_rows, axis=1)
        backs = jnp.einsum(
            "ckm,kmi->cki", picked, values, preferred_element_type=jnp.float32
        ).astype(jnp.bfloat16)
        return (
            jnp.zeros((channels, pair_count * capacity, block), jnp.bfloat16).at[:, flat].set(backs)
        )

    back_embed = contributions(mesh_of(fetched_embed))
    back_cot = contributions(mesh_of(fetched_cot))
    returned_embed, returned_cot = move_sums(back_embed, back_cot)
    owned_marks = (wanted_flat[:, None] == jnp.arange(grid_count, dtype=jnp.int32)[None, :]).astype(
        jnp.bfloat16
    )
    decoded = jnp.einsum(
        "cnb,ng->cgb", returned_embed, owned_marks, preferred_element_type=jnp.float32
    ).astype(jnp.bfloat16)
    embed_grad = jnp.einsum(
        "cnb,ng->cgb", returned_cot, owned_marks, preferred_element_type=jnp.float32
    ).astype(jnp.bfloat16)
    grad_rows = lax.all_to_all(
        embed_grad.reshape(channels, grid_rows), "fsdp", split_axis=1, concat_axis=0, tiled=True
    )
    upstream = grad_rows.astype(jnp.float32)
    raw_grad = inv_std * (
        upstream
        - jnp.mean(upstream, axis=0, keepdims=True)
        - normed * jnp.mean(upstream * normed, axis=0, keepdims=True)
    )
    raw_grad = raw_grad.astype(jnp.bfloat16)
    hidden_grad = jnp.dot(frozen_output_weight, raw_grad, preferred_element_type=jnp.float32)
    gate_sig = jax.nn.sigmoid(preactivation_values)
    preactivation_gradient = (
        hidden_grad * gate_sig * (1.0 + preactivation_values * (1.0 - gate_sig))
    ).astype(jnp.bfloat16)
    adapter_up_contribution = contract_trailing_axes(adapter_middle_state, preactivation_gradient)
    middle_gradient = jnp.dot(
        adapter_up_weight, preactivation_gradient, preferred_element_type=jnp.float32
    ).astype(jnp.bfloat16)
    down_term = contract_trailing_axes(feature_rows, middle_gradient)
    grad_down, up_gradient = lax.psum((down_term, adapter_up_contribution), ("lat", "fsdp", "sub"))
    return (decoded.reshape(1, 1, channels, grid_rows), grad_down, up_gradient)


def solution(mesh):
    in_specs = (
        P(("parts", "lat"), "sub", None, "fsdp"),
        P(("parts", "lat"), "sub", "fsdp", None),
        P(),
        P(),
        P("parts", None),
        P("parts", None),
        P("lat", "sub", None, None, None),
        P("lat", "sub", None),
        P("lat", "sub", None),
        P(),
    )
    out_specs = (P(("parts", "lat"), "sub", "fsdp", None), P("parts", None), P("parts", None))
    return jax.shard_map(body, mesh=mesh, in_specs=in_specs, out_specs=out_specs, check_vma=False)
```

profile of v0, /device:TPU:0, one launch (start us, length us, event | category | flops | bytes accessed | tf_op | source)
XLA Modules:
  0.0 938.9 jit_solution(5802893609640966010)
XLA Ops:
  40.6 8.2 gather_fusion.4
  48.8 8.2 all-to-all-done.1
  61.1 8.1 gather_fusion.1
  69.2 9.6 %bitcast_select_fusion = (bf16[256,128,128]{2,0,1:T(8,128)(2,1)S(1)}, bf16[256,128,128]{2,0,1:T(8,128)(2,1)}) fusion(bf16[128,256,128]{2,1,0:T(8,128)(2,1)} %gather_fusion.4, pred[128]{0:T(512)(128)(4,1)S(1)} %get-tuple-element.10, pred[128]{0:T(512)(128)(4,1)S(1)} %get-tuple-element.16, bf16[128,256,128]{2,1,0:T(8,128)(2,1)} %gather_fusion.1), kind=kLoop, calls=%fused_computation.14 | loop fusion | flops 16777216 | bytes 33554688 | tf_op jit(solution)/shard_map/jit(_where)/select_n | solution.py:93
  78.8 188.8 %all_to_all.58 = bf16[256,128,128]{2,0,1:T(8,128)(2,1)} all-to-all(bf16[256,128,128]{2,0,1:T(8,128)(2,1)S(1)} %get-tuple-element.14), channel_id=1, replica_groups=mesh['parts'=2,'lat'=4,'fsdp'=2,'sub'=2] {'lat','sub'}, dimensions={1} | all-to-all | bytes 16777216 | tf_op jit(solution)/shard_map/all_to_all | solution.py:33
  273.1 9.4 gather_fusion.5
  282.5 9.2 fusion.27
  291.7 15.3 %fusion.61 = bf16[256,12,128]{2,1,0:T(8,128)(2,1)S(1)} fusion(f32[256,96,128]{2,0,1:T(8,128)} %fusion.27, s32[96]{0:T(128)S(1)} %bitcast.136), kind=kOutput, calls=%fused_computation.72 | convolution fusion | flops 453379200 | bytes 13369728 | tf_op jit(solution)/shard_map/ckm,kr->crm/dot_general | solution.py:103
  308.1 17.8 %gather_fusion.6 = bf16[96,256,128]{2,1,0:T(8,128)(2,1)} fusion(bf16[256,12,128]{2,0,1:T(8,128)(2,1)} %copy.61, s32[1024]{0:T(1024)S(1)} %pad_clamp_fusion), kind=kCustom, calls=%fused_computation.5.clone | custom fusion | bytes 12583296 | tf_op jit(solution)/shard_map/jit(_take)/gather | solution.py:107
  325.8 7.3 fusion.39
  338.6 17.8 %scatter_fusion.1 = bf16[256,128,128]{2,0,1:T(8,128)(2,1)} fusion(bf16[256,128,128]{2,0,1:T(8,128)(2,1)} %broadcast.226.clone.1, s32[96]{0:T(128)S(1)} %fusion.84, bf16[96,256,128]{2,1,0:T(8,128)(2,1)} %fusion.39), kind=kCustom, calls=%fused_computation.9 | custom fusion | bytes 18874752 | tf_op jit(solution)/shard_map/scatter | solution.py:112
  356.3 100.6 %all-to-all-done.2 = bf16[256,128,128]{2,0,1:T(8,128)(2,1)} async-done(((bf16[256,128,128]{2,0,1:T(8,128)(2,1)}), bf16[256,128,128]{2,0,1:T(8,128)(2,1)}, u32[]{:S(2)}, u32[]{:S(2)}) %all-to-all-start.2) | async-done | bytes 8388640 | tf_op jit(solution)/shard_map/all_to_all | solution.py:32
  461.9 9.4 %gather_fusion.2 = bf16[96,256,128]{2,1,0:T(8,128)(2,1)} fusion(bf16[256,128,128]{2,0,1:T(8,128)(2,1)} %all-to-all-done.2, s32[1024]{0:T(1024)S(1)} %pad_clamp_fusion.1), kind=kCustom, calls=%fused_computation.1.clone | custom fusion | bytes 12583296 | tf_op jit(solution)/shard_map/jit(_take)/gather | solution.py:101
  471.3 9.2 fusion.24
  480.5 15.3 %fusion.64 = bf16[256,12,128]{2,1,0:T(8,128)(2,1)S(1)} fusion(f32[256,96,128]{2,0,1:T(8,128)} %fusion.24, s32[96]{0:T(128)S(1)} %bitcast.137), kind=kOutput, calls=%fused_computation.73 | convolution fusion | flops 453379200 | bytes 13369728 | tf_op jit(solution)/shard_map/ckm,kr->crm/dot_general | solution.py:103
  496.8 7.3 gather_fusion.3
  504.1 7.3 fusion.36
  516.7 17.7 %scatter_fusion = bf16[256,128,128]{2,0,1:T(8,128)(2,1)} fusion(bf16[256,128,128]{2,0,1:T(8,128)(2,1)} %broadcast.226.clone, s32[96]{0:T(128)S(1)} %fusion.84, bf16[96,256,128]{2,1,0:T(8,128)(2,1)} %fusion.36), kind=kCustom, calls=%fused_computation.8 | custom fusion | bytes 18874752 | tf_op jit(solution)/shard_map/scatter | solution.py:112
  534.4 111.3 %all-to-all-done.5 = bf16[256,128,128]{2,0,1:T(8,128)(2,1)} async-done(((bf16[256,128,128]{2,0,1:T(8,128)(2,1)}), bf16[256,128,128]{2,0,1:T(8,128)(2,1)}, u32[]{:S(2)}, u32[]{:S(2)}) %all-to-all-start.5) | async-done | bytes 8388640 | tf_op jit(solution)/shard_map/all_to_all | solution.py:40
  650.7 9.9 %convert_bitcast_fusion = bf16[256,32,128]{2,1,0:T(8,128)(2,1)} fusion(bf16[256,128,128]{2,0,1:T(8,128)(2,1)} %all-to-all-done.5, s32[128]{0:T(128)S(1)} %eq.48), kind=kOutput, calls=%fused_computation.67 | convolution fusion | flops 269488128 | bytes 10486272 | tf_op jit(solution)/shard_map/cnb,ng->cgb/dot_general | solution.py:124
  668.4 166.2 %all-to-all-done.3 = bf16[256,128,128]{2,0,1:T(8,128)(2,1)} async-done(((bf16[256,128,128]{2,0,1:T(8,128)(2,1)}), bf16[256,128,128]{2,0,1:T(8,128)(2,1)}, u32[]{:S(2)}, u32[]{:S(2)}) %all-to-all-start.3) | async-done | bytes 8388640 | tf_op jit(solution)/shard_map/all_to_all | solution.py:39
  839.9 9.9 %convert_bitcast_fusion.1 = bf16[256,32,128]{2,1,0:T(8,128)(2,1)} fusion(bf16[256,128,128]{2,0,1:T(8,128)(2,1)} %all-to-all-done.3, s32[128]{0:T(128)S(1)} %eq.48), kind=kOutput, calls=%fused_computation.68 | convolution fusion | flops 269488128 | bytes 10486272 | tf_op jit(solution)/shard_map/cnb,ng->cgb/dot_general | solution.py:121
  854.0 11.0 %all-to-all-done.6 = bf16[256,2,2048]{2,0,1:T(8,128)(2,1)} async-done(((bf16[256,2,2048]{2,0,1:T(8,128)(2,1)}), bf16[256,2,2048]{2,0,1:T(8,128)(2,1)}, u32[]{:S(2)}, u32[]{:S(2)}) %all-to-all-start.6) | async-done | bytes 2097184 | tf_op jit(solution)/shard_map/all_to_all | solution.py:127
  880.0 58.8 %all-reduce = (f32[227,16]{0,1:T(8,128)}, f32[16,512]{1,0:T(8,128)}) all-reduce(f32[227,16]{0,1:T(8,128)S(1)} %fusion.68, f32[16,512]{1,0:T(8,128)S(1)} %fusion.94), channel_id=1, replica_groups=mesh['parts'=2,'lat'=4,'fsdp'=2,'sub'=2] {'lat','fsdp','sub'}, use_global_device_ids=true, to_apply=%region_9.13 | all-reduce | flops 11824 | bytes 94592 | tf_op jit(solution)/shard_map/psum | solution.py:147
  (74 shorter events, 104.5 us)
Async XLA Ops:
  0.6 281.9 %copy-start = (bf16[1,1,96,128,128]{4,3,2,1,0:T(8,128)(2,1)S(1)}, bf16[1,1,96,128,128]{4,3,2,1,0:T(8,128)(2,1)}, u32[]{:S(2)}) copy-start(bf16[1,1,96,128,128]{4,3,2,1,0:T(8,128)(2,1)} %param.22) | copy-start | bytes 9437188
  6.5 19.7 %all-to-all-start = ((s32[8,1,16]{2,1,0:T(1,128)}), s32[8,1,16]{2,1,0:T(1,128)S(1)}, u32[]{:S(2)}, u32[]{:S(2)}) async-start(s32[8,1,16]{2,1,0:T(1,128)} %bitcast.6), calls=%async_computation | async-start | bytes 8192 | tf_op jit(solution)/shard_map/all_to_all | solution.py:80
  12.9 3.6 copy-start.6
  16.5 1.0 copy-start.8
  17.5 2.1 copy-start.4
  19.6 2.7 copy-start.1
  26.2 30.7 %all-to-all-start.1 = ((bf16[2,256,2048]{1,2,0:T(8,128)(2,1)}), bf16[2,256,2048]{1,2,0:T(8,128)(2,1)}, u32[]{:S(2)}, u32[]{:S(2)}) async-start(bf16[2,256,2048]{1,2,0:T(8,128)(2,1)} %copy.53), calls=%async_computation.1 | async-start | bytes 4194304 | tf_op jit(solution)/shard_map/all_to_all | solution.py:70
  267.6 5.5 copy-start.7
  267.6 189.4 %all-to-all-start.2 = ((bf16[256,128,128]{2,0,1:T(8,128)(2,1)}), bf16[256,128,128]{2,0,1:T(8,128)(2,1)}, u32[]{:S(2)}, u32[]{:S(2)}) async-start(bf16[256,128,128]{2,0,1:T(8,128)(2,1)} %get-tuple-element.15), calls=%async_computation.2 | async-start | bytes 16777216 | tf_op jit(solution)/shard_map/all_to_all | solution.py:32
  456.9 188.8 %all-to-all-start.5 = ((bf16[256,128,128]{2,0,1:T(8,128)(2,1)}), bf16[256,128,128]{2,0,1:T(8,128)(2,1)}, u32[]{:S(2)}, u32[]{:S(2)}) async-start(bf16[256,128,128]{2,0,1:T(8,128)(2,1)} %scatter_fusion.1), calls=%async_computation.5 | async-start | bytes 16777216 | tf_op jit(solution)/shard_map/all_to_all | solution.py:40
  645.8 188.9 %all-to-all-start.3 = ((bf16[256,128,128]{2,0,1:T(8,128)(2,1)}), bf16[256,128,128]{2,0,1:T(8,128)(2,1)}, u32[]{:S(2)}, u32[]{:S(2)}) async-start(bf16[256,128,128]{2,0,1:T(8,128)(2,1)} %scatter_fusion), calls=%async_computation.3 | async-start | bytes 16777216 | tf_op jit(solution)/shard_map/all_to_all | solution.py:39
  834.6 30.3 %all-to-all-start.6 = ((bf16[256,2,2048]{2,0,1:T(8,128)(2,1)}), bf16[256,2,2048]{2,0,1:T(8,128)(2,1)}, u32[]{:S(2)}, u32[]{:S(2)}) async-start(bf16[256,2,2048]{2,0,1:T(8,128)(2,1)} %copy.63), calls=%async_computation.6 | async-start | bytes 4194304 | tf_op jit(solution)/shard_map/all_to_all | solution.py:127
  864.9 5.7 copy-start.2
  870.6 2.9 copy-start.5
  870.6 2.9 copy-start.9
  875.5 1.4 copy-start.3
where the time goes:
time: 949 us; the launch traced here: 939 us
  waiting for transfers between devices  397 us (42%)
  blocking collectives  248 us (26%)
  local copies, waits for them, and re-layouts  143 us (15%)
  matrix products  94.2 us (10%)
  starting transfers between devices  31.9 us (3%)
  other arithmetic  24.1 us (3%)
    all_to_all x1, blocking collectives, move_panels(): lax.all_to_all(second, ('lat', 'sub'), split_axis=1, concat_axis=1, tiled...  189 us
    all_to_all x1, waiting for transfers between devices, move_sums(): lax.all_to_all(first, ('lat', 'sub'), split_axis=1, concat_axis=1, tiled=...  166 us
    all_to_all x1, waiting for transfers between devices, move_sums(): lax.all_to_all(second, ('lat', 'sub'), split_axis=1, concat_axis=1, tiled...  111 us
    all_to_all x1, waiting for transfers between devices, move_panels(): lax.all_to_all(first, ('lat', 'sub'), split_axis=1, concat_axis=1, tiled=...  101 us
    psum x1, blocking collectives, body(): lax.psum((down_term, adapter_up_contribution), ('lat', 'fsdp', 'sub'))  58.8 us
    scatter x2, local copies, waits for them, and re-layouts, contributions(): jnp.zeros((channels, pair_count * capacity, block), jnp.bfloat16)  35.4 us
    dot_general x2, matrix products, mesh_of(): jnp.einsum('ckm,kr->crm', products, row_marks, precision=lax.Precision.HI...  30.6 us
    gather x2, local copies, waits for them, and re-layouts, contributions(): picked = jnp.take(mesh_blocks, mesh_rows, axis=1)  25.1 us
  transfers between devices with their start and end apart: 6, of which 5 were waited for; matrix products, arithmetic and copies ran while one was open for 23% of the time, Pallas kernels for 0%

commit v1 on v0

v1 whole, which is shorter than its diff:
```python
import functools

import jax
import jax.numpy as jnp
from jax import lax
from jax.experimental import pallas as pl
from jax.experimental.pallas import tpu as pltpu
from jax.sharding import PartitionSpec as P

MBLK = 12
BF = jnp.bfloat16
F32 = jnp.float32
VMEM_LIMIT = 44 * 1024 * 1024


def params(**kw):
    return pltpu.CompilerParams(vmem_limit_bytes=VMEM_LIMIT, **kw)


def dg(a, b, ca, cb):
    return lax.dot_general(a, b, (((ca,), (cb,)), ((), ())), preferred_element_type=F32)


def places_of(storage, cols):
    ids = jnp.arange(storage.shape[0], dtype=jnp.int32)
    return jnp.sum(jnp.where(cols[..., None] == ids, storage, 0), axis=-1)


def ranks_in(mask):
    size = mask.shape[-1]
    before = jnp.arange(size)[:, None] > jnp.arange(size)[None, :]
    return jnp.sum(jnp.where(before, mask[..., None, :], 0), axis=-1)


def pack_kernel(src, interp, *rest):
    outs, sem = rest[:-1], rest[-1]
    pairs, width = outs[0].shape[0], outs[0].shape[1]
    copies = []
    for h, out in enumerate(outs):
        for o in range(pairs):
            for c in range(width):
                copies.append(
                    pltpu.make_async_copy(
                        interp.at[src[o, h * width + c]], out.at[o, c], sem.at[len(copies)]
                    )
                )
    for copy in copies:
        copy.start()
    for copy in copies:
        copy.wait()


def pack(src, values, pieces):
    pairs, width = src.shape[0], src.shape[1] // pieces
    block = values.shape[1]
    return pl.pallas_call(
        pack_kernel,
        grid_spec=pltpu.PrefetchScalarGridSpec(
            num_scalar_prefetch=1,
            grid=(1,),
            in_specs=[pl.BlockSpec(memory_space=pl.ANY)],
            out_specs=[pl.BlockSpec(memory_space=pl.ANY)] * pieces,
            scratch_shapes=[pltpu.SemaphoreType.DMA((pairs * src.shape[1],))],
        ),
        out_shape=[jax.ShapeDtypeStruct((pairs, width, block, block), BF)] * pieces,
        compiler_params=params(),
        name="pack",
    )(src, values)


def forward_kernel(meta, x, w_in, a_down, a_up, w_out, emb, normed, slope, inv, mid, hold):
    feats = x[...]
    middle = dg(a_down[...], feats, 0, 0).astype(BF)
    pre = dg(w_in[...], feats, 0, 0) + dg(a_up[...], middle, 0, 0)
    sig = jax.nn.sigmoid(pre)
    hidden = (pre * sig).astype(BF)
    slope[...] = sig * (1.0 + pre * (1.0 - sig))
    raw = dg(w_out[...], hidden, 0, 0)
    center = raw - jnp.mean(raw, axis=0, keepdims=True)
    istd = lax.rsqrt(jnp.mean(center * center, axis=0, keepdims=True) + 1e-05)
    norm = center * istd
    normed[...] = norm
    inv[...] = istd
    mid[...] = middle
    hold[...] = norm.astype(BF)
    nf, chans = emb.shape[0], emb.shape[1]
    for r in range(nf):
        at = lax.rem(meta[0] + r, nf) * chans
        emb[r] = hold[pl.ds(pl.multiple_of(at, chans), chans), :]


def forward(meta, x, w_in, a_down, a_up, w_out, nf):
    width, rows = w_out.shape[0], x.shape[1]
    rank = a_down.shape[1]
    step = min(512, rows)
    chans = width // nf
    full = lambda a: pl.BlockSpec(a.shape, lambda i, m: (0, 0))
    return pl.pallas_call(
        forward_kernel,
        grid_spec=pltpu.PrefetchScalarGridSpec(
            num_scalar_prefetch=1,
            grid=(rows // step,),
            in_specs=[
                pl.BlockSpec((x.shape[0], step), lambda i, m: (0, i)),
                full(w_in),
                full(a_down),
                full(a_up),
                full(w_out),
            ],
            out_specs=[
                pl.BlockSpec((nf, chans, step), lambda i, m: (0, 0, i)),
                pl.BlockSpec((width, step), lambda i, m: (0, i)),
                pl.BlockSpec((width, step), lambda i, m: (0, i)),
                pl.BlockSpec((1, step), lambda i, m: (0, i)),
                pl.BlockSpec((rank, step), lambda i, m: (0, i)),
            ],
            scratch_shapes=[pltpu.VMEM((width, step), BF)],
        ),
        out_shape=[
            jax.ShapeDtypeStruct((nf, chans, rows), BF),
            jax.ShapeDtypeStruct((width, rows), F32),
            jax.ShapeDtypeStruct((width, rows), F32),
            jax.ShapeDtypeStruct((1, rows), F32),
            jax.ShapeDtypeStruct((rank, rows), BF),
        ],
        compiler_params=params(),
        cost_estimate=pl.CostEstimate(
            flops=2 * rows * width * (width + x.shape[0]), bytes_accessed=rows * width * 12, transcendentals=0
        ),
        name="forward",
    )(meta, x, w_in, a_down, a_up, w_out)


def backward_kernel(offs, *refs, count):
    pieces = refs[:count]
    normed, slope, inv, mid, x, w_out, a_up, up, down, hold = refs[count:]
    chans = pieces[0].shape[0]
    for i, piece in enumerate(pieces):
        hold[pl.ds(pl.multiple_of(offs[i], chans), chans), :] = piece[...].astype(F32)
    e = hold[...]
    norm = normed[...]
    raw = inv[...] * (
        e
        - jnp.mean(e, axis=0, keepdims=True)
        - norm * jnp.mean(e * norm, axis=0, keepdims=True)
    )
    hidden_grad = dg(w_out[...], raw.astype(BF), 1, 0)
    pre_grad = (hidden_grad * slope[...]).astype(BF)
    up_term = dg(mid[...], pre_grad, 1, 1)
    mid_grad = dg(a_up[...], pre_grad, 1, 0).astype(BF)
    down_term = dg(mid_grad, x[...], 1, 1)

    @pl.when(pl.program_id(0) == 0)
    def _():
        up[...] = jnp.zeros_like(up)
        down[...] = jnp.zeros_like(down)

    up[...] += up_term
    down[...] += down_term


def backward(offs, pieces, normed, slope, inv, mid, x, w_out, a_up):
    width, rows = normed.shape
    rank = a_up.shape[0]
    step = min(512, rows)
    full = lambda a: pl.BlockSpec(a.shape, lambda i, m: (0, 0))
    tall = lambda a: pl.BlockSpec((a.shape[0], step), lambda i, m: (0, i))
    return pl.pallas_call(
        functools.partial(backward_kernel, count=len(pieces)),
        grid_spec=pltpu.PrefetchScalarGridSpec(
            num_scalar_prefetch=1,
            grid=(rows // step,),
            in_specs=[tall(p) for p in pieces]
            + [tall(normed), tall(slope), tall(inv), tall(mid), tall(x), full(w_out), full(a_up)],
            out_specs=[
                pl.BlockSpec((rank, width), lambda i, m: (0, 0)),
                pl.BlockSpec((rank, x.shape[0]), lambda i, m: (0, 0)),
            ],
            scratch_shapes=[pltpu.VMEM((width, step), F32)],
        ),
        out_shape=[
            jax.ShapeDtypeStruct((rank, width), F32),
            jax.ShapeDtypeStruct((rank, x.shape[0]), F32),
        ],
        compiler_params=params(),
        cost_estimate=pl.CostEstimate(
            flops=2 * rows * width * width, bytes_accessed=rows * width * 10, transcendentals=0
        ),
        name="backward",
    )(offs, *pieces, normed, slope, inv, mid, x, w_out, a_up)


def encode_kernel(tab_j, tab_m, meta, *refs, panels, weights, n, ns):
    xs, ws = refs[:panels], refs[panels : panels + weights]
    out, acc = refs[panels + weights], refs[panels + weights + 1]
    r = pl.program_id(0)
    p = lax.rem(meta[0] + r, n) * ns + meta[1]
    block = out.shape[3]
    if panels > 1:
        hold = refs[panels + weights + 2]
        wide = xs[0].shape[1]

        @pl.when(r == 0)
        def _():
            for i, piece in enumerate(xs):
                at = lax.rem(meta[2] + panels - i, panels) * wide
                hold[:, pl.ds(pl.multiple_of(at, wide), wide)] = piece[...]

        source = hold
    else:
        source = xs[0]
    acc[...] = jnp.zeros_like(acc)
    slot = 0
    for w in ws:
        for c in range(w.shape[1]):
            j, m = tab_j[p, slot], tab_m[p, slot]
            slot += 1
            panel = source[:, pl.ds(pl.multiple_of(j * block, block), block)]
            acc[m] += dg(panel, w[0, c], 1, 1)
    out[0] = acc[0 : out.shape[1]].astype(BF)


def encode(tab_j, tab_m, meta, pieces, chunk, chunks, weights, n, ns):
    chans, wide = pieces[0].shape[0] // chunks, pieces[0].shape[1]
    panels = len(pieces)
    block = weights[0].shape[2]
    cap = sum(w.shape[1] for w in weights)
    scratch = [pltpu.VMEM((MBLK + 1, chans, block), F32)]
    if panels > 1:
        scratch.append(pltpu.VMEM((chans, wide * panels), BF))
    where = lambda r, j, m, t: (lax.rem(t[0] + r, n) * ns + t[1], 0, 0, 0)
    return pl.pallas_call(
        functools.partial(encode_kernel, panels=panels, weights=len(weights), n=n, ns=ns),
        grid_spec=pltpu.PrefetchScalarGridSpec(
            num_scalar_prefetch=3,
            grid=(n,),
            in_specs=[pl.BlockSpec((chans, wide), lambda r, j, m, t: (chunk, 0))] * panels
            + [pl.BlockSpec((1,) + w.shape[1:], where) for w in weights],
            out_specs=pl.BlockSpec((1, MBLK, chans, block), lambda r, j, m, t: (r, 0, 0, 0)),
            scratch_shapes=scratch,
        ),
        out_shape=jax.ShapeDtypeStruct((n, MBLK, chans, block), BF),
        compiler_params=params(),
        cost_estimate=pl.CostEstimate(
            flops=2 * n * cap * chans * block * block * 4,
            bytes_accessed=n * MBLK * chans * block * 4,
            transcendentals=0,
        ),
        name="encode",
    )(tab_j, tab_m, meta, *pieces, *weights)


def decode_kernel(tab_j, tab_m, meta, *refs, n, ns, weights, alias, split):
    count = 2 * n - 1
    mine, theirs = refs[:count], refs[count : 2 * count]
    ws = refs[2 * count : 2 * count + weights]
    rest = refs[2 * count + weights + (1 if alias else 0) :]
    out, hold, acc, sem = rest
    z, s = meta[0], meta[1]
    block = hold.shape[3]

    def copies(side, group, go):
        for r in range(n):
            at = r * ns + side
            if r == 0:
                go(pltpu.make_async_copy(group[0], hold.at[at], sem.at[at]))
                continue
            below, above = group[n - r], group[n - 1 + r]

            @pl.when(z + r < n)
            def _():
                go(pltpu.make_async_copy(above, hold.at[at], sem.at[at]))

            @pl.when(z + r >= n)
            def _():
                go(pltpu.make_async_copy(below, hold.at[at], sem.at[at]))

    for side, group in enumerate((mine, theirs)):
        copies(side, group, lambda c: c.start())
    acc[...] = jnp.zeros_like(acc)

    def step(i, carry):
        r, side = i // ns, lax.rem(i, ns)
        p = lax.rem(z + r, n) * ns + lax.rem(s + side, ns)
        pltpu.make_async_copy(mine[0], hold.at[i], sem.at[i]).wait()
        slot = 0
        for w in ws:
            for c in range(w.shape[1]):
                j, m = tab_j[p, slot], tab_m[p, slot]
                slot += 1
                acc[j] += dg(hold[i, jnp.minimum(m, MBLK - 1)], w[p, c], 1, 0)
        return carry

    lax.fori_loop(0, n * ns, step, 0)
    for g in range(acc.shape[0] - 1):
        if split:
            per = out.shape[2] // block
            to = lax.rem(g // per - meta[2] + out.shape[0], out.shape[0])
            out[to, :, (g % per) * block : (g % per + 1) * block] = acc[g].astype(BF)
        else:
            out[:, g * block : (g + 1) * block] = acc[g].astype(BF)


def decode(tab_j, tab_m, meta, mine, theirs, weights, grid_count, chunk, chunks, base, nf, n, ns):
    chans, block = mine[0].shape[1], mine[0].shape[2]
    rows = grid_count * block
    split = nf is not None
    if split:
        shape = (nf, chans, rows // nf)
        out_spec = pl.BlockSpec(shape, lambda i, j, m, t: (0, 0, 0))
    else:
        shape = (chans * chunks, rows)
        out_spec = pl.BlockSpec((chans, rows), lambda i, j, m, t: (chunk, 0))
    alias = base is not None
    count = 2 * len(mine)
    return pl.pallas_call(
        functools.partial(
            decode_kernel, n=n, ns=ns, weights=len(weights), alias=alias, split=split
        ),
        grid_spec=pltpu.PrefetchScalarGridSpec(
            num_scalar_prefetch=3,
            grid=(1,),
            in_specs=[pl.BlockSpec(memory_space=pl.ANY)] * count
            + [pl.BlockSpec(w.shape, lambda i, j, m, t: (0, 0, 0, 0)) for w in weights]
            + ([pl.BlockSpec(memory_space=pl.ANY)] if alias else []),
            out_specs=out_spec,
            scratch_shapes=[
                pltpu.VMEM((n * ns, MBLK, chans, block), BF),
                pltpu.VMEM((grid_count + 1, chans, block), F32),
                pltpu.SemaphoreType.DMA((n * ns,)),
            ],
        ),
        out_shape=jax.ShapeDtypeStruct(shape, BF),
        input_output_aliases={3 + count + len(weights): 0} if alias else {},
        compiler_params=params(),
        cost_estimate=pl.CostEstimate(
            flops=2 * n * ns * 16 * chans * block * block * 4,
            bytes_accessed=2 * n * MBLK * chans * block * 4,
            transcendentals=0,
        ),
        name="decode",
    )(tab_j, tab_m, meta, *mine, *theirs, *weights, *([base] if alias else []))


def total(*terms):
    out = terms[0].astype(F32)
    for term in terms[1:]:
        out = out + term.astype(F32)
    return out.astype(BF)


def swap_sub(a):
    ns = lax.axis_size("sub")
    return lax.ppermute(a, "sub", [(i, (i + 1) % ns) for i in range(ns)])


def reduce_line(own, other):
    n = own.shape[0]
    up = down = None
    for t in range(1, n):
        ups = [own[n - t], other[n - t]] + ([up] if up is not None else [])
        downs = [own[t], other[t]] + ([down] if down is not None else [])
        up = lax.ppermute(total(*ups), "lat", [(i, i + 1) for i in range(n - 1) if i <= t - 1])
        down = lax.ppermute(
            total(*downs), "lat", [(i, i - 1) for i in range(1, n) if i >= n - t]
        )
    return total(own[0], other[0], up, down)


def spread_line(block):
    n = lax.axis_size("lat")
    ups, downs = [block], [block]
    for t in range(1, n):
        ups.append(
            lax.ppermute(ups[-1], "lat", [(i, i + 1) for i in range(n - 1) if i >= t - 1])
        )
        downs.append(lax.ppermute(downs[-1], "lat", [(i, i - 1) for i in range(1, n) if i <= n - t]))
    return ups + downs[1:]


def add_all(value, axes):
    for axis in axes:
        size, step = lax.axis_size(axis), 1
        while step < size:
            value = value + lax.ppermute(value, axis, [(i, i ^ step) for i in range(size)])
            step *= 2
    return value


def body(
    grid_input_channels,
    cotangent,
    frozen_input_weight,
    frozen_output_weight,
    adapter_down_weight,
    adapter_up_weight,
    interp,
    nonzero_block_rows,
    nonzero_block_columns,
    grid_block_storage,
):
    n, ns = lax.axis_size("lat"), lax.axis_size("sub")
    nf, npart = lax.axis_size("fsdp"), lax.axis_size("parts")
    z, s = lax.axis_index("lat"), lax.axis_index("sub")
    f, y = lax.axis_index("fsdp"), lax.axis_index("parts")
    pairs = n * ns
    me = z * ns + s
    slots, block = interp.shape[2], interp.shape[3]
    chans, grid_rows = cotangent.shape[2], cotangent.shape[3]
    grid_count = grid_rows // block
    width = frozen_output_weight.shape[0]
    cap = max(2, (4 * slots + 3 * pairs - 1) // (3 * pairs))
    x = grid_input_channels.reshape(grid_input_channels.shape[2:])
    cot = cotangent.reshape(chans, grid_rows)
    values = interp.reshape(slots, block, block)
    storage = grid_block_storage.astype(jnp.int32)
    cols = nonzero_block_columns.reshape(slots)
    rows = nonzero_block_rows.reshape(slots)
    pair_ids = jnp.arange(pairs, dtype=jnp.int32)

    place = places_of(storage, cols)
    marks = (place[None, :] // grid_count == pair_ids[:, None]).astype(jnp.int32)
    rank = ranks_in(marks)
    shared = nf == 2 and npart == 2 and cap % 8 == 0
    if shared:
        r0 = y * 2 + f
        cs = cap // 4
        send_ranks = r0 * cs + jnp.arange(cs, dtype=jnp.int32)
    else:
        send_ranks = jnp.arange(cap, dtype=jnp.int32)
    hit = (rank[:, None, :] == send_ranks[None, :, None]) & (marks[:, None, :] > 0)
    src = jnp.sum(jnp.where(hit, jnp.arange(slots, dtype=jnp.int32), 0), axis=-1)
    a2a = lambda v: lax.all_to_all(v, ("lat", "sub"), 0, 0, tiled=True)
    if shared:
        first, second = pack(src, values, 2)
        first, second = a2a(first), a2a(second)
        flip = [(0, 1), (1, 0)]
        over_x = lambda v: lax.ppermute(v, "fsdp", flip)
        over_y = lambda v: lax.ppermute(v, "parts", flip)
        x1, y1, x2, y2 = over_x(first), over_y(first), over_x(second), over_y(second)
        weights = [first, second, x1, x2, y1, y2, over_x(y1), over_y(x2)]
        half = jnp.arange(cs, dtype=jnp.int32)
        slot_ranks = jnp.concatenate([(r0 ^ k) * cs + half for k in range(4)])
    else:
        weights = [a2a(pack(src, values, 1)[0])]
        slot_ranks = send_ranks

    both = lax.all_gather(jnp.stack([cols, rows])[None], ("lat", "sub"), tiled=True)
    every = places_of(storage, both[:, 0])
    mine = (every // grid_count == me).astype(jnp.int32)
    mine_rank = ranks_in(mine)
    hit = (mine_rank[:, None, :] == slot_ranks[None, :, None]) & (mine[:, None, :] > 0)
    found = jnp.any(hit, axis=-1)
    local = jnp.sum(jnp.where(hit, (every % grid_count)[:, None, :], 0), axis=-1)
    tab_m = jnp.where(found, jnp.sum(jnp.where(hit, both[:, 1][:, None, :], 0), axis=-1), MBLK)
    tab_get = jnp.where(found, local, 0)
    tab_put = jnp.where(found, local, grid_count)

    meta_f = jnp.stack([f]).astype(jnp.int32)
    emb, normed, slope, inv, mid = forward(
        meta_f, x, frozen_input_weight, adapter_down_weight, adapter_up_weight,
        frozen_output_weight, nf,
    )
    shift = lambda v, r: lax.ppermute(v, "fsdp", [(i, (i + r) % nf) for i in range(nf)])
    emb_pieces = [emb[r] if r == 0 else shift(emb[r], r) for r in range(nf)]

    meta_own = jnp.stack([z, s, f]).astype(jnp.int32)
    meta_sib = jnp.stack([z, (s + 1) % ns, f]).astype(jnp.int32)
    chunks = 2

    def mesh_of(pieces, chunk):
        args = (pieces, chunk, chunks, weights, n, ns)
        other = swap_sub(encode(tab_get, tab_m, meta_sib, *args))
        own = encode(tab_get, tab_m, meta_own, *args)
        return reduce_line(own, other)

    def grid_of(mesh, chunk, base, split):
        here = spread_line(mesh)
        there = [swap_sub(a) for a in here]
        return decode(
            tab_put, tab_m, meta_own, here, there, weights, grid_count, chunk, chunks, base,
            nf if split else None, n, ns,
        )

    cot_mesh = [mesh_of([cot], c) for c in range(chunks)]
    emb_mesh = [mesh_of(emb_pieces, c) for c in range(chunks)]
    grads, offs = [], []
    for c in range(chunks):
        grad = grid_of(cot_mesh[c], c, None, True)
        for r in range(nf):
            grads.append(grad[r] if r == 0 else shift(grad[r], r))
            offs.append(((f - r + nf) % nf) * chans + c * (chans // chunks))
    decoded = None
    for c in range(chunks):
        decoded = grid_of(emb_mesh[c], c, decoded, False)

    up, down = backward(
        jnp.stack(offs).astype(jnp.int32), grads, normed, slope, inv, mid, x,
        frozen_output_weight, adapter_up_weight,
    )
    sums = add_all(jnp.concatenate([up, down], axis=1), ("sub", "fsdp", "lat"))
    up_gradient, grad_down = sums[:, :width], sums[:, width:].T
    return (decoded.reshape(1, 1, chans, grid_rows), grad_down, up_gradient)


def solution(mesh):
    in_specs = (
        P(("parts", "lat"), "sub", None, "fsdp"),
        P(("parts", "lat"), "sub", "fsdp", None),
        P(),
        P(),
        P("parts", None),
        P("parts", None),
        P("lat", "sub", None, None, None),
        P("lat", "sub", None),
        P("lat", "sub", None),
        P(),
    )
    out_specs = (P(("parts", "lat"), "sub", "fsdp", None), P("parts", None), P("parts", None))
    return jax.shard_map(body, mesh=mesh, in_specs=in_specs, out_specs=out_specs, check_vma=False)
```

time: 949 us -> 444 us (0.47)
  waiting for transfers between devices: 397 us -> 157 us
  blocking collectives: 248 us -> 31.3 us
  local copies, waits for them, and re-layouts: 143 us -> 29.5 us
  starting transfers between devices: 31.9 us -> 127 us
  matrix products: 94.2 us -> 0 us
  Pallas kernels: 0 us -> 69.3 us
    all_to_all x6 -> x1, waiting for transfers between devices: 397 us -> 0.01 us  [body(): a2a = lambda v: lax.all_to_all(v, ('lat', 'sub'), 0, 0, tiled=True)]
    all_to_all x1, blocking collectives: 189 us -> 17.9 us  [body(): a2a = lambda v: lax.all_to_all(v, ('lat', 'sub'), 0, 0, tiled=True)]
    ppermute x0 -> x93, waiting for transfers between devices: none -> 157 us  [the longest x12 70.9 us: spread_line(): lax.ppermute(downs[-1], 'lat', [(i, i - 1) for i in range(1, n) if i <= n...]
    ppermute x0 -> x93, starting transfers between devices: none -> 123 us  [the longest x12 42.5 us: reduce_line(): lax.ppermute(total(*ups), 'lat', [(i, i + 1) for i in range(n - 1) if i <...]
    dot_general x15 -> x0, matrix products: 94.2 us -> none  [the longest x2 30.6 us: mesh_of(): jnp.einsum('ckm,kr->crm', products, row_marks, precision=lax.Precision.HI...]
    pallas_call x0 -> x15, Pallas kernels: none -> 69.3 us  [the longest x8 27.6 us: encode(): pl.pallas_call(functools.partial(encode_kernel, panels=panels, weights=le...]
    gather x7 -> x0, local copies, waits for them, and re-layouts: 61.9 us -> none  [the longest x2 25.1 us: contributions(): picked = jnp.take(mesh_blocks, mesh_rows, axis=1)]
    psum x1 -> x0, blocking collectives: 58.8 us -> none  [body(): lax.psum((down_term, adapter_up_contribution), ('lat', 'fsdp', 'sub'))]
  transfers between devices with their start and end apart: 6 -> 94, of which waited for: 5 -> 26; matrix products, arithmetic and copies ran while one was open for 23% -> 7% of each run, Pallas kernels for 0% -> 15%
where the time goes in v1:
time: 444 us; the launch traced here: 441 us
  waiting for transfers between devices  157 us (35%)
  starting transfers between devices  127 us (29%)
  Pallas kernels  69.3 us (16%)
  blocking collectives  31.3 us (7%)
  local copies, waits for them, and re-layouts  29.5 us (7%)
  other arithmetic  26 us (6%)
    ppermute x12, waiting for transfers between devices, spread_line(): lax.ppermute(downs[-1], 'lat', [(i, i - 1) for i in range(1, n) if i <= n...  70.9 us
    ppermute x3, waiting for transfers between devices, body(): over_x = lambda v: lax.ppermute(v, 'fsdp', flip)  43.3 us
    ppermute x12, starting transfers between devices, reduce_line(): lax.ppermute(total(*ups), 'lat', [(i, i + 1) for i in range(n - 1) if i <...  42.5 us
    ppermute x12, starting transfers between devices, spread_line(): lax.ppermute(ups[-1], 'lat', [(i, i + 1) for i in range(n - 1) if i >= t...  29.6 us
    pallas_call x8, Pallas kernels, encode(): pl.pallas_call(functools.partial(encode_kernel, panels=panels, weights=le...  27.6 us
    pallas_call x4, Pallas kernels, decode(): pl.pallas_call(functools.partial(decode_kernel, n=n, ns=ns, weights=len(w...  24.5 us
    convert_element_type x20, other arithmetic, total(): return out.astype(BF)  21.7 us
    unnamed x66, local copies, waits for them, and re-layouts  20.5 us
  transfers between devices with their start and end apart: 94, of which 26 were waited for; matrix products, arithmetic and copies ran while one was open for 7% of the time, Pallas kernels for 15%

profile of v1, /device:TPU:0, one launch (start us, length us, event | category | flops | bytes accessed | tf_op | source)
XLA Modules:
  0.0 441.5 jit_solution(1752866738046663551)
XLA Ops:
  1.3 13.4 %all-gather.1 = s32[8,2,96]{2,1,0:T(2,128)S(1)} all-gather(s32[1,2,96]{2,1,0:T(2,128)S(1)} %add_bitcast_fusion), channel_id=2, replica_groups=mesh['parts'=2,'lat'=4,'fsdp'=2,'sub'=2] {'lat','sub'}, dimensions={0}, use_global_device_ids=true | all-gather | bytes 6912 | tf_op jit(solution)/shard_map/all_gather | solution.py:448
  21.8 17.9 %all_to_all.10.refs_2_.refs_14_.refs_1_ = bf16[8,2,128,128]{3,2,1,0:T(8,128)(2,1)S(1)} all-to-all(bf16[8,2,128,128]{3,2,1,0:T(8,128)(2,1)S(1)} %get-tuple-element.13), channel_id=1, replica_groups=mesh['parts'=2,'lat'=4,'fsdp'=2,'sub'=2] {'lat','sub'}, dimensions={0} | all-to-all | bytes 1048576 | tf_op jit(solution)/shard_map/all_to_all | solution.py:433
  45.6 7.5 %forward.1 = (bf16[2,256,2048]{2,1,0:T(8,128)(2,1)S(1)}, f32[512,2048]{1,0:T(8,128)S(1)}, f32[512,2048]{1,0:T(8,128)}, f32[1,2048]{1,0:T(1,128)S(1)}, bf16[16,2048]{1,0:T(8,128)(2,1)S(1)}) custom-call(s32[1]{0:T(128)} %bitcast.7.meta, bf16[227,2048]{1,0:T(8,128)(2,1)S(1)} %bitcast.130, bf16[227,512]{1,0:T(8,128)(2,1)S(1)} %copy-done.30, ...), custom_call_target="tpu_custom_call" | custom-call | flops 1549795328 | bytes 12582912 | tf_op jit(solution)/shard_map/forward/pallas_call | solution.py:98
  75.5 32.3 %collective-permute-done.1.refs_4_.refs_16_.refs_3_ = bf16[8,2,128,128]{3,2,1,0:T(8,128)(2,1)S(1)} collective-permute-done((bf16[8,2,128,128]{3,2,1,0:T(8,128)(2,1)S(1)}, bf16[8,2,128,128]{3,2,1,0:T(8,128)(2,1)S(1)}, u32[]{:S(2)}, u32[]{:S(2)}) %collective-permute-start.1) | collective-permute-done | bytes 524320 | tf_op jit(solution)/shard_map/ppermute | solution.py:438
  107.8 10.4 %collective-permute-done.5.refs_8_.refs_20_.refs_7_ = bf16[8,2,128,128]{3,2,1,0:T(8,128)(2,1)S(1)} collective-permute-done((bf16[8,2,128,128]{3,2,1,0:T(8,128)(2,1)S(1)}, bf16[8,2,128,128]{3,2,1,0:T(8,128)(2,1)S(1)}, u32[]{:S(2)}, u32[]{:S(2)}) %collective-permute-start.5) | collective-permute-done | bytes 524320 | tf_op jit(solution)/shard_map/ppermute | solution.py:438
  165.6 6.5 %collective-permute-done.48 = bf16[12,128,128]{2,1,0:T(8,128)(2,1)S(1)} collective-permute-done((bf16[12,128,128]{2,1,0:T(8,128)(2,1)S(1)}, bf16[12,128,128]{2,1,0:T(8,128)(2,1)S(1)}, u32[]{:S(2)}, u32[]{:S(2)}) %collective-permute-start.48) | collective-permute-done | bytes 393248 | tf_op jit(solution)/shard_map/ppermute | solution.py:363
  208.3 5.0 %collective-permute-start.71 = (bf16[12,128,128]{2,1,0:T(8,128)(2,1)S(1)}, bf16[12,128,128]{2,1,0:T(8,128)(2,1)S(1)}, u32[]{:S(2)}, u32[]{:S(2)}) collective-permute-start(bf16[12,128,128]{2,1,0:T(8,128)(2,1)S(1)} %get-tuple-element.27), channel_id=1, source_target_pairs={{0,4},{4,8},{8,12},{1,5},{5,9},{9,13},{2,6},{6,10},{10,14},{3,7},{... | collective-permute-start | bytes 1179656 | tf_op jit(solution)/shard_map/ppermute | solution.py:363
  216.5 5.0 %collective-permute-start.50 = (bf16[12,128,128]{2,1,0:T(8,128)(2,1)S(1)}, bf16[12,128,128]{2,1,0:T(8,128)(2,1)S(1)}, u32[]{:S(2)}, u32[]{:S(2)}) collective-permute-start(bf16[12,128,128]{2,1,0:T(8,128)(2,1)S(1)} %get-tuple-element.31), channel_id=1, source_target_pairs={{0,4},{4,8},{8,12},{1,5},{5,9},{9,13},{2,6},{6,10},{10,14},{3,7},{... | collective-permute-start | bytes 1179656 | tf_op jit(solution)/shard_map/ppermute | solution.py:363
  235.8 8.8 %collective-permute-done.74 = bf16[12,128,128]{2,1,0:T(8,128)(2,1)S(1)} collective-permute-done((bf16[12,128,128]{2,1,0:T(8,128)(2,1)S(1)}, bf16[12,128,128]{2,1,0:T(8,128)(2,1)S(1)}, u32[]{:S(2)}, u32[]{:S(2)}) %collective-permute-start.74) | collective-permute-done | bytes 393248 | tf_op jit(solution)/shard_map/ppermute | solution.py:364
  255.7 9.7 %collective-permute-start.54 = (bf16[12,128,128]{2,1,0:T(8,128)(2,1)S(1)}, bf16[12,128,128]{2,1,0:T(8,128)(2,1)S(1)}, u32[]{:S(2)}, u32[]{:S(2)}) collective-permute-start(bf16[12,128,128]{2,1,0:T(8,128)(2,1)S(1)} %fusion.11.refs_0_), channel_id=1, source_target_pairs={{0,4},{4,8},{8,12},{1,5},{5,9},{9,13},{2,6},{6,10},{10,14},{3,7},{... | collective-permute-start | bytes 1179656 | tf_op jit(solution)/shard_map/ppermute | solution.py:375
  270.6 9.0 %collective-permute-done.57.refs_4_ = bf16[12,128,128]{2,1,0:T(8,128)(2,1)S(1)} collective-permute-done((bf16[12,128,128]{2,1,0:T(8,128)(2,1)S(1)}, bf16[12,128,128]{2,1,0:T(8,128)(2,1)S(1)}, u32[]{:S(2)}, u32[]{:S(2)}) %collective-permute-start.57) | collective-permute-done | bytes 393248 | tf_op jit(solution)/shard_map/ppermute | solution.py:377
  281.1 7.0 %collective-permute-done.79.refs_5_ = bf16[12,128,128]{2,1,0:T(8,128)(2,1)S(1)} collective-permute-done((bf16[12,128,128]{2,1,0:T(8,128)(2,1)S(1)}, bf16[12,128,128]{2,1,0:T(8,128)(2,1)S(1)}, u32[]{:S(2)}, u32[]{:S(2)}) %collective-permute-start.79) | collective-permute-done | bytes 393248 | tf_op jit(solution)/shard_map/ppermute | solution.py:377
  291.4 15.3 %collective-permute-done.80.refs_6_ = bf16[12,128,128]{2,1,0:T(8,128)(2,1)S(1)} collective-permute-done((bf16[12,128,128]{2,1,0:T(8,128)(2,1)S(1)}, bf16[12,128,128]{2,1,0:T(8,128)(2,1)S(1)}, u32[]{:S(2)}, u32[]{:S(2)}) %collective-permute-start.80) | collective-permute-done | bytes 393248 | tf_op jit(solution)/shard_map/ppermute | solution.py:377
  306.9 5.9 %collective-permute-done.58.refs_5_ = bf16[12,128,128]{2,1,0:T(8,128)(2,1)S(1)} collective-permute-done((bf16[12,128,128]{2,1,0:T(8,128)(2,1)S(1)}, bf16[12,128,128]{2,1,0:T(8,128)(2,1)S(1)}, u32[]{:S(2)}, u32[]{:S(2)}) %collective-permute-start.58) | collective-permute-done | bytes 393248 | tf_op jit(solution)/shard_map/ppermute | solution.py:377
  316.6 6.3 %decode.7 = bf16[2,128,2048]{2,1,0:T(8,128)(2,1)} custom-call(s32[8,16]{1,0:T(8,128)S(1)} %get-tuple-element.52.tab_j, s32[8,16]{1,0:T(8,128)S(1)} %get-tuple-element.53.tab_m, s32[3]{0:T(128)S(1)} %add_add_fusion.meta, bf16[12,128,128]{2,1,0:T(8,128)(2,1)S(1)} %fusion.5.refs_0_, bf16[12,128,128]{2,1,0:T(8,128)(2,1)S(1)} %collective-permute-done.75.refs_1_, ...), custom_call_target="tpu_custom_call" | custom-call | flops 2147483648 | bytes 6291456 | tf_op jit(solution)/shard_map/decode/pallas_call | solution.py:316
  338.3 6.3 %decode.6 = bf16[2,128,2048]{2,1,0:T(8,128)(2,1)} custom-call(s32[8,16]{1,0:T(8,128)S(1)} %get-tuple-element.52.tab_j, s32[8,16]{1,0:T(8,128)S(1)} %get-tuple-element.53.tab_m, s32[3]{0:T(128)S(1)} %add_add_fusion.meta, bf16[12,128,128]{2,1,0:T(8,128)(2,1)S(1)} %fusion.11.refs_0_, bf16[12,128,128]{2,1,0:T(8,128)(2,1)S(1)} %collective-permute-done.54.refs_1_, ...), custom_call_target="tpu_custom_call" | custom-call | flops 2147483648 | bytes 6291456 | tf_op jit(solution)/shard_map/decode/pallas_call | solution.py:316
  349.9 5.3 %collective-permute-start.14 = (bf16[12,128,128]{2,1,0:T(8,128)(2,1)}, bf16[12,128,128]{2,1,0:T(8,128)(2,1)}, u32[]{:S(2)}, u32[]{:S(2)}) collective-permute-start(bf16[12,128,128]{2,1,0:T(8,128)(2,1)} %fusion.23.refs_0_), channel_id=1, source_target_pairs={{0,4},{4,8},{8,12},{1,5},{5,9},{9,13},{2,6},{6,10},{10,14},{3,7},{... | collective-permute-start | bytes 1179656 | tf_op jit(solution)/shard_map/ppermute | solution.py:375
  357.3 5.9 %collective-permute-done.14.refs_1_ = bf16[12,128,128]{2,1,0:T(8,128)(2,1)} collective-permute-done((bf16[12,128,128]{2,1,0:T(8,128)(2,1)}, bf16[12,128,128]{2,1,0:T(8,128)(2,1)}, u32[]{:S(2)}, u32[]{:S(2)}) %collective-permute-start.14) | collective-permute-done | bytes 393248 | tf_op jit(solution)/shard_map/ppermute | solution.py:375
  382.3 7.1 %backward.1 = (f32[16,512]{1,0:T(8,128)S(1)}, f32[16,227]{1,0:T(8,128)S(1)}) custom-call(s32[4]{0:T(128)S(1)} %pad_add_fusion.1.offs, bf16[128,2048]{1,0:T(8,128)(2,1)S(1)} %copy-done.12, bf16[128,2048]{1,0:T(8,128)(2,1)} %collective-permute-done.67.refs_1_, bf16[128,2048]{1,0:T(8,128)(2,1)S(1)} %copy-done.11, ...), custom_call_target="tpu_custom_call" | custom-call | flops 1073741824 | bytes 10485760 | tf_op jit(solution)/shard_map/backward/pallas_call | solution.py:168
  393.5 12.0 %collective-permute-done.18.refs_5_ = bf16[12,128,128]{2,1,0:T(8,128)(2,1)S(1)} collective-permute-done((bf16[12,128,128]{2,1,0:T(8,128)(2,1)}, bf16[12,128,128]{2,1,0:T(8,128)(2,1)S(1)}, u32[]{:S(2)}, u32[]{:S(2)}) %collective-permute-start.18) | collective-permute-done | bytes 393248 | tf_op jit(solution)/shard_map/ppermute | solution.py:377
  407.8 6.0 %collective-permute-done.39.refs_6_ = bf16[12,128,128]{2,1,0:T(8,128)(2,1)S(1)} collective-permute-done((bf16[12,128,128]{2,1,0:T(8,128)(2,1)S(1)}, bf16[12,128,128]{2,1,0:T(8,128)(2,1)S(1)}, u32[]{:S(2)}, u32[]{:S(2)}) %collective-permute-start.39) | collective-permute-done | bytes 393248 | tf_op jit(solution)/shard_map/ppermute | solution.py:377
  418.6 8.5 %collective-permute-done.19.refs_6_ = bf16[12,128,128]{2,1,0:T(8,128)(2,1)S(1)} collective-permute-done((bf16[12,128,128]{2,1,0:T(8,128)(2,1)S(1)}, bf16[12,128,128]{2,1,0:T(8,128)(2,1)S(1)}, u32[]{:S(2)}, u32[]{:S(2)}) %collective-permute-start.19) | collective-permute-done | bytes 393248 | tf_op jit(solution)/shard_map/ppermute | solution.py:377
  428.2 6.3 %decode.4.refs_22_ = bf16[256,4096]{1,0:T(8,128)(2,1)} custom-call(s32[8,16]{1,0:T(8,128)S(1)} %get-tuple-element.52.tab_j, s32[8,16]{1,0:T(8,128)S(1)} %get-tuple-element.53.tab_m, s32[3]{0:T(128)S(1)} %add_add_fusion.meta, bf16[12,128,128]{2,1,0:T(8,128)(2,1)S(1)} %fusion.17.refs_0_, bf16[12,128,128]{2,1,0:T(8,128)(2,1)S(1)} %copy-done.19, ...), custom_call_target="tpu_custom_call" | custom-call | flops 2147483648 | bytes 6291456 | tf_op jit(solution)/shard_map/decode/pallas_call | solution.py:316
  434.6 5.6 %decode.5 = bf16[256,4096]{1,0:T(8,128)(2,1)} custom-call(s32[8,16]{1,0:T(8,128)S(1)} %get-tuple-element.52.tab_j, s32[8,16]{1,0:T(8,128)S(1)} %get-tuple-element.53.tab_m, s32[3]{0:T(128)S(1)} %add_add_fusion.meta, bf16[12,128,128]{2,1,0:T(8,128)(2,1)} %fusion.23.refs_0_, ...), custom_call_target="tpu_custom_call", output_to_operand_aliasing={{}: (25, {})} | custom-call | flops 2147483648 | bytes 6291456 | tf_op jit(solution)/shard_map/decode/pallas_call | solution.py:316
  (297 shorter events, 216.2 us)
Async XLA Ops:
  64.0 62.7 %collective-permute-start = (bf16[256,2048]{1,0:T(8,128)(2,1)}, bf16[256,2048]{1,0:T(8,128)(2,1)}, u32[]{:S(2)}, u32[]{:S(2)}) collective-permute-start(bf16[256,2048]{1,0:T(8,128)(2,1)} %get-tuple-element.43), channel_id=1, source_target_pairs={{0,2},{2,0},{1,3},{3,1},{4,6},{6,4},{5,7},{7,5},{8,10},{10,8},{9,1... | collective-permute-start | bytes 3145736 | tf_op jit(solution)/shard_map/ppermute | solution.py:464
  64.9 42.9 %collective-permute-start.1 = (bf16[8,2,128,128]{3,2,1,0:T(8,128)(2,1)S(1)}, bf16[8,2,128,128]{3,2,1,0:T(8,128)(2,1)S(1)}, u32[]{:S(2)}, u32[]{:S(2)}) collective-permute-start(bf16[8,2,128,128]{3,2,1,0:T(8,128)(2,1)S(1)} %all_to_all.10.refs_2_.refs_14_.refs_1_), channel_id=1, source_target_pairs={{0,2},{2,0},{1,3},{3,1},{4,6},{6,4},{5,7},{7,5},{8,10},{10,8},{9,1... | collective-permute-start | bytes 1572872 | tf_op jit(solution)/shard_map/ppermute | solution.py:438
  66.5 41.3 %collective-permute-start.4 = (bf16[8,2,128,128]{3,2,1,0:T(8,128)(2,1)S(1)}, bf16[8,2,128,128]{3,2,1,0:T(8,128)(2,1)S(1)}, u32[]{:S(2)}, u32[]{:S(2)}) collective-permute-start(bf16[8,2,128,128]{3,2,1,0:T(8,128)(2,1)S(1)} %all-to-all-done.1.refs_3_.refs_15_.refs_2_), channel_id=1, source_target_pairs={{0,16},{16,0},{1,17},{17,1},{2,18},{18,2},{3,19},{19,3},{4,20},{20... | collective-permute-start | bytes 1572872 | tf_op jit(solution)/shard_map/ppermute | solution.py:439
  72.0 46.2 %collective-permute-start.5 = (bf16[8,2,128,128]{3,2,1,0:T(8,128)(2,1)S(1)}, bf16[8,2,128,128]{3,2,1,0:T(8,128)(2,1)S(1)}, u32[]{:S(2)}, u32[]{:S(2)}) collective-permute-start(bf16[8,2,128,128]{3,2,1,0:T(8,128)(2,1)S(1)} %collective-permute-done.3.refs_6_.refs_18_.refs_5_), channel_id=1, source_target_pairs={{0,2},{2,0},{1,3},{3,1},{4,6},{6,4},{5,7},{7,5},{8,10},{10,8},{9,1... | collective-permute-start | bytes 1572872 | tf_op jit(solution)/shard_map/ppermute | solution.py:438
  74.1 44.2 %collective-permute-start.6 = (bf16[8,2,128,128]{3,2,1,0:T(8,128)(2,1)S(1)}, bf16[8,2,128,128]{3,2,1,0:T(8,128)(2,1)S(1)}, u32[]{:S(2)}, u32[]{:S(2)}) collective-permute-start(bf16[8,2,128,128]{3,2,1,0:T(8,128)(2,1)S(1)} %collective-permute-done.2.refs_5_.refs_17_.refs_4_), channel_id=1, source_target_pairs={{0,16},{16,0},{1,17},{17,1},{2,18},{18,2},{3,19},{19,3},{4,20},{20... | collective-permute-start | bytes 1572872 | tf_op jit(solution)/shard_map/ppermute | solution.py:439
  123.1 26.2 %collective-permute-start.68 = (bf16[4,12,128,128]{3,2,1,0:T(8,128)(2,1)S(1)}, bf16[4,12,128,128]{3,2,1,0:T(8,128)(2,1)}, u32[]{:S(2)}, u32[]{:S(2)}) collective-permute-start(bf16[4,12,128,128]{3,2,1,0:T(8,128)(2,1)S(1)} %encode.15), channel_id=1, source_target_pairs={{0,1},{1,0},{2,3},{3,2},{4,5},{5,4},{6,7},{7,6},{8,9},{9,8},{10,11... | collective-permute-start | bytes 4718600 | tf_op jit(solution)/shard_map/ppermute | solution.py:354
  126.1 28.9 %collective-permute-start.47 = (bf16[4,12,128,128]{3,2,1,0:T(8,128)(2,1)S(1)}, bf16[4,12,128,128]{3,2,1,0:T(8,128)(2,1)}, u32[]{:S(2)}, u32[]{:S(2)}) collective-permute-start(bf16[4,12,128,128]{3,2,1,0:T(8,128)(2,1)S(1)} %encode.13), channel_id=1, source_target_pairs={{0,1},{1,0},{2,3},{3,2},{4,5},{5,4},{6,7},{7,6},{8,9},{9,8},{10,11... | collective-permute-start | bytes 4718600 | tf_op jit(solution)/shard_map/ppermute | solution.py:354
  130.7 27.0 %collective-permute-start.27 = (bf16[4,12,128,128]{3,2,1,0:T(8,128)(2,1)S(1)}, bf16[4,12,128,128]{3,2,1,0:T(8,128)(2,1)}, u32[]{:S(2)}, u32[]{:S(2)}) collective-permute-start(bf16[4,12,128,128]{3,2,1,0:T(8,128)(2,1)S(1)} %encode.11), channel_id=1, source_target_pairs={{0,1},{1,0},{2,3},{3,2},{4,5},{5,4},{6,7},{7,6},{8,9},{9,8},{10,11... | collective-permute-start | bytes 4718600 | tf_op jit(solution)/shard_map/ppermute | solution.py:354
  134.8 25.0 %collective-permute-start.7 = (bf16[4,12,128,128]{3,2,1,0:T(8,128)(2,1)S(1)}, bf16[4,12,128,128]{3,2,1,0:T(8,128)(2,1)S(1)}, u32[]{:S(2)}, u32[]{:S(2)}) collective-permute-start(bf16[4,12,128,128]{3,2,1,0:T(8,128)(2,1)S(1)} %encode.9), channel_id=1, source_target_pairs={{0,1},{1,0},{2,3},{3,2},{4,5},{5,4},{6,7},{7,6},{8,9},{9,8},{10,11... | collective-permute-start | bytes 4718600 | tf_op jit(solution)/shard_map/ppermute | solution.py:354
  154.3 39.3 %collective-permute-start.72 = (bf16[12,128,128]{2,1,0:T(8,128)(2,1)S(1)}, bf16[12,128,128]{2,1,0:T(8,128)(2,1)S(1)}, u32[]{:S(2)}, u32[]{:S(2)}) collective-permute-start(bf16[12,128,128]{2,1,0:T(8,128)(2,1)S(1)} %get-tuple-element.30), channel_id=1, source_target_pairs={{12,8},{13,9},{14,10},{15,11},{28,24},{29,25},{30,26},{31,27}} | collective-permute-start | bytes 1179656 | tf_op jit(solution)/shard_map/ppermute | solution.py:364
  157.7 45.7 %collective-permute-start.51 = (bf16[12,128,128]{2,1,0:T(8,128)(2,1)S(1)}, bf16[12,128,128]{2,1,0:T(8,128)(2,1)S(1)}, u32[]{:S(2)}, u32[]{:S(2)}) collective-permute-start(bf16[12,128,128]{2,1,0:T(8,128)(2,1)S(1)} %get-tuple-element.34), channel_id=1, source_target_pairs={{12,8},{13,9},{14,10},{15,11},{28,24},{29,25},{30,26},{31,27}} | collective-permute-start | bytes 1179656 | tf_op jit(solution)/shard_map/ppermute | solution.py:364
  163.7 44.6 %collective-permute-start.31 = (bf16[12,128,128]{2,1,0:T(8,128)(2,1)S(1)}, bf16[12,128,128]{2,1,0:T(8,128)(2,1)S(1)}, u32[]{:S(2)}, u32[]{:S(2)}) collective-permute-start(bf16[12,128,128]{2,1,0:T(8,128)(2,1)S(1)} %get-tuple-element.38), channel_id=1, source_target_pairs={{12,8},{13,9},{14,10},{15,11},{28,24},{29,25},{30,26},{31,27}} | collective-permute-start | bytes 1179656 | tf_op jit(solution)/shard_map/ppermute | solution.py:364
  193.6 22.9 %collective-permute-start.11 = (bf16[12,128,128]{2,1,0:T(8,128)(2,1)S(1)}, bf16[12,128,128]{2,1,0:T(8,128)(2,1)S(1)}, u32[]{:S(2)}, u32[]{:S(2)}) collective-permute-start(bf16[12,128,128]{2,1,0:T(8,128)(2,1)S(1)} %get-tuple-element.42), channel_id=1, source_target_pairs={{12,8},{13,9},{14,10},{15,11},{28,24},{29,25},{30,26},{31,27}} | collective-permute-start | bytes 1179656 | tf_op jit(solution)/shard_map/ppermute | solution.py:364
  208.3 26.7 %collective-permute-start.71 = (bf16[12,128,128]{2,1,0:T(8,128)(2,1)S(1)}, bf16[12,128,128]{2,1,0:T(8,128)(2,1)S(1)}, u32[]{:S(2)}, u32[]{:S(2)}) collective-permute-start(bf16[12,128,128]{2,1,0:T(8,128)(2,1)S(1)} %get-tuple-element.27), channel_id=1, source_target_pairs={{0,4},{4,8},{8,12},{1,5},{5,9},{9,13},{2,6},{6,10},{10,14},{3,7},{... | collective-permute-start | bytes 1179656 | tf_op jit(solution)/shard_map/ppermute | solution.py:363
  216.5 30.6 %collective-permute-start.50 = (bf16[12,128,128]{2,1,0:T(8,128)(2,1)S(1)}, bf16[12,128,128]{2,1,0:T(8,128)(2,1)S(1)}, u32[]{:S(2)}, u32[]{:S(2)}) collective-permute-start(bf16[12,128,128]{2,1,0:T(8,128)(2,1)S(1)} %get-tuple-element.31), channel_id=1, source_target_pairs={{0,4},{4,8},{8,12},{1,5},{5,9},{9,13},{2,6},{6,10},{10,14},{3,7},{... | collective-permute-start | bytes 1179656 | tf_op jit(solution)/shard_map/ppermute | solution.py:363
  223.8 31.8 %collective-permute-start.30 = (bf16[12,128,128]{2,1,0:T(8,128)(2,1)S(1)}, bf16[12,128,128]{2,1,0:T(8,128)(2,1)S(1)}, u32[]{:S(2)}, u32[]{:S(2)}) collective-permute-start(bf16[12,128,128]{2,1,0:T(8,128)(2,1)S(1)} %get-tuple-element.35), channel_id=1, source_target_pairs={{0,4},{4,8},{8,12},{1,5},{5,9},{9,13},{2,6},{6,10},{10,14},{3,7},{... | collective-permute-start | bytes 1179656 | tf_op jit(solution)/shard_map/ppermute | solution.py:363
  289.4 23.4 %collective-permute-start.58 = (bf16[12,128,128]{2,1,0:T(8,128)(2,1)S(1)}, bf16[12,128,128]{2,1,0:T(8,128)(2,1)S(1)}, u32[]{:S(2)}, u32[]{:S(2)}) collective-permute-start(bf16[12,128,128]{2,1,0:T(8,128)(2,1)S(1)} %collective-permute-done.57.refs_4_), channel_id=1, source_target_pairs={{4,0},{8,4},{5,1},{9,5},{6,2},{10,6},{7,3},{11,7},{20,16},{24,20},... | collective-permute-start | bytes 1179656 | tf_op jit(solution)/shard_map/ppermute | solution.py:377
  290.7 22.0 %collective-permute-start.83 = (bf16[12,128,128]{2,1,0:T(8,128)(2,1)S(1)}, bf16[12,128,128]{2,1,0:T(8,128)(2,1)S(1)}, u32[]{:S(2)}, u32[]{:S(2)}) collective-permute-start(bf16[12,128,128]{2,1,0:T(8,128)(2,1)S(1)} %collective-permute-done.76.refs_2_), channel_id=1, source_target_pairs={{0,1},{1,0},{2,3},{3,2},{4,5},{5,4},{6,7},{7,6},{8,9},{9,8},{10,11... | collective-permute-start | bytes 1179656 | tf_op jit(solution)/shard_map/ppermute | solution.py:354
  290.8 22.5 %collective-permute-start.86 = (bf16[12,128,128]{2,1,0:T(8,128)(2,1)S(1)}, bf16[12,128,128]{2,1,0:T(8,128)(2,1)S(1)}, u32[]{:S(2)}, u32[]{:S(2)}) collective-permute-start(bf16[12,128,128]{2,1,0:T(8,128)(2,1)S(1)} %collective-permute-done.79.refs_5_), channel_id=1, source_target_pairs={{0,1},{1,0},{2,3},{3,2},{4,5},{5,4},{6,7},{7,6},{8,9},{9,8},{10,11... | collective-permute-start | bytes 1179656 | tf_op jit(solution)/shard_map/ppermute | solution.py:354
  291.3 22.7 %collective-permute-start.84 = (bf16[12,128,128]{2,1,0:T(8,128)(2,1)S(1)}, bf16[12,128,128]{2,1,0:T(8,128)(2,1)S(1)}, u32[]{:S(2)}, u32[]{:S(2)}) collective-permute-start(bf16[12,128,128]{2,1,0:T(8,128)(2,1)S(1)} %collective-permute-done.77.refs_3_), channel_id=1, source_target_pairs={{0,1},{1,0},{2,3},{3,2},{4,5},{5,4},{6,7},{7,6},{8,9},{9,8},{10,11... | collective-permute-start | bytes 1179656 | tf_op jit(solution)/shard_map/ppermute | solution.py:354
  346.9 22.5 %collective-permute-start.88 = (bf16[128,2048]{1,0:T(8,128)(2,1)}, bf16[128,2048]{1,0:T(8,128)(2,1)}, u32[]{:S(2)}, u32[]{:S(2)}) collective-permute-start(bf16[128,2048]{1,0:T(8,128)(2,1)} %get-tuple-element.45), channel_id=1, source_target_pairs={{0,2},{2,0},{1,3},{3,1},{4,6},{6,4},{5,7},{7,5},{8,10},{10,8},{9,1... | collective-permute-start | bytes 1572872 | tf_op jit(solution)/shard_map/ppermute | solution.py:464
  348.4 24.3 %collective-permute-start.67 = (bf16[128,2048]{1,0:T(8,128)(2,1)}, bf16[128,2048]{1,0:T(8,128)(2,1)}, u32[]{:S(2)}, u32[]{:S(2)}) collective-permute-start(bf16[128,2048]{1,0:T(8,128)(2,1)} %get-tuple-element.47), channel_id=1, source_target_pairs={{0,2},{2,0},{1,3},{3,1},{4,6},{6,4},{5,7},{7,5},{8,10},{10,8},{9,1... | collective-permute-start | bytes 1572872 | tf_op jit(solution)/shard_map/ppermute | solution.py:464
  363.2 26.3 %collective-permute-start.35 = (bf16[12,128,128]{2,1,0:T(8,128)(2,1)}, bf16[12,128,128]{2,1,0:T(8,128)(2,1)S(1)}, u32[]{:S(2)}, u32[]{:S(2)}) collective-permute-start(bf16[12,128,128]{2,1,0:T(8,128)(2,1)} %copy-done.18), channel_id=1, source_target_pairs={{4,8},{8,12},{5,9},{9,13},{6,10},{10,14},{7,11},{11,15},{20,24},{2... | collective-permute-start | bytes 1179656 | tf_op jit(solution)/shard_map/ppermute | solution.py:375
  368.1 22.8 %collective-permute-start.41 = (bf16[12,128,128]{2,1,0:T(8,128)(2,1)}, bf16[12,128,128]{2,1,0:T(8,128)(2,1)S(1)}, u32[]{:S(2)}, u32[]{:S(2)}) collective-permute-start(bf16[12,128,128]{2,1,0:T(8,128)(2,1)} %copy-done.18), channel_id=1, source_target_pairs={{0,1},{1,0},{2,3},{3,2},{4,5},{5,4},{6,7},{7,6},{8,9},{9,8},{10,11... | collective-permute-start | bytes 1179656 | tf_op jit(solution)/shard_map/ppermute | solution.py:354
  (102 other events, 1807.3 us)

commit v2 on v1

--- a/solution.py
+++ b/solution.py
@@ -10,7 +10,7 @@
 MBLK = 12
 BF = jnp.bfloat16
 F32 = jnp.float32
-VMEM_LIMIT = 44 * 1024 * 1024
+VMEM_LIMIT = 28 * 1024 * 1024
 
 
 def params(**kw):
@@ -32,43 +32,35 @@
     return jnp.sum(jnp.where(before, mask[..., None, :], 0), axis=-1)
 
 
-def pack_kernel(src, interp, *rest):
-    outs, sem = rest[:-1], rest[-1]
+def pack_kernel(src, interp, *outs):
     pairs, width = outs[0].shape[0], outs[0].shape[1]
-    copies = []
     for h, out in enumerate(outs):
         for o in range(pairs):
             for c in range(width):
-                copies.append(
-                    pltpu.make_async_copy(
-                        interp.at[src[o, h * width + c]], out.at[o, c], sem.at[len(copies)]
-                    )
-                )
-    for copy in copies:
-        copy.start()
-    for copy in copies:
-        copy.wait()
+                out[o, c] = interp[src[o, h * width + c]]
 
 
 def pack(src, values, pieces):
     pairs, width = src.shape[0], src.shape[1] // pieces
     block = values.shape[1]
+    shape = (pairs, width, block, block)
     return pl.pallas_call(
         pack_kernel,
         grid_spec=pltpu.PrefetchScalarGridSpec(
             num_scalar_prefetch=1,
             grid=(1,),
-            in_specs=[pl.BlockSpec(memory_space=pl.ANY)],
-            out_specs=[pl.BlockSpec(memory_space=pl.ANY)] * pieces,
-            scratch_shapes=[pltpu.SemaphoreType.DMA((pairs * src.shape[1],))],
-        ),
-        out_shape=[jax.ShapeDtypeStruct((pairs, width, block, block), BF)] * pieces,
+            in_specs=[pl.BlockSpec(values.shape, lambda i, t: (0, 0, 0))],
+            out_specs=[pl.BlockSpec(shape, lambda i, t: (0, 0, 0, 0))] * pieces,
+        ),
+        out_shape=[jax.ShapeDtypeStruct(shape, BF)] * pieces,
         compiler_params=params(),
         name="pack",
     )(src, values)
 
 
-def forward_kernel(meta, x, w_in, a_down, a_up, w_out, emb, normed, slope, inv, mid, hold):
+def forward_kernel(meta, x, w_in, a_down, a_up, w_out, *rest, nf, deps):
+    embs, rest = rest[deps : deps + nf], rest[deps + nf :]
+    normed, slope, inv, mid, hold = rest
     feats = x[...]
     middle = dg(a_down[...], feats, 0, 0).astype(BF)
     pre = dg(w_in[...], feats, 0, 0) + dg(a_up[...], middle, 0, 0)
@@ -83,20 +75,20 @@
     inv[...] = istd
     mid[...] = middle
     hold[...] = norm.astype(BF)
-    nf, chans = emb.shape[0], emb.shape[1]
-    for r in range(nf):
+    chans = embs[0].shape[0]
+    for r, emb in enumerate(embs):
         at = lax.rem(meta[0] + r, nf) * chans
-        emb[r] = hold[pl.ds(pl.multiple_of(at, chans), chans), :]
-
-
-def forward(meta, x, w_in, a_down, a_up, w_out, nf):
+        emb[...] = hold[pl.ds(pl.multiple_of(at, chans), chans), :]
+
+
+def forward(meta, x, w_in, a_down, a_up, w_out, nf, deps):
     width, rows = w_out.shape[0], x.shape[1]
     rank = a_down.shape[1]
     step = min(512, rows)
     chans = width // nf
     full = lambda a: pl.BlockSpec(a.shape, lambda i, m: (0, 0))
     return pl.pallas_call(
-        forward_kernel,
+        functools.partial(forward_kernel, nf=nf, deps=len(deps)),
         grid_spec=pltpu.PrefetchScalarGridSpec(
             num_scalar_prefetch=1,
             grid=(rows // step,),
@@ -106,9 +98,10 @@
                 full(a_down),
                 full(a_up),
                 full(w_out),
-            ],
-            out_specs=[
-                pl.BlockSpec((nf, chans, step), lambda i, m: (0, 0, i)),
+            ]
+            + [pl.BlockSpec(memory_space=pl.ANY)] * len(deps),
+            out_specs=[pl.BlockSpec((chans, step), lambda i, m: (0, i))] * nf
+            + [
                 pl.BlockSpec((width, step), lambda i, m: (0, i)),
                 pl.BlockSpec((width, step), lambda i, m: (0, i)),
                 pl.BlockSpec((1, step), lambda i, m: (0, i)),
@@ -116,8 +109,8 @@
             ],
             scratch_shapes=[pltpu.VMEM((width, step), BF)],
         ),
-        out_shape=[
-            jax.ShapeDtypeStruct((nf, chans, rows), BF),
+        out_shape=[jax.ShapeDtypeStruct((chans, rows), BF)] * nf
+        + [
             jax.ShapeDtypeStruct((width, rows), F32),
             jax.ShapeDtypeStruct((width, rows), F32),
             jax.ShapeDtypeStruct((1, rows), F32),
@@ -128,7 +121,7 @@
             flops=2 * rows * width * (width + x.shape[0]), bytes_accessed=rows * width * 12, transcendentals=0
         ),
         name="forward",
-    )(meta, x, w_in, a_down, a_up, w_out)
+    )(meta, x, w_in, a_down, a_up, w_out, *deps)
 
 
 def backward_kernel(offs, *refs, count):
@@ -190,8 +183,9 @@
     )(offs, *pieces, normed, slope, inv, mid, x, w_out, a_up)
 
 
-def encode_kernel(tab_j, tab_m, meta, *refs, panels, weights, n, ns):
+def encode_kernel(tab_j, tab_m, meta, *refs, panels, weights, deps, n, ns):
     xs, ws = refs[:panels], refs[panels : panels + weights]
+    refs = refs[: panels + weights] + refs[panels + weights + deps :]
     out, acc = refs[panels + weights], refs[panels + weights + 1]
     r = pl.program_id(0)
     p = lax.rem(meta[0] + r, n) * ns + meta[1]
@@ -220,7 +214,7 @@
     out[0] = acc[0 : out.shape[1]].astype(BF)
 
 
-def encode(tab_j, tab_m, meta, pieces, chunk, chunks, weights, n, ns):
+def encode(tab_j, tab_m, meta, pieces, chunk, chunks, weights, deps, n, ns):
     chans, wide = pieces[0].shape[0] // chunks, pieces[0].shape[1]
     panels = len(pieces)
     block = weights[0].shape[2]
@@ -230,12 +224,15 @@
         scratch.append(pltpu.VMEM((chans, wide * panels), BF))
     where = lambda r, j, m, t: (lax.rem(t[0] + r, n) * ns + t[1], 0, 0, 0)
     return pl.pallas_call(
-        functools.partial(encode_kernel, panels=panels, weights=len(weights), n=n, ns=ns),
+        functools.partial(
+            encode_kernel, panels=panels, weights=len(weights), deps=len(deps), n=n, ns=ns
+        ),
         grid_spec=pltpu.PrefetchScalarGridSpec(
             num_scalar_prefetch=3,
             grid=(n,),
             in_specs=[pl.BlockSpec((chans, wide), lambda r, j, m, t: (chunk, 0))] * panels
-            + [pl.BlockSpec((1,) + w.shape[1:], where) for w in weights],
+            + [pl.BlockSpec((1,) + w.shape[1:], where) for w in weights]
+            + [pl.BlockSpec(memory_space=pl.ANY)] * len(deps),
             out_specs=pl.BlockSpec((1, MBLK, chans, block), lambda r, j, m, t: (r, 0, 0, 0)),
             scratch_shapes=scratch,
         ),
@@ -247,42 +244,24 @@
             transcendentals=0,
         ),
         name="encode",
-    )(tab_j, tab_m, meta, *pieces, *weights)
-
-
-def decode_kernel(tab_j, tab_m, meta, *refs, n, ns, weights, alias, split):
-    count = 2 * n - 1
-    mine, theirs = refs[:count], refs[count : 2 * count]
-    ws = refs[2 * count : 2 * count + weights]
-    rest = refs[2 * count + weights + (1 if alias else 0) :]
-    out, hold, acc, sem = rest
+    )(tab_j, tab_m, meta, *pieces, *weights, *deps)
+
+
+def decode_kernel(tab_j, tab_m, meta, *refs, n, ns, weights, alias, nf):
+    here, there, refs = refs[:n], refs[n : 2 * n], refs[2 * n :]
+    ws, rest = refs[:weights], refs[weights + (1 if alias else 0) :]
+    outs, (hold, acc, sem) = rest[:-3], rest[-3:]
     z, s = meta[0], meta[1]
     block = hold.shape[3]
-
-    def copies(side, group, go):
-        for r in range(n):
+    for r in range(n):
+        for side, mesh in enumerate((here[r], there[r])):
             at = r * ns + side
-            if r == 0:
-                go(pltpu.make_async_copy(group[0], hold.at[at], sem.at[at]))
-                continue
-            below, above = group[n - r], group[n - 1 + r]
-
-            @pl.when(z + r < n)
-            def _():
-                go(pltpu.make_async_copy(above, hold.at[at], sem.at[at]))
-
-            @pl.when(z + r >= n)
-            def _():
-                go(pltpu.make_async_copy(below, hold.at[at], sem.at[at]))
-
-    for side, group in enumerate((mine, theirs)):
-        copies(side, group, lambda c: c.start())
+            pltpu.make_async_copy(mesh, hold.at[at], sem.at[at]).start()
     acc[...] = jnp.zeros_like(acc)
 
     def step(i, carry):
-        r, side = i // ns, lax.rem(i, ns)
-        p = lax.rem(z + r, n) * ns + lax.rem(s + side, ns)
-        pltpu.make_async_copy(mine[0], hold.at[i], sem.at[i]).wait()
+        p = lax.rem(z + i // ns, n) * ns + lax.rem(s + lax.rem(i, ns), ns)
+        pltpu.make_async_copy(here[0], hold.at[i], sem.at[i]).wait()
         slot = 0
         for w in ws:
             for c in range(w.shape[1]):
@@ -292,46 +271,44 @@
         return carry
 
     lax.fori_loop(0, n * ns, step, 0)
-    for g in range(acc.shape[0] - 1):
-        if split:
-            per = out.shape[2] // block
-            to = lax.rem(g // per - meta[2] + out.shape[0], out.shape[0])
-            out[to, :, (g % per) * block : (g % per + 1) * block] = acc[g].astype(BF)
-        else:
-            out[:, g * block : (g + 1) * block] = acc[g].astype(BF)
-
-
-def decode(tab_j, tab_m, meta, mine, theirs, weights, grid_count, chunk, chunks, base, nf, n, ns):
-    chans, block = mine[0].shape[1], mine[0].shape[2]
+    per = (acc.shape[0] - 1) // nf
+    for r, out in enumerate(outs):
+        first = lax.rem(meta[2] + r, nf) * per
+        for g in range(per):
+            out[:, g * block : (g + 1) * block] = acc[first + g].astype(BF)
+
+
+def decode(tab_j, tab_m, meta, here, there, weights, grid_count, chunk, chunks, base, nf, n, ns):
+    chans, block = here[0].shape[1], here[0].shape[2]
+    meshes = [*here, *there]
     rows = grid_count * block
-    split = nf is not None
-    if split:
-        shape = (nf, chans, rows // nf)
-        out_spec = pl.BlockSpec(shape, lambda i, j, m, t: (0, 0, 0))
+    if nf > 1:
+        shape = (chans, rows // nf)
+        out_spec = pl.BlockSpec(shape, lambda i, j, m, t: (0, 0))
     else:
         shape = (chans * chunks, rows)
         out_spec = pl.BlockSpec((chans, rows), lambda i, j, m, t: (chunk, 0))
     alias = base is not None
-    count = 2 * len(mine)
+    whole = lambda a: pl.BlockSpec(a.shape, lambda i, j, m, t: (0,) * a.ndim)
     return pl.pallas_call(
         functools.partial(
-            decode_kernel, n=n, ns=ns, weights=len(weights), alias=alias, split=split
+            decode_kernel, n=n, ns=ns, weights=len(weights), alias=alias, nf=nf
         ),
         grid_spec=pltpu.PrefetchScalarGridSpec(
             num_scalar_prefetch=3,
             grid=(1,),
-            in_specs=[pl.BlockSpec(memory_space=pl.ANY)] * count
-            + [pl.BlockSpec(w.shape, lambda i, j, m, t: (0, 0, 0, 0)) for w in weights]
+            in_specs=[pl.BlockSpec(memory_space=pl.ANY)] * len(meshes)
+            + [whole(w) for w in weights]
             + ([pl.BlockSpec(memory_space=pl.ANY)] if alias else []),
-            out_specs=out_spec,
+            out_specs=[out_spec] * nf,
             scratch_shapes=[
                 pltpu.VMEM((n * ns, MBLK, chans, block), BF),
                 pltpu.VMEM((grid_count + 1, chans, block), F32),
                 pltpu.SemaphoreType.DMA((n * ns,)),
             ],
         ),
-        out_shape=jax.ShapeDtypeStruct(shape, BF),
-        input_output_aliases={3 + count + len(weights): 0} if alias else {},
+        out_shape=[jax.ShapeDtypeStruct(shape, BF)] * nf,
+        input_output_aliases={3 + 2 * n + len(weights): 0} if alias else {},
         compiler_params=params(),
         cost_estimate=pl.CostEstimate(
             flops=2 * n * ns * 16 * chans * block * block * 4,
@@ -339,14 +316,7 @@
             transcendentals=0,
         ),
         name="decode",
-    )(tab_j, tab_m, meta, *mine, *theirs, *weights, *([base] if alias else []))
-
-
-def total(*terms):
-    out = terms[0].astype(F32)
-    for term in terms[1:]:
-        out = out + term.astype(F32)
-    return out.astype(BF)
+    )(tab_j, tab_m, meta, *meshes, *weights, *([base] if alias else []))
 
 
 def swap_sub(a):
@@ -354,28 +324,58 @@
     return lax.ppermute(a, "sub", [(i, (i + 1) % ns) for i in range(ns)])
 
 
-def reduce_line(own, other):
+def add_kernel(*refs, terms, deps):
+    ins, outs = refs[: sum(terms)], refs[sum(terms) + deps :]
+    for out, count in zip(outs, terms):
+        value = ins[0][0].astype(F32) + ins[1][0].astype(F32)
+        for ref in ins[2:count]:
+            value = value + ref[...].astype(F32)
+        out[...] = value.astype(BF)
+        ins = ins[count:]
+
+
+def add(own, other, groups, deps):
+    shape = own.shape[1:]
+    parts = 3 if shape[0] % 3 == 0 else 1
+    piece = (shape[0] // parts,) + shape[1:]
+    spec = pl.BlockSpec(piece, lambda i: (i, 0, 0))
+    arrays, specs = [], []
+    for place, terms in groups:
+        pick = pl.BlockSpec((1,) + piece, lambda i, place=place: (place, i, 0, 0))
+        arrays += [own, other, *terms]
+        specs += [pick, pick] + [spec] * len(terms)
+    return pl.pallas_call(
+        functools.partial(
+            add_kernel, terms=[2 + len(terms) for _, terms in groups], deps=len(deps)
+        ),
+        grid=(parts,),
+        in_specs=specs + [pl.BlockSpec(memory_space=pl.ANY)] * len(deps),
+        out_specs=[spec] * len(groups),
+        out_shape=[jax.ShapeDtypeStruct(shape, BF)] * len(groups),
+        compiler_params=params(),
+        name="add",
+    )(*arrays, *deps)
+
+
+def reduce_step(t, own, other, up, down, deps):
     n = own.shape[0]
-    up = down = None
-    for t in range(1, n):
-        ups = [own[n - t], other[n - t]] + ([up] if up is not None else [])
-        downs = [own[t], other[t]] + ([down] if down is not None else [])
-        up = lax.ppermute(total(*ups), "lat", [(i, i + 1) for i in range(n - 1) if i <= t - 1])
-        down = lax.ppermute(
-            total(*downs), "lat", [(i, i - 1) for i in range(1, n) if i >= n - t]
-        )
-    return total(own[0], other[0], up, down)
-
-
-def spread_line(block):
+    first = up is None
+    up, down = add(
+        own, other, [(n - t, [] if first else [up]), (t, [] if first else [down])], deps
+    )
+    return (
+        up,
+        lax.ppermute(up, "lat", [(i, i + 1) for i in range(n - 1) if i <= t - 1]),
+        lax.ppermute(down, "lat", [(i, i - 1) for i in range(1, n) if i >= n - t]),
+    )
+
+
+def spread_step(t, up, down):
     n = lax.axis_size("lat")
-    ups, downs = [block], [block]
-    for t in range(1, n):
-        ups.append(
-            lax.ppermute(ups[-1], "lat", [(i, i + 1) for i in range(n - 1) if i >= t - 1])
-        )
-        downs.append(lax.ppermute(downs[-1], "lat", [(i, i - 1) for i in range(1, n) if i <= n - t]))
-    return ups + downs[1:]
+    return (
+        lax.ppermute(up, "lat", [(i, i + 1) for i in range(n - 1) if i >= t - 1]),
+        lax.ppermute(down, "lat", [(i, i - 1) for i in range(1, n) if i <= n - t]),
+    )
 
 
 def add_all(value, axes):
@@ -431,8 +431,14 @@
     hit = (rank[:, None, :] == send_ranks[None, :, None]) & (marks[:, None, :] > 0)
     src = jnp.sum(jnp.where(hit, jnp.arange(slots, dtype=jnp.int32), 0), axis=-1)
     a2a = lambda v: lax.all_to_all(v, ("lat", "sub"), 0, 0, tiled=True)
+    meta_f = jnp.stack([f]).astype(jnp.int32)
+    *emb, normed, slope, inv, mid = forward(
+        meta_f, x, frozen_input_weight, adapter_down_weight, adapter_up_weight,
+        frozen_output_weight, nf, [],
+    )
     if shared:
         first, second = pack(src, values, 2)
+        second, _ = lax.optimization_barrier((second, mid))
         first, second = a2a(first), a2a(second)
         flip = [(0, 1), (1, 0)]
         over_x = lambda v: lax.ppermute(v, "fsdp", flip)
@@ -445,7 +451,10 @@
         weights = [a2a(pack(src, values, 1)[0])]
         slot_ranks = send_ranks
 
-    both = lax.all_gather(jnp.stack([cols, rows])[None], ("lat", "sub"), tiled=True)
+    pattern = jnp.stack([cols, rows])[None]
+    if shared:
+        pattern, _ = lax.optimization_barrier((pattern, first))
+    both = lax.all_gather(pattern, ("lat", "sub"), tiled=True)
     every = places_of(storage, both[:, 0])
     mine = (every // grid_count == me).astype(jnp.int32)
     mine_rank = ranks_in(mine)
@@ -456,49 +465,89 @@
     tab_get = jnp.where(found, local, 0)
     tab_put = jnp.where(found, local, grid_count)
 
-    meta_f = jnp.stack([f]).astype(jnp.int32)
-    emb, normed, slope, inv, mid = forward(
-        meta_f, x, frozen_input_weight, adapter_down_weight, adapter_up_weight,
-        frozen_output_weight, nf,
-    )
     shift = lambda v, r: lax.ppermute(v, "fsdp", [(i, (i + r) % nf) for i in range(nf)])
     emb_pieces = [emb[r] if r == 0 else shift(emb[r], r) for r in range(nf)]
 
     meta_own = jnp.stack([z, s, f]).astype(jnp.int32)
     meta_sib = jnp.stack([z, (s + 1) % ns, f]).astype(jnp.int32)
-    chunks = 2
-
-    def mesh_of(pieces, chunk):
-        args = (pieces, chunk, chunks, weights, n, ns)
-        other = swap_sub(encode(tab_get, tab_m, meta_sib, *args))
-        own = encode(tab_get, tab_m, meta_own, *args)
-        return reduce_line(own, other)
-
-    def grid_of(mesh, chunk, base, split):
-        here = spread_line(mesh)
-        there = [swap_sub(a) for a in here]
-        return decode(
-            tab_put, tab_m, meta_own, here, there, weights, grid_count, chunk, chunks, base,
-            nf if split else None, n, ns,
-        )
-
-    cot_mesh = [mesh_of([cot], c) for c in range(chunks)]
-    emb_mesh = [mesh_of(emb_pieces, c) for c in range(chunks)]
-    grads, offs = [], []
-    for c in range(chunks):
-        grad = grid_of(cot_mesh[c], c, None, True)
-        for r in range(nf):
-            grads.append(grad[r] if r == 0 else shift(grad[r], r))
-            offs.append(((f - r + nf) % nf) * chans + c * (chans // chunks))
-    decoded = None
-    for c in range(chunks):
-        decoded = grid_of(emb_mesh[c], c, decoded, False)
-
-    up, down = backward(
-        jnp.stack(offs).astype(jnp.int32), grads, normed, slope, inv, mid, x,
-        frozen_output_weight, adapter_up_weight,
-    )
-    sums = add_all(jnp.concatenate([up, down], axis=1), ("sub", "fsdp", "lat"))
+    chunks = 1
+
+    lag = n
+    sources = [([cot], c) for c in range(chunks)] + [(emb_pieces, c) for c in range(chunks)]
+    state = [{} for _ in sources]
+    grads, offs, decoded = [], [], None
+    token = mid
+    last = lag * (len(sources) - 1) + 2 * (n - 1) + 3
+    for now in range(-1, last):
+        made, put = [], []
+
+        def keep(where, key, value):
+            made.append(value)
+            put.append((where, key))
+
+        for k, (pieces, chunk) in enumerate(sources):
+            st, at = state[k], now - lag * k
+            if at == -1:
+                args = (pieces, chunk, chunks, weights, [token], n, ns)
+                keep(st, "other", swap_sub(encode(tab_get, tab_m, meta_sib, *args)))
+                keep(st, "own", encode(tab_get, tab_m, meta_own, *args))
+            elif 0 <= at < n - 1:
+                behind = [state[k - 1][key, at + 1] for key in ("up", "down")] if k else []
+                sent, up, down = reduce_step(
+                    at + 1, st["own"], st["other"], st.get("up"), st.get("down"), behind
+                )
+                if at == n - 2:
+                    token = sent
+                keep(st, "up", up)
+                keep(st, "down", down)
+            elif n - 1 <= at < 2 * n - 2:
+                t = at - n + 2
+                if t == 1:
+                    behind = [state[k - 1]["grad", 0]] if k else []
+                    (mesh,) = add(
+                        st["own"], st["other"], [(0, [st["up"], st["down"]])], behind
+                    )
+                    st["here"], st["there"] = {0: mesh}, {0: swap_sub(mesh)}
+                    st["up"], st["down"] = mesh, mesh
+                if k >= chunks and t > 1:
+                    if t == n - 1:
+                        sums = backward(
+                            jnp.stack(offs).astype(jnp.int32), grads, normed, slope, inv, mid, x,
+                            frozen_output_weight, adapter_up_weight,
+                        )
+                    done = list(sums) if t == n - 1 else grads
+                    st["up"], st["down"], *_ = lax.optimization_barrier(
+                        (st["up"], st["down"], *done)
+                    )
+                st["up"], st["down"] = spread_step(t, st["up"], st["down"])
+                st["up", t], st["down", t] = st["up"], st["down"]
+                for r in range(1, n):
+                    if max(r, n - r) == t:
+                        st["here"][r] = jnp.where(z + r < n, st["down", r], st["up", n - r])
+                        st["there"][r] = swap_sub(st["here"][r])
+            elif at == 2 * n - 2:
+                grad = k < chunks
+                if not grad:
+                    sums = add_all(jnp.concatenate(sums, axis=1), ("sub", "fsdp", "lat"))
+                    st["here"][0], _ = lax.optimization_barrier((st["here"][0], sums))
+                out = decode(
+                    tab_put, tab_m, meta_own, [st["here"][r] for r in range(n)],
+                    [st["there"][r] for r in range(n)], weights, grid_count,
+                    chunk, chunks, None if grad else decoded, nf if grad else 1, n, ns,
+                )
+                if grad:
+                    for r in range(nf):
+                        st["grad", r] = out[r]
+                else:
+                    decoded = out[0]
+                if grad:
+                    for r in range(nf):
+                        piece = st["grad", r]
+                        grads.append(piece if r == 0 else shift(piece, r))
+                        offs.append(((f - r + nf) % nf) * chans + chunk * (chans // chunks))
+        for spot, value in zip(put, made):
+            spot[0][spot[1]] = value
+
     up_gradient, grad_down = sums[:, :width], sums[:, width:].T
     return (decoded.reshape(1, 1, chans, grid_rows), grad_down, up_gradient)
 

time: 444 us -> 358 us (0.81)
  starting transfers between devices: 127 us -> 93.9 us
  Pallas kernels: 69.3 us -> 48.5 us
  other arithmetic: 26 us -> 5.77 us
  blocking collectives: 31.3 us -> 12.9 us
  waiting for transfers between devices: 157 us -> 171 us
  local copies, waits for them, and re-layouts: 29.5 us -> 22.2 us
    ppermute x48 -> x24, starting transfers between devices: 98.6 us -> 69.8 us  [the longest x6 43.6 us: reduce_step(): lax.ppermute(up, 'lat', [(i, i + 1) for i in range(n - 1) if i <= t - 1])]
    ppermute x3, waiting for transfers between devices: 43.3 us -> 21.1 us  [body(): over_x = lambda v: lax.ppermute(v, 'fsdp', flip)]
    convert_element_type x20 -> x0, other arithmetic: 21.7 us -> none  [total(): return out.astype(BF)]
    all_to_all x1 -> x0, blocking collectives: 17.9 us -> none  [body(): a2a = lambda v: lax.all_to_all(v, ('lat', 'sub'), 0, 0, tiled=True)]
    pallas_call x8 -> x4, Pallas kernels: 27.6 us -> 13.9 us  [encode(): pl.pallas_call(functools.partial(encode_kernel, panels=panels, weights=le...]
    ppermute x4, waiting for transfers between devices: 0.01 us -> 13.4 us  [add_all(): lax.ppermute(value, axis, [(i, i ^ step) for i in range(size)])]
    ppermute x48 -> x24, waiting for transfers between devices: 109 us -> 122 us  [the longest x6 58.1 us: reduce_step(): lax.ppermute(up, 'lat', [(i, i + 1) for i in range(n - 1) if i <= t - 1])]
    pallas_call x4 -> x2, Pallas kernels: 24.5 us -> 12.4 us  [decode(): pl.pallas_call(functools.partial(decode_kernel, n=n, ns=ns, weights=len(w...]
  transfers between devices with their start and end apart: 94 -> 48, of which waited for: 26 -> 24; matrix products, arithmetic and copies ran while one was open for 7% -> 2% of each run, Pallas kernels for 15% -> 9%
where the time goes in v2:
time: 358 us; the launch traced here: 356 us
  waiting for transfers between devices  171 us (48%)
  starting transfers between devices  93.9 us (26%)
  Pallas kernels  48.5 us (14%)
  local copies, waits for them, and re-layouts  22.2 us (6%)
  blocking collectives  12.9 us (4%)
  other arithmetic  5.77 us (2%)
    ppermute x6, waiting for transfers between devices, reduce_step(): lax.ppermute(up, 'lat', [(i, i + 1) for i in range(n - 1) if i <= t - 1])  58.1 us
    ppermute x6, starting transfers between devices, reduce_step(): lax.ppermute(up, 'lat', [(i, i + 1) for i in range(n - 1) if i <= t - 1])  43.6 us
    ppermute x6, waiting for transfers between devices, spread_step(): lax.ppermute(down, 'lat', [(i, i - 1) for i in range(1, n) if i <= n - t])  37.7 us
    ppermute x3, waiting for transfers between devices, body(): over_x = lambda v: lax.ppermute(v, 'fsdp', flip)  21.1 us
    unnamed x128, local copies, waits for them, and re-layouts  20.9 us
    ppermute x6, waiting for transfers between devices, reduce_step(): lax.ppermute(down, 'lat', [(i, i - 1) for i in range(1, n) if i >= n - t])  20.4 us
    pallas_call x4, Pallas kernels, encode(): pl.pallas_call(functools.partial(encode_kernel, panels=panels, weights=le...  13.9 us
    ppermute x4, waiting for transfers between devices, add_all(): lax.ppermute(value, axis, [(i, i ^ step) for i in range(size)])  13.4 us
  transfers between devices with their start and end apart: 48, of which 24 were waited for; matrix products, arithmetic and copies ran while one was open for 2% of the time, Pallas kernels for 9%

profile of v2, /device:TPU:0, one launch (start us, length us, event | category | flops | bytes accessed | tf_op | source)
XLA Modules:
  0.0 356.2 jit_solution(16604282178804052263)
XLA Ops:
  5.6 6.3 %all-to-all-start = ((bf16[8,2,128,128]{3,2,1,0:T(8,128)(2,1)}), bf16[8,2,128,128]{3,2,1,0:T(8,128)(2,1)S(1)}, u32[]{:S(2)}, u32[]{:S(2)}) async-start(bf16[8,2,128,128]{3,2,1,0:T(8,128)(2,1)} %get-tuple-element.34), calls=%async_computation | async-start | bytes 1048576 | tf_op jit(solution)/shard_map/all_to_all | solution.py:433
  12.2 6.7 %forward.1 = (bf16[256,2048]{1,0:T(8,128)(2,1)S(1)}, bf16[256,2048]{1,0:T(8,128)(2,1)S(1)}, f32[512,2048]{1,0:T(8,128)S(1)}, f32[512,2048]{1,0:T(8,128)S(1)}, f3...) custom-call(s32[1]{0:T(128)} %bitcast.9.meta, bf16[227,2048]{1,0:T(8,128)(2,1)S(1)} %bitcast.22, ...), custom_call_target="tpu_custom_call" | custom-call | flops 1549795328 | bytes 12582912 | tf_op jit(solution)/shard_map/forward/pallas_call | solution.py:90
  34.1 12.9 %all_gather.3 = s32[8,2,96]{2,1,0:T(2,128)S(1)} all-gather(s32[1,2,96]{2,1,0:T(2,128)S(1)} %add_bitcast_fusion), channel_id=1, replica_groups=mesh['parts'=2,'lat'=4,'fsdp'=2,'sub'=2] {'lat','sub'}, dimensions={0}, use_global_device_ids=true | all-gather | bytes 6912 | tf_op jit(solution)/shard_map/all_gather | solution.py:457
  51.6 11.8 %collective-permute-done.2.refs_4_.refs_5_.refs_11_ = bf16[8,2,128,128]{3,2,1,0:T(8,128)(2,1)S(1)} collective-permute-done((bf16[8,2,128,128]{3,2,1,0:T(8,128)(2,1)S(1)}, bf16[8,2,128,128]{3,2,1,0:T(8,128)(2,1)S(1)}, u32[]{:S(2)}, u32[]{:S(2)}) %collective-permute-start.2) | collective-permute-done | bytes 524320 | tf_op jit(solution)/shard_map/ppermute | solution.py:444
  64.4 9.3 %collective-permute-done.5.refs_7_.refs_8_.refs_14_ = bf16[8,2,128,128]{3,2,1,0:T(8,128)(2,1)S(1)} collective-permute-done((bf16[8,2,128,128]{3,2,1,0:T(8,128)(2,1)S(1)}, bf16[8,2,128,128]{3,2,1,0:T(8,128)(2,1)S(1)}, u32[]{:S(2)}, u32[]{:S(2)}) %collective-permute-start.5) | collective-permute-done | bytes 524320 | tf_op jit(solution)/shard_map/ppermute | solution.py:444
  92.8 14.7 %collective-permute-done.8.refs_2_ = bf16[12,256,128]{2,1,0:T(8,128)(2,1)S(1)} collective-permute-done((bf16[12,256,128]{2,1,0:T(8,128)(2,1)S(1)}, bf16[12,256,128]{2,1,0:T(8,128)(2,1)S(1)}, u32[]{:S(2)}, u32[]{:S(2)}) %collective-permute-start.8) | collective-permute-done | bytes 786464 | tf_op jit(solution)/shard_map/ppermute | solution.py:368
  113.3 15.5 %collective-permute-done.10.refs_2_ = bf16[12,256,128]{2,1,0:T(8,128)(2,1)S(1)} collective-permute-done((bf16[12,256,128]{2,1,0:T(8,128)(2,1)S(1)}, bf16[12,256,128]{2,1,0:T(8,128)(2,1)S(1)}, u32[]{:S(2)}, u32[]{:S(2)}) %collective-permute-start.10) | collective-permute-done | bytes 786464 | tf_op jit(solution)/shard_map/ppermute | solution.py:368
  134.7 9.7 %collective-permute-start.13 = (bf16[12,256,128]{2,1,0:T(8,128)(2,1)S(1)}, bf16[12,256,128]{2,1,0:T(8,128)(2,1)S(1)}, u32[]{:S(2)}, u32[]{:S(2)}) collective-permute-start(bf16[12,256,128]{2,1,0:T(8,128)(2,1)S(1)} %get-tuple-element.45.refs_10_), channel_id=1, source_target_pairs={{0,4},{4,8},{8,12},{1,5},{5,9},{9,13},{2,6},{6,10},{10,14},{3,7},{... | collective-permute-start | bytes 2359304 | tf_op jit(solution)/shard_map/ppermute | solution.py:368
  144.5 16.2 %collective-permute-done.14.refs_3_ = bf16[12,256,128]{2,1,0:T(8,128)(2,1)S(1)} collective-permute-done((bf16[12,256,128]{2,1,0:T(8,128)(2,1)S(1)}, bf16[12,256,128]{2,1,0:T(8,128)(2,1)S(1)}, u32[]{:S(2)}, u32[]{:S(2)}) %collective-permute-start.14) | collective-permute-done | bytes 786464 | tf_op jit(solution)/shard_map/ppermute | solution.py:369
  163.6 5.1 %collective-permute-start.15 = (bf16[12,256,128]{2,1,0:T(8,128)(2,1)S(1)}, bf16[12,256,128]{2,1,0:T(8,128)(2,1)S(1)}, u32[]{:S(2)}, u32[]{:S(2)}) collective-permute-start(bf16[12,256,128]{2,1,0:T(8,128)(2,1)S(1)} %add.168.refs_0_), channel_id=1, source_target_pairs={{0,4},{4,8},{8,12},{1,5},{5,9},{9,13},{2,6},{6,10},{10,14},{3,7},{... | collective-permute-start | bytes 2359304 | tf_op jit(solution)/shard_map/ppermute | solution.py:376
  168.6 15.4 %collective-permute-done.16.refs_5_ = bf16[12,256,128]{2,1,0:T(8,128)(2,1)S(1)} collective-permute-done((bf16[12,256,128]{2,1,0:T(8,128)(2,1)S(1)}, bf16[12,256,128]{2,1,0:T(8,128)(2,1)S(1)}, u32[]{:S(2)}, u32[]{:S(2)}) %collective-permute-start.16) | collective-permute-done | bytes 786464 | tf_op jit(solution)/shard_map/ppermute | solution.py:377
  192.7 9.2 %collective-permute-start.17 = (bf16[12,256,128]{2,1,0:T(8,128)(2,1)}, bf16[12,256,128]{2,1,0:T(8,128)(2,1)}, u32[]{:S(2)}, u32[]{:S(2)}) collective-permute-start(bf16[12,256,128]{2,1,0:T(8,128)(2,1)} %get-tuple-element.47), channel_id=1, source_target_pairs={{0,4},{1,5},{2,6},{3,7},{16,20},{17,21},{18,22},{19,23}} | collective-permute-start | bytes 2359304 | tf_op jit(solution)/shard_map/ppermute | solution.py:368
  207.4 9.1 %collective-permute-done.17.refs_2_ = bf16[12,256,128]{2,1,0:T(8,128)(2,1)} collective-permute-done((bf16[12,256,128]{2,1,0:T(8,128)(2,1)}, bf16[12,256,128]{2,1,0:T(8,128)(2,1)}, u32[]{:S(2)}, u32[]{:S(2)}) %collective-permute-start.17) | collective-permute-done | bytes 786464 | tf_op jit(solution)/shard_map/ppermute | solution.py:368
  221.0 4.6 %collective-permute-start.21 = (bf16[12,256,128]{2,1,0:T(8,128)(2,1)S(1)}, bf16[12,256,128]{2,1,0:T(8,128)(2,1)S(1)}, u32[]{:S(2)}, u32[]{:S(2)}) collective-permute-start(bf16[12,256,128]{2,1,0:T(8,128)(2,1)S(1)} %get-tuple-element.49), channel_id=1, source_target_pairs={{0,4},{4,8},{1,5},{5,9},{2,6},{6,10},{3,7},{7,11},{16,20},{20,24},... | collective-permute-start | bytes 2359304 | tf_op jit(solution)/shard_map/ppermute | solution.py:368
  229.6 10.2 %collective-permute-done.21.refs_2_ = bf16[12,256,128]{2,1,0:T(8,128)(2,1)S(1)} collective-permute-done((bf16[12,256,128]{2,1,0:T(8,128)(2,1)S(1)}, bf16[12,256,128]{2,1,0:T(8,128)(2,1)S(1)}, u32[]{:S(2)}, u32[]{:S(2)}) %collective-permute-start.21) | collective-permute-done | bytes 786464 | tf_op jit(solution)/shard_map/ppermute | solution.py:368
  240.4 12.1 %collective-permute-start.25 = (bf16[12,256,128]{2,1,0:T(8,128)(2,1)S(1)}, bf16[12,256,128]{2,1,0:T(8,128)(2,1)S(1)}, u32[]{:S(2)}, u32[]{:S(2)}) collective-permute-start(bf16[12,256,128]{2,1,0:T(8,128)(2,1)S(1)} %get-tuple-element.51), channel_id=1, source_target_pairs={{0,4},{4,8},{8,12},{1,5},{5,9},{9,13},{2,6},{6,10},{10,14},{3,7},{... | collective-permute-start | bytes 2359304 | tf_op jit(solution)/shard_map/ppermute | solution.py:368
  254.1 5.5 %decode.2 = (bf16[256,2048]{1,0:T(8,128)(2,1)S(1)}, bf16[256,2048]{1,0:T(8,128)(2,1)S(1)}) custom-call(s32[8,16]{1,0:T(8,128)S(1)} %get-tuple-element.72.tab_j, s32[8,16]{1,0:T(8,128)S(1)} %get-tuple-element.73.tab_m, s32[3]{0:T(128)S(1)} %add_add_fusion.meta, bf16[12,256,128]{2,1,0:T(8,128)(2,1)S(1)} %copy-done.52, ...), custom_call_target="tpu_custom_call" | custom-call | flops 4294967296 | bytes 12582912 | tf_op jit(solution)/shard_map/decode/pallas_call | solution.py:293
  261.2 7.4 %collective-permute-done.25.refs_2_ = bf16[12,256,128]{2,1,0:T(8,128)(2,1)S(1)} collective-permute-done((bf16[12,256,128]{2,1,0:T(8,128)(2,1)S(1)}, bf16[12,256,128]{2,1,0:T(8,128)(2,1)S(1)}, u32[]{:S(2)}, u32[]{:S(2)}) %collective-permute-start.25) | collective-permute-done | bytes 786464 | tf_op jit(solution)/shard_map/ppermute | solution.py:368
  276.7 7.0 %collective-permute-done.31.refs_1_ = bf16[256,2048]{1,0:T(8,128)(2,1)S(1)} collective-permute-done((bf16[256,2048]{1,0:T(8,128)(2,1)S(1)}, bf16[256,2048]{1,0:T(8,128)(2,1)S(1)}, u32[]{:S(2)}, u32[]{:S(2)}) %collective-permute-start.31) | collective-permute-done | bytes 1048608 | tf_op jit(solution)/shard_map/ppermute | solution.py:468
  284.6 5.9 %collective-permute-done.37 = bf16[12,256,128]{2,1,0:T(8,128)(2,1)S(1)} collective-permute-done((bf16[12,256,128]{2,1,0:T(8,128)(2,1)S(1)}, bf16[12,256,128]{2,1,0:T(8,128)(2,1)S(1)}, u32[]{:S(2)}, u32[]{:S(2)}) %collective-permute-start.37) | collective-permute-done | bytes 786464 | tf_op jit(solution)/shard_map/ppermute | solution.py:376
  305.9 6.1 %backward.1 = (f32[16,512]{1,0:T(8,128)S(1)}, f32[16,227]{1,0:T(8,128)S(1)}) custom-call(s32[2]{0:T(128)S(1)} %pad_add_fusion.1.offs, bf16[256,2048]{1,0:T(8,128)(2,1)S(1)} %copy-done.39, bf16[256,2048]{1,0:T(8,128)(2,1)S(1)} %copy-done.46, f32[512,2048]{1,0:T(8,128)S(1)} %copy-done.35, f32[512,2048]{1,0:T(8,128)S(1)} %copy-done.37, ...), custom_call_target="tpu_custom_call" | custom-call | flops 1073741824 | bytes 10485760 | tf_op jit(solution)/shard_map/backward/pallas_call | solution.py:161
  316.8 15.2 %collective-permute-done.41 = bf16[12,256,128]{2,1,0:T(8,128)(2,1)S(1)} collective-permute-done((bf16[12,256,128]{2,1,0:T(8,128)(2,1)S(1)}, bf16[12,256,128]{2,1,0:T(8,128)(2,1)S(1)}, u32[]{:S(2)}, u32[]{:S(2)}) %collective-permute-start.41) | collective-permute-done | bytes 786464 | tf_op jit(solution)/shard_map/ppermute | solution.py:377
  343.0 4.9 %collective-permute-done.35 = f32[16,739]{1,0:T(8,128)S(1)} collective-permute-done((f32[16,739]{1,0:T(8,128)S(1)}, f32[16,739]{1,0:T(8,128)S(1)}, u32[]{:S(2)}, u32[]{:S(2)}) %collective-permute-start.35) | collective-permute-done | bytes 47328 | tf_op jit(solution)/shard_map/ppermute | solution.py:385
  349.2 6.8 %decode.3 = bf16[256,4096]{1,0:T(8,128)(2,1)} custom-call(s32[8,16]{1,0:T(8,128)S(1)} %get-tuple-element.72.tab_j, s32[8,16]{1,0:T(8,128)S(1)} %get-tuple-element.73.tab_m, s32[3]{0:T(128)S(1)} %add_add_fusion.meta, bf16[12,256,128]{2,1,0:T(8,128)(2,1)S(1)} %copy-done.50, bf16[12,256,128]{2,1,0:T(8,128)(2,1)S(1)} %broadcast_select_fusion.4.refs_1_, ...), custom_call_target="tpu_custom_call" | custom-call | flops 4294967296 | bytes 12582912 | tf_op jit(solution)/shard_map/decode/pallas_call | solution.py:293
  (254 shorter events, 126.6 us)
Async XLA Ops:
  5.6 21.7 %all-to-all-start = ((bf16[8,2,128,128]{3,2,1,0:T(8,128)(2,1)}), bf16[8,2,128,128]{3,2,1,0:T(8,128)(2,1)S(1)}, u32[]{:S(2)}, u32[]{:S(2)}) async-start(bf16[8,2,128,128]{3,2,1,0:T(8,128)(2,1)} %get-tuple-element.34), calls=%async_computation | async-start | bytes 1048576 | tf_op jit(solution)/shard_map/all_to_all | solution.py:433
  32.7 31.7 %collective-permute-start.1 = (bf16[8,2,128,128]{3,2,1,0:T(8,128)(2,1)S(1)}, bf16[8,2,128,128]{3,2,1,0:T(8,128)(2,1)S(1)}, u32[]{:S(2)}, u32[]{:S(2)}) collective-permute-start(bf16[8,2,128,128]{3,2,1,0:T(8,128)(2,1)S(1)} %all-to-all-done.refs_1_.refs_2_.refs_8_), channel_id=1, source_target_pairs={{0,2},{2,0},{1,3},{3,1},{4,6},{6,4},{5,7},{7,5},{8,10},{10,8},{9,1... | collective-permute-start | bytes 1572872 | tf_op jit(solution)/shard_map/ppermute | solution.py:444
  51.0 22.7 %collective-permute-start.5 = (bf16[8,2,128,128]{3,2,1,0:T(8,128)(2,1)S(1)}, bf16[8,2,128,128]{3,2,1,0:T(8,128)(2,1)S(1)}, u32[]{:S(2)}, u32[]{:S(2)}) collective-permute-start(bf16[8,2,128,128]{3,2,1,0:T(8,128)(2,1)S(1)} %collective-permute-done.3.refs_5_.refs_6_.refs_12_), channel_id=1, source_target_pairs={{0,2},{2,0},{1,3},{3,1},{4,6},{6,4},{5,7},{7,5},{8,10},{10,8},{9,1... | collective-permute-start | bytes 1572872 | tf_op jit(solution)/shard_map/ppermute | solution.py:444
  86.9 20.7 %collective-permute-start.8 = (bf16[12,256,128]{2,1,0:T(8,128)(2,1)S(1)}, bf16[12,256,128]{2,1,0:T(8,128)(2,1)S(1)}, u32[]{:S(2)}, u32[]{:S(2)}) collective-permute-start(bf16[12,256,128]{2,1,0:T(8,128)(2,1)S(1)} %get-tuple-element.41), channel_id=1, source_target_pairs={{0,4},{1,5},{2,6},{3,7},{16,20},{17,21},{18,22},{19,23}} | collective-permute-start | bytes 2359304 | tf_op jit(solution)/shard_map/ppermute | solution.py:368
  91.2 38.2 %collective-permute-start = (bf16[256,2048]{1,0:T(8,128)(2,1)S(1)}, bf16[256,2048]{1,0:T(8,128)(2,1)S(1)}, u32[]{:S(2)}, u32[]{:S(2)}) collective-permute-start(bf16[256,2048]{1,0:T(8,128)(2,1)S(1)} %copy-done.57), channel_id=1, source_target_pairs={{0,2},{2,0},{1,3},{3,1},{4,6},{6,4},{5,7},{7,5},{8,10},{10,8},{9,1... | collective-permute-start | bytes 3145736 | tf_op jit(solution)/shard_map/ppermute | solution.py:468
  108.2 20.6 %collective-permute-start.10 = (bf16[12,256,128]{2,1,0:T(8,128)(2,1)S(1)}, bf16[12,256,128]{2,1,0:T(8,128)(2,1)S(1)}, u32[]{:S(2)}, u32[]{:S(2)}) collective-permute-start(bf16[12,256,128]{2,1,0:T(8,128)(2,1)S(1)} %get-tuple-element.43), channel_id=1, source_target_pairs={{0,4},{4,8},{1,5},{5,9},{2,6},{6,10},{3,7},{7,11},{16,20},{20,24},... | collective-permute-start | bytes 2359304 | tf_op jit(solution)/shard_map/ppermute | solution.py:368
  133.0 57.5 %collective-permute-start.12 = (bf16[4,12,256,128]{3,2,1,0:T(8,128)(2,1)S(1)}, bf16[4,12,256,128]{3,2,1,0:T(8,128)(2,1)S(1)}, u32[]{:S(2)}, u32[]{:S(2)}) collective-permute-start(bf16[4,12,256,128]{3,2,1,0:T(8,128)(2,1)S(1)} %encode.7), channel_id=1, source_target_pairs={{0,1},{1,0},{2,3},{3,2},{4,5},{5,4},{6,7},{7,6},{8,9},{9,8},{10,11... | collective-permute-start | bytes 9437192 | tf_op jit(solution)/shard_map/ppermute | solution.py:324
  133.2 27.5 %collective-permute-start.14 = (bf16[12,256,128]{2,1,0:T(8,128)(2,1)S(1)}, bf16[12,256,128]{2,1,0:T(8,128)(2,1)S(1)}, u32[]{:S(2)}, u32[]{:S(2)}) collective-permute-start(bf16[12,256,128]{2,1,0:T(8,128)(2,1)S(1)} %get-tuple-element.46), channel_id=1, source_target_pairs={{4,0},{8,4},{12,8},{5,1},{9,5},{13,9},{6,2},{10,6},{14,10},{7,3},{... | collective-permute-start | bytes 2359304 | tf_op jit(solution)/shard_map/ppermute | solution.py:369
  134.7 27.1 %collective-permute-start.13 = (bf16[12,256,128]{2,1,0:T(8,128)(2,1)S(1)}, bf16[12,256,128]{2,1,0:T(8,128)(2,1)S(1)}, u32[]{:S(2)}, u32[]{:S(2)}) collective-permute-start(bf16[12,256,128]{2,1,0:T(8,128)(2,1)S(1)} %get-tuple-element.45.refs_10_), channel_id=1, source_target_pairs={{0,4},{4,8},{8,12},{1,5},{5,9},{9,13},{2,6},{6,10},{10,14},{3,7},{... | collective-permute-start | bytes 2359304 | tf_op jit(solution)/shard_map/ppermute | solution.py:368
  162.3 21.8 %collective-permute-start.16 = (bf16[12,256,128]{2,1,0:T(8,128)(2,1)S(1)}, bf16[12,256,128]{2,1,0:T(8,128)(2,1)S(1)}, u32[]{:S(2)}, u32[]{:S(2)}) collective-permute-start(bf16[12,256,128]{2,1,0:T(8,128)(2,1)S(1)} %add.168.refs_0_), channel_id=1, source_target_pairs={{4,0},{8,4},{12,8},{5,1},{9,5},{13,9},{6,2},{10,6},{14,10},{7,3},{... | collective-permute-start | bytes 2359304 | tf_op jit(solution)/shard_map/ppermute | solution.py:377
  163.6 21.8 %collective-permute-start.15 = (bf16[12,256,128]{2,1,0:T(8,128)(2,1)S(1)}, bf16[12,256,128]{2,1,0:T(8,128)(2,1)S(1)}, u32[]{:S(2)}, u32[]{:S(2)}) collective-permute-start(bf16[12,256,128]{2,1,0:T(8,128)(2,1)S(1)} %add.168.refs_0_), channel_id=1, source_target_pairs={{0,4},{4,8},{8,12},{1,5},{5,9},{9,13},{2,6},{6,10},{10,14},{3,7},{... | collective-permute-start | bytes 2359304 | tf_op jit(solution)/shard_map/ppermute | solution.py:376
  184.0 20.5 %collective-permute-start.20 = (bf16[12,256,128]{2,1,0:T(8,128)(2,1)S(1)}, bf16[12,256,128]{2,1,0:T(8,128)(2,1)}, u32[]{:S(2)}, u32[]{:S(2)}) collective-permute-start(bf16[12,256,128]{2,1,0:T(8,128)(2,1)S(1)} %collective-permute-done.16.refs_5_), channel_id=1, source_target_pairs={{4,0},{8,4},{5,1},{9,5},{6,2},{10,6},{7,3},{11,7},{20,16},{24,20},... | collective-permute-start | bytes 2359304 | tf_op jit(solution)/shard_map/ppermute | solution.py:377
  185.4 20.5 %collective-permute-start.19 = (bf16[12,256,128]{2,1,0:T(8,128)(2,1)S(1)}, bf16[12,256,128]{2,1,0:T(8,128)(2,1)}, u32[]{:S(2)}, u32[]{:S(2)}) collective-permute-start(bf16[12,256,128]{2,1,0:T(8,128)(2,1)S(1)} %collective-permute-done.15.refs_4_), channel_id=1, source_target_pairs={{4,8},{8,12},{5,9},{9,13},{6,10},{10,14},{7,11},{11,15},{20,24},{2... | collective-permute-start | bytes 2359304 | tf_op jit(solution)/shard_map/ppermute | solution.py:376
  192.7 23.8 %collective-permute-start.17 = (bf16[12,256,128]{2,1,0:T(8,128)(2,1)}, bf16[12,256,128]{2,1,0:T(8,128)(2,1)}, u32[]{:S(2)}, u32[]{:S(2)}) collective-permute-start(bf16[12,256,128]{2,1,0:T(8,128)(2,1)} %get-tuple-element.47), channel_id=1, source_target_pairs={{0,4},{1,5},{2,6},{3,7},{16,20},{17,21},{18,22},{19,23}} | collective-permute-start | bytes 2359304 | tf_op jit(solution)/shard_map/ppermute | solution.py:368
  204.6 22.3 %collective-permute-start.24 = (bf16[12,256,128]{2,1,0:T(8,128)(2,1)}, bf16[12,256,128]{2,1,0:T(8,128)(2,1)}, u32[]{:S(2)}, u32[]{:S(2)}) collective-permute-start(bf16[12,256,128]{2,1,0:T(8,128)(2,1)} %collective-permute-done.20.refs_7_), channel_id=1, source_target_pairs={{4,0},{5,1},{6,2},{7,3},{20,16},{21,17},{22,18},{23,19}} | collective-permute-start | bytes 2359304 | tf_op jit(solution)/shard_map/ppermute | solution.py:377
  205.9 22.8 %collective-permute-start.23 = (bf16[12,256,128]{2,1,0:T(8,128)(2,1)}, bf16[12,256,128]{2,1,0:T(8,128)(2,1)}, u32[]{:S(2)}, u32[]{:S(2)}) collective-permute-start(bf16[12,256,128]{2,1,0:T(8,128)(2,1)} %collective-permute-done.19.refs_6_), channel_id=1, source_target_pairs={{8,12},{9,13},{10,14},{11,15},{24,28},{25,29},{26,30},{27,31}} | collective-permute-start | bytes 2359304 | tf_op jit(solution)/shard_map/ppermute | solution.py:376
  207.4 45.0 %collective-permute-start.27 = (bf16[12,256,128]{2,1,0:T(8,128)(2,1)}, bf16[12,256,128]{2,1,0:T(8,128)(2,1)S(1)}, u32[]{:S(2)}, u32[]{:S(2)}) collective-permute-start(bf16[12,256,128]{2,1,0:T(8,128)(2,1)} %copy-done.51), channel_id=1, source_target_pairs={{0,1},{1,0},{2,3},{3,2},{4,5},{5,4},{6,7},{7,6},{8,9},{9,8},{10,11... | collective-permute-start | bytes 2359304 | tf_op jit(solution)/shard_map/ppermute | solution.py:324
  226.8 27.1 %collective-permute-start.29 = (bf16[12,256,128]{2,1,0:T(8,128)(2,1)S(1)}, bf16[12,256,128]{2,1,0:T(8,128)(2,1)S(1)}, u32[]{:S(2)}, u32[]{:S(2)}) collective-permute-start(bf16[12,256,128]{2,1,0:T(8,128)(2,1)S(1)} %broadcast_select_fusion.3.refs_2_), channel_id=1, source_target_pairs={{0,1},{1,0},{2,3},{3,2},{4,5},{5,4},{6,7},{7,6},{8,9},{9,8},{10,11... | collective-permute-start | bytes 2359304 | tf_op jit(solution)/shard_map/ppermute | solution.py:324
  228.1 25.8 %collective-permute-start.30 = (bf16[12,256,128]{2,1,0:T(8,128)(2,1)S(1)}, bf16[12,256,128]{2,1,0:T(8,128)(2,1)S(1)}, u32[]{:S(2)}, u32[]{:S(2)}) collective-permute-start(bf16[12,256,128]{2,1,0:T(8,128)(2,1)S(1)} %broadcast_select_fusion.1.refs_3_), channel_id=1, source_target_pairs={{0,1},{1,0},{2,3},{3,2},{4,5},{5,4},{6,7},{7,6},{8,9},{9,8},{10,11... | collective-permute-start | bytes 2359304 | tf_op jit(solution)/shard_map/ppermute | solution.py:324
  240.4 28.2 %collective-permute-start.25 = (bf16[12,256,128]{2,1,0:T(8,128)(2,1)S(1)}, bf16[12,256,128]{2,1,0:T(8,128)(2,1)S(1)}, u32[]{:S(2)}, u32[]{:S(2)}) collective-permute-start(bf16[12,256,128]{2,1,0:T(8,128)(2,1)S(1)} %get-tuple-element.51), channel_id=1, source_target_pairs={{0,4},{4,8},{8,12},{1,5},{5,9},{9,13},{2,6},{6,10},{10,14},{3,7},{... | collective-permute-start | bytes 2359304 | tf_op jit(solution)/shard_map/ppermute | solution.py:368
  259.6 24.0 %collective-permute-start.31 = (bf16[256,2048]{1,0:T(8,128)(2,1)S(1)}, bf16[256,2048]{1,0:T(8,128)(2,1)S(1)}, u32[]{:S(2)}, u32[]{:S(2)}) collective-permute-start(bf16[256,2048]{1,0:T(8,128)(2,1)S(1)} %get-tuple-element.54), channel_id=1, source_target_pairs={{0,2},{2,0},{1,3},{3,1},{4,6},{6,4},{5,7},{7,5},{8,10},{10,8},{9,1... | collective-permute-start | bytes 3145736 | tf_op jit(solution)/shard_map/ppermute | solution.py:468
  315.8 33.3 %collective-permute-start.42 = (bf16[12,256,128]{2,1,0:T(8,128)(2,1)S(1)}, bf16[12,256,128]{2,1,0:T(8,128)(2,1)S(1)}, u32[]{:S(2)}, u32[]{:S(2)}) collective-permute-start(bf16[12,256,128]{2,1,0:T(8,128)(2,1)S(1)} %copy-done.50), channel_id=1, source_target_pairs={{0,1},{1,0},{2,3},{3,2},{4,5},{5,4},{6,7},{7,6},{8,9},{9,8},{10,11... | collective-permute-start | bytes 2359304 | tf_op jit(solution)/shard_map/ppermute | solution.py:324
  316.1 33.0 %collective-permute-start.44 = (bf16[12,256,128]{2,1,0:T(8,128)(2,1)S(1)}, bf16[12,256,128]{2,1,0:T(8,128)(2,1)S(1)}, u32[]{:S(2)}, u32[]{:S(2)}) collective-permute-start(bf16[12,256,128]{2,1,0:T(8,128)(2,1)S(1)} %broadcast_select_fusion.2.refs_2_), channel_id=1, source_target_pairs={{0,1},{1,0},{2,3},{3,2},{4,5},{5,4},{6,7},{7,6},{8,9},{9,8},{10,11... | collective-permute-start | bytes 2359304 | tf_op jit(solution)/shard_map/ppermute | solution.py:324
  316.7 32.4 %collective-permute-start.43 = (bf16[12,256,128]{2,1,0:T(8,128)(2,1)S(1)}, bf16[12,256,128]{2,1,0:T(8,128)(2,1)S(1)}, u32[]{:S(2)}, u32[]{:S(2)}) collective-permute-start(bf16[12,256,128]{2,1,0:T(8,128)(2,1)S(1)} %broadcast_select_fusion.4.refs_1_), channel_id=1, source_target_pairs={{0,1},{1,0},{2,3},{3,2},{4,5},{5,4},{6,7},{7,6},{8,9},{9,8},{10,11... | collective-permute-start | bytes 2359304 | tf_op jit(solution)/shard_map/ppermute | solution.py:324
  (87 other events, 2247.8 us)

commit v3 on v2

--- a/solution.py
+++ b/solution.py
@@ -183,21 +183,22 @@
     )(offs, *pieces, normed, slope, inv, mid, x, w_out, a_up)
 
 
-def encode_kernel(tab_j, tab_m, meta, *refs, panels, weights, deps, n, ns):
+def encode_kernel(tab_j, tab_m, meta, *refs, panels, weights, deps, n, ns, place, chunks):
     xs, ws = refs[:panels], refs[panels : panels + weights]
     refs = refs[: panels + weights] + refs[panels + weights + deps :]
-    out, acc = refs[panels + weights], refs[panels + weights + 1]
+    outs, rest = refs[panels + weights :][:chunks], refs[panels + weights + chunks :]
+    acc = rest[0]
     r = pl.program_id(0)
-    p = lax.rem(meta[0] + r, n) * ns + meta[1]
-    block = out.shape[3]
+    p = meta[place] * ns + r
+    chans, block = outs[0].shape[2:]
     if panels > 1:
-        hold = refs[panels + weights + 2]
+        hold = rest[1]
         wide = xs[0].shape[1]
 
         @pl.when(r == 0)
         def _():
             for i, piece in enumerate(xs):
-                at = lax.rem(meta[2] + panels - i, panels) * wide
+                at = lax.rem(meta[n] + panels - i, panels) * wide
                 hold[:, pl.ds(pl.multiple_of(at, wide), wide)] = piece[...]
 
         source = hold
@@ -211,66 +212,92 @@
             slot += 1
             panel = source[:, pl.ds(pl.multiple_of(j * block, block), block)]
             acc[m] += dg(panel, w[0, c], 1, 1)
-    out[0] = acc[0 : out.shape[1]].astype(BF)
-
-
-def encode(tab_j, tab_m, meta, pieces, chunk, chunks, weights, deps, n, ns):
-    chans, wide = pieces[0].shape[0] // chunks, pieces[0].shape[1]
+    for k, out in enumerate(outs):
+        out[0] = acc[0 : out.shape[1], k * chans : (k + 1) * chans].astype(BF)
+
+
+def encode(tab_j, tab_m, meta, pieces, weights, deps, n, ns, place, chunks):
+    chans, wide = pieces[0].shape
     panels = len(pieces)
     block = weights[0].shape[2]
     cap = sum(w.shape[1] for w in weights)
     scratch = [pltpu.VMEM((MBLK + 1, chans, block), F32)]
     if panels > 1:
         scratch.append(pltpu.VMEM((chans, wide * panels), BF))
-    where = lambda r, j, m, t: (lax.rem(t[0] + r, n) * ns + t[1], 0, 0, 0)
+    where = lambda r, j, m, t: (t[place] * ns + r, 0, 0, 0)
     return pl.pallas_call(
         functools.partial(
-            encode_kernel, panels=panels, weights=len(weights), deps=len(deps), n=n, ns=ns
+            encode_kernel, panels=panels, weights=len(weights), deps=len(deps), n=n, ns=ns,
+            place=place, chunks=chunks,
         ),
         grid_spec=pltpu.PrefetchScalarGridSpec(
             num_scalar_prefetch=3,
-            grid=(n,),
-            in_specs=[pl.BlockSpec((chans, wide), lambda r, j, m, t: (chunk, 0))] * panels
+            grid=(ns,),
+            in_specs=[pl.BlockSpec((chans, wide), lambda r, j, m, t: (0, 0))] * panels
             + [pl.BlockSpec((1,) + w.shape[1:], where) for w in weights]
             + [pl.BlockSpec(memory_space=pl.ANY)] * len(deps),
-            out_specs=pl.BlockSpec((1, MBLK, chans, block), lambda r, j, m, t: (r, 0, 0, 0)),
+            out_specs=[
+                pl.BlockSpec((1, MBLK, chans // chunks, block), lambda r, j, m, t: (r, 0, 0, 0))
+            ]
+            * chunks,
             scratch_shapes=scratch,
         ),
-        out_shape=jax.ShapeDtypeStruct((n, MBLK, chans, block), BF),
+        out_shape=[jax.ShapeDtypeStruct((ns, MBLK, chans // chunks, block), BF)] * chunks,
         compiler_params=params(),
         cost_estimate=pl.CostEstimate(
-            flops=2 * n * cap * chans * block * block * 4,
-            bytes_accessed=n * MBLK * chans * block * 4,
+            flops=2 * ns * cap * chans * block * block * 4,
+            bytes_accessed=ns * MBLK * chans * block * 4,
             transcendentals=0,
         ),
         name="encode",
     )(tab_j, tab_m, meta, *pieces, *weights, *deps)
 
 
-def decode_kernel(tab_j, tab_m, meta, *refs, n, ns, weights, alias, nf):
-    here, there, refs = refs[:n], refs[n : 2 * n], refs[2 * n :]
-    ws, rest = refs[:weights], refs[weights + (1 if alias else 0) :]
+def decode_kernel(tab_j, tab_m, meta, *refs, n, ns, weights, nf, chunks):
+    each = 2 * n - 1
+    count = each * chunks
+    ws, rest = refs[count : count + weights], refs[count + weights :]
     outs, (hold, acc, sem) = rest[:-3], rest[-3:]
     z, s = meta[0], meta[1]
-    block = hold.shape[3]
-    for r in range(n):
-        for side, mesh in enumerate((here[r], there[r])):
-            at = r * ns + side
-            pltpu.make_async_copy(mesh, hold.at[at], sem.at[at]).start()
+    chans, block = refs[0].shape[2:]
+    for k in range(chunks):
+        group = refs[k * each : (k + 1) * each]
+        mine, theirs = group[:n], (None,) + group[n:]
+
+        def copy(ref, r):
+            to = hold.at[r, :, :, pl.ds(k * chans, chans), :]
+            pltpu.make_async_copy(ref, to, sem.at[r, k]).start()
+
+        copy(group[0], 0)
+        for r in range(1, n):
+            above = z + r < n
+            for here, test in ((mine, 1), (theirs, 0)):
+
+                @pl.when(jnp.logical_and(above, s == test))
+                def _():
+                    copy(here[r], r)
+
+                @pl.when(jnp.logical_and(jnp.logical_not(above), s == 1 - test))
+                def _():
+                    copy(here[n - r], r)
+
     acc[...] = jnp.zeros_like(acc)
 
     def step(i, carry):
-        p = lax.rem(z + i // ns, n) * ns + lax.rem(s + lax.rem(i, ns), ns)
-        pltpu.make_async_copy(here[0], hold.at[i], sem.at[i]).wait()
-        slot = 0
-        for w in ws:
-            for c in range(w.shape[1]):
-                j, m = tab_j[p, slot], tab_m[p, slot]
-                slot += 1
-                acc[j] += dg(hold[i, jnp.minimum(m, MBLK - 1)], w[p, c], 1, 0)
+        for k in range(chunks):
+            to = hold.at[i, :, :, pl.ds(k * chans, chans), :]
+            pltpu.make_async_copy(refs[k * each], to, sem.at[i, k]).wait()
+        for side in range(ns):
+            p = lax.rem(z + i, n) * ns + side
+            slot = 0
+            for w in ws:
+                for c in range(w.shape[1]):
+                    j, m = tab_j[p, slot], tab_m[p, slot]
+                    slot += 1
+                    acc[j] += dg(hold[i, side, jnp.minimum(m, MBLK - 1)], w[p, c], 1, 0)
         return carry
 
-    lax.fori_loop(0, n * ns, step, 0)
+    lax.fori_loop(0, n, step, 0)
     per = (acc.shape[0] - 1) // nf
     for r, out in enumerate(outs):
         first = lax.rem(meta[2] + r, nf) * per
@@ -278,37 +305,27 @@
             out[:, g * block : (g + 1) * block] = acc[first + g].astype(BF)
 
 
-def decode(tab_j, tab_m, meta, here, there, weights, grid_count, chunk, chunks, base, nf, n, ns):
-    chans, block = here[0].shape[1], here[0].shape[2]
-    meshes = [*here, *there]
+def decode(tab_j, tab_m, meta, meshes, weights, grid_count, nf, n, ns, chunks):
+    chans, block = meshes[0].shape[2] * chunks, meshes[0].shape[3]
     rows = grid_count * block
-    if nf > 1:
-        shape = (chans, rows // nf)
-        out_spec = pl.BlockSpec(shape, lambda i, j, m, t: (0, 0))
-    else:
-        shape = (chans * chunks, rows)
-        out_spec = pl.BlockSpec((chans, rows), lambda i, j, m, t: (chunk, 0))
-    alias = base is not None
-    whole = lambda a: pl.BlockSpec(a.shape, lambda i, j, m, t: (0,) * a.ndim)
+    shape = (chans, rows // nf)
     return pl.pallas_call(
         functools.partial(
-            decode_kernel, n=n, ns=ns, weights=len(weights), alias=alias, nf=nf
+            decode_kernel, n=n, ns=ns, weights=len(weights), nf=nf, chunks=chunks
         ),
         grid_spec=pltpu.PrefetchScalarGridSpec(
             num_scalar_prefetch=3,
             grid=(1,),
             in_specs=[pl.BlockSpec(memory_space=pl.ANY)] * len(meshes)
-            + [whole(w) for w in weights]
-            + ([pl.BlockSpec(memory_space=pl.ANY)] if alias else []),
-            out_specs=[out_spec] * nf,
+            + [pl.BlockSpec(w.shape, lambda i, j, m, t: (0, 0, 0, 0)) for w in weights],
+            out_specs=[pl.BlockSpec(shape, lambda i, j, m, t: (0, 0))] * nf,
             scratch_shapes=[
-                pltpu.VMEM((n * ns, MBLK, chans, block), BF),
+                pltpu.VMEM((n, ns, MBLK, chans, block), BF),
                 pltpu.VMEM((grid_count + 1, chans, block), F32),
-                pltpu.SemaphoreType.DMA((n * ns,)),
+                pltpu.SemaphoreType.DMA((n, chunks)),
             ],
         ),
         out_shape=[jax.ShapeDtypeStruct(shape, BF)] * nf,
-        input_output_aliases={3 + 2 * n + len(weights): 0} if alias else {},
         compiler_params=params(),
         cost_estimate=pl.CostEstimate(
             flops=2 * n * ns * 16 * chans * block * block * 4,
@@ -316,7 +333,7 @@
             transcendentals=0,
         ),
         name="decode",
-    )(tab_j, tab_m, meta, *meshes, *weights, *([base] if alias else []))
+    )(tab_j, tab_m, meta, *meshes, *weights)
 
 
 def swap_sub(a):
@@ -324,58 +341,43 @@
     return lax.ppermute(a, "sub", [(i, (i + 1) % ns) for i in range(ns)])
 
 
-def add_kernel(*refs, terms, deps):
-    ins, outs = refs[: sum(terms)], refs[sum(terms) + deps :]
-    for out, count in zip(outs, terms):
-        value = ins[0][0].astype(F32) + ins[1][0].astype(F32)
-        for ref in ins[2:count]:
-            value = value + ref[...].astype(F32)
-        out[...] = value.astype(BF)
-        ins = ins[count:]
-
-
-def add(own, other, groups, deps):
-    shape = own.shape[1:]
-    parts = 3 if shape[0] % 3 == 0 else 1
-    piece = (shape[0] // parts,) + shape[1:]
-    spec = pl.BlockSpec(piece, lambda i: (i, 0, 0))
-    arrays, specs = [], []
-    for place, terms in groups:
-        pick = pl.BlockSpec((1,) + piece, lambda i, place=place: (place, i, 0, 0))
-        arrays += [own, other, *terms]
-        specs += [pick, pick] + [spec] * len(terms)
+def add_kernel(*refs, count):
+    value = refs[0][...].astype(F32)
+    for ref in refs[1:count]:
+        value = value + ref[...].astype(F32)
+    refs[-1][...] = value.astype(BF)
+
+
+def add(terms, deps):
+    shape = terms[0].shape
+    parts = 3 if shape[1] % 3 == 0 else 1
+    spec = pl.BlockSpec((1, shape[1] // parts) + shape[2:], lambda i, j: (i, j, 0, 0))
     return pl.pallas_call(
-        functools.partial(
-            add_kernel, terms=[2 + len(terms) for _, terms in groups], deps=len(deps)
-        ),
-        grid=(parts,),
-        in_specs=specs + [pl.BlockSpec(memory_space=pl.ANY)] * len(deps),
-        out_specs=[spec] * len(groups),
-        out_shape=[jax.ShapeDtypeStruct(shape, BF)] * len(groups),
+        functools.partial(add_kernel, count=len(terms)),
+        grid=(shape[0], parts),
+        in_specs=[spec] * len(terms) + [pl.BlockSpec(memory_space=pl.ANY)] * len(deps),
+        out_specs=spec,
+        out_shape=jax.ShapeDtypeStruct(shape, BF),
         compiler_params=params(),
         name="add",
-    )(*arrays, *deps)
-
-
-def reduce_step(t, own, other, up, down, deps):
-    n = own.shape[0]
-    first = up is None
-    up, down = add(
-        own, other, [(n - t, [] if first else [up]), (t, [] if first else [down])], deps
-    )
-    return (
-        up,
-        lax.ppermute(up, "lat", [(i, i + 1) for i in range(n - 1) if i <= t - 1]),
-        lax.ppermute(down, "lat", [(i, i - 1) for i in range(1, n) if i >= n - t]),
-    )
-
-
-def spread_step(t, up, down):
+    )(*terms, *deps)
+
+
+def along(value, reach_up, reach_down):
+    n, ns = lax.axis_size("lat"), lax.axis_size("sub")
+    pairs = [(i * ns, (i + 1) * ns) for i in range(n - 1) if reach_up(i)]
+    pairs += [(i * ns + 1, (i - 1) * ns + 1) for i in range(1, n) if reach_down(i)]
+    return lax.ppermute(value, ("lat", "sub"), pairs)
+
+
+def reduce_step(t, value):
     n = lax.axis_size("lat")
-    return (
-        lax.ppermute(up, "lat", [(i, i + 1) for i in range(n - 1) if i >= t - 1]),
-        lax.ppermute(down, "lat", [(i, i - 1) for i in range(1, n) if i <= n - t]),
-    )
+    return along(value, lambda i: i <= t - 1, lambda i: i >= n - t)
+
+
+def spread_step(t, value):
+    n = lax.axis_size("lat")
+    return along(value, lambda i: i >= t - 1, lambda i: i <= n - t)
 
 
 def add_all(value, axes):
@@ -469,85 +471,84 @@
     emb_pieces = [emb[r] if r == 0 else shift(emb[r], r) for r in range(nf)]
 
     meta_own = jnp.stack([z, s, f]).astype(jnp.int32)
-    meta_sib = jnp.stack([z, (s + 1) % ns, f]).astype(jnp.int32)
-    chunks = 1
-
-    lag = n
-    sources = [([cot], c) for c in range(chunks)] + [(emb_pieces, c) for c in range(chunks)]
-    state = [{} for _ in sources]
-    grads, offs, decoded = [], [], None
+    place_ids = jnp.arange(n, dtype=jnp.int32)
+    away = jnp.where(s == 0, (n - place_ids) % n, place_ids)
+    meta_enc = jnp.concatenate([(z + away) % n, f[None]]).astype(jnp.int32)
+
+    chunks = 2
+    halves = range(chunks)
+    passes = [{"h": [{} for _ in halves]} for _ in range(2)]
     token = mid
-    last = lag * (len(sources) - 1) + 2 * (n - 1) + 3
-    for now in range(-1, last):
-        made, put = [], []
-
-        def keep(where, key, value):
-            made.append(value)
-            put.append((where, key))
-
-        for k, (pieces, chunk) in enumerate(sources):
-            st, at = state[k], now - lag * k
-            if at == -1:
-                args = (pieces, chunk, chunks, weights, [token], n, ns)
-                keep(st, "other", swap_sub(encode(tab_get, tab_m, meta_sib, *args)))
-                keep(st, "own", encode(tab_get, tab_m, meta_own, *args))
-            elif 0 <= at < n - 1:
-                behind = [state[k - 1][key, at + 1] for key in ("up", "down")] if k else []
-                sent, up, down = reduce_step(
-                    at + 1, st["own"], st["other"], st.get("up"), st.get("down"), behind
+    for now in range(3 * n - 1):
+        for k, pieces in enumerate(([cot], emb_pieces)):
+            whole, at = passes[k], now - n * k
+            grad = k == 0
+
+            def make(q, after):
+                outs = encode(
+                    tab_get, tab_m, meta_enc, pieces, weights, [after], n, ns, q, chunks
                 )
-                if at == n - 2:
-                    token = sent
-                keep(st, "up", up)
-                keep(st, "down", down)
-            elif n - 1 <= at < 2 * n - 2:
-                t = at - n + 2
-                if t == 1:
-                    behind = [state[k - 1]["grad", 0]] if k else []
-                    (mesh,) = add(
-                        st["own"], st["other"], [(0, [st["up"], st["down"]])], behind
-                    )
-                    st["here"], st["there"] = {0: mesh}, {0: swap_sub(mesh)}
-                    st["up"], st["down"] = mesh, mesh
-                if k >= chunks and t > 1:
-                    if t == n - 1:
-                        sums = backward(
-                            jnp.stack(offs).astype(jnp.int32), grads, normed, slope, inv, mid, x,
-                            frozen_output_weight, adapter_up_weight,
-                        )
-                    done = list(sums) if t == n - 1 else grads
-                    st["up"], st["down"], *_ = lax.optimization_barrier(
-                        (st["up"], st["down"], *done)
-                    )
-                st["up"], st["down"] = spread_step(t, st["up"], st["down"])
-                st["up", t], st["down", t] = st["up"], st["down"]
-                for r in range(1, n):
-                    if max(r, n - r) == t:
-                        st["here"][r] = jnp.where(z + r < n, st["down", r], st["up", n - r])
-                        st["there"][r] = swap_sub(st["here"][r])
-            elif at == 2 * n - 2:
-                grad = k < chunks
-                if not grad:
-                    sums = add_all(jnp.concatenate(sums, axis=1), ("sub", "fsdp", "lat"))
-                    st["here"][0], _ = lax.optimization_barrier((st["here"][0], sums))
-                out = decode(
-                    tab_put, tab_m, meta_own, [st["here"][r] for r in range(n)],
-                    [st["there"][r] for r in range(n)], weights, grid_count,
-                    chunk, chunks, None if grad else decoded, nf if grad else 1, n, ns,
+                for h in halves:
+                    whole["h"][h]["sums", q] = outs[h]
+
+            if at == -1 or (at == 0 and grad):
+                for q in (n - 1, 1):
+                    make(q, token)
+                for st in whole["h"]:
+                    st["other", 1] = swap_sub(st["sums", n - 1])
+            for h, st in enumerate(whole["h"]):
+                ahead = passes[0]["h"][h]
+                if 0 <= at < n - 1:
+                    t = at + 1
+                    behind = emb_pieces[1:] if t == n - 1 else []
+                    behind = behind if grad else [ahead["came", t]]
+                    terms = [st["sums", t], st["other", t]] + ([st["now"]] if t > 1 else [])
+                    sent = add(terms, behind)
+                    st["now"] = reduce_step(t, sent)
+                    if h == chunks - 1:
+                        if t == 1:
+                            for q in range(n):
+                                if q not in (1, n - 1):
+                                    make(q, sent)
+                            for other in whole["h"]:
+                                for u in range(2, n):
+                                    other["other", u] = swap_sub(other["sums", n - u])
+                        if t == n - 1:
+                            token = sent
+                elif n - 1 <= at < 2 * n - 2:
+                    t = at - n + 2
+                    if t == 1:
+                        behind = [] if grad else [passes[0]["out"][0]]
+                        half = add([st["sums", 0], st["now"]], behind)
+                        st["mesh"] = st["now"] = add([half, swap_sub(half)], [])
+                    if not grad and t > 1 and h == chunks - 1:
+                        if t == n - 1:
+                            sums = backward(
+                                offs, grads, normed, slope, inv, mid, x,
+                                frozen_output_weight, adapter_up_weight,
+                            )
+                            sums = add_all(jnp.concatenate(sums, axis=1), ("sub", "fsdp"))
+                        done = [sums] if t == n - 1 else grads
+                        st["now"], *_ = lax.optimization_barrier((st["now"], *done))
+                    st["now"] = st["came", t] = spread_step(t, st["now"])
+                    st["theirs", t] = swap_sub(st["now"])
+            if at == 2 * n - 2:
+                meshes = []
+                for st in whole["h"]:
+                    meshes.append(st["mesh"])
+                    meshes += [st["came", t] for t in range(1, n)]
+                    meshes += [st["theirs", t] for t in range(1, n)]
+                whole["out"] = decode(
+                    tab_put, tab_m, meta_own, meshes, weights, grid_count, nf if grad else 1,
+                    n, ns, chunks,
                 )
                 if grad:
-                    for r in range(nf):
-                        st["grad", r] = out[r]
-                else:
-                    decoded = out[0]
-                if grad:
-                    for r in range(nf):
-                        piece = st["grad", r]
-                        grads.append(piece if r == 0 else shift(piece, r))
-                        offs.append(((f - r + nf) % nf) * chans + chunk * (chans // chunks))
-        for spot, value in zip(put, made):
-            spot[0][spot[1]] = value
-
+                    grads = [shift(g, r) if r else g for r, g in enumerate(whole["out"])]
+                    turns = jnp.arange(nf, dtype=jnp.int32)
+                    offs = (((f - turns + nf) % nf) * chans).astype(jnp.int32)
+    decoded = passes[1]["out"][0]
+
+    sums = add_all(sums, ("lat",))
     up_gradient, grad_down = sums[:, :width], sums[:, width:].T
     return (decoded.reshape(1, 1, chans, grid_rows), grad_down, up_gradient)
 

time: 358 us -> 316 us (0.88)
  waiting for transfers between devices: 171 us -> 98 us
  starting transfers between devices: 93.9 us -> 140 us
  local copies, waits for them, and re-layouts: 22.2 us -> 9.98 us
    ppermute x24, waiting for transfers between devices: 122 us -> 38.7 us  [along(): return lax.ppermute(value, ('lat', 'sub'), pairs)]
    ppermute x4, starting transfers between devices: 2.29 us -> 32.3 us  [add_all(): lax.ppermute(value, axis, [(i, i ^ step) for i in range(size)])]
    ppermute x2, waiting for transfers between devices: 6.98 us -> 21.3 us  [body(): lax.ppermute(v, 'fsdp', [(i, (i + r) % nf) for i in range(nf)])]
    unnamed x128 -> x40, local copies, waits for them, and re-layouts: 20.9 us -> 8.66 us
    ppermute x10 -> x28, starting transfers between devices: 1.55 us -> 13.1 us  [swap_sub(): return lax.ppermute(a, 'sub', [(i, (i + 1) % ns) for i in range(ns)])]
    ppermute x4, waiting for transfers between devices: 13.4 us -> 8.17 us  [add_all(): lax.ppermute(value, axis, [(i, i ^ step) for i in range(size)])]
    ppermute x24, starting transfers between devices: 69.8 us -> 74.4 us  [along(): return lax.ppermute(value, ('lat', 'sub'), pairs)]
    pallas_call x4 -> x8, Pallas kernels: 13.9 us -> 17 us  [encode(): pl.pallas_call(functools.partial(encode_kernel, panels=panels, weights=le...]
  transfers between devices with their start and end apart: 48 -> 66, of which waited for: 24 -> 23; matrix products, arithmetic and copies ran while one was open for 2% -> 1% of each run, Pallas kernels for 9% -> 13%
where the time goes in v3:
time: 316 us; the launch traced here: 315 us
  starting transfers between devices  140 us (44%)
  waiting for transfers between devices  98 us (31%)
  Pallas kernels  49.5 us (16%)
  blocking collectives  12.9 us (4%)
  local copies, waits for them, and re-layouts  9.98 us (3%)
    ppermute x24, starting transfers between devices, along(): return lax.ppermute(value, ('lat', 'sub'), pairs)  74.4 us
    ppermute x24, waiting for transfers between devices, along(): return lax.ppermute(value, ('lat', 'sub'), pairs)  38.7 us
    ppermute x4, starting transfers between devices, add_all(): lax.ppermute(value, axis, [(i, i ^ step) for i in range(size)])  32.3 us
    ppermute x2, waiting for transfers between devices, body(): lax.ppermute(v, 'fsdp', [(i, (i + r) % nf) for i in range(nf)])  21.3 us
    ppermute x3, waiting for transfers between devices, body(): over_x = lambda v: lax.ppermute(v, 'fsdp', flip)  21.2 us
    pallas_call x8, Pallas kernels, encode(): pl.pallas_call(functools.partial(encode_kernel, panels=panels, weights=le...  17 us
    ppermute x28, starting transfers between devices, swap_sub(): return lax.ppermute(a, 'sub', [(i, (i + 1) % ns) for i in range(ns)])  13.1 us
    all_gather x1, blocking collectives, body(): both = lax.all_gather(pattern, ('lat', 'sub'), tiled=True)  12.9 us
  transfers between devices with their start and end apart: 66, of which 23 were waited for; matrix products, arithmetic and copies ran while one was open for 1% of the time, Pallas kernels for 13%

profile of v3, /device:TPU:0, one launch (start us, length us, event | category | flops | bytes accessed | tf_op | source)
XLA Modules:
  0.0 315.3 jit_solution(1393640616795226481)
XLA Ops:
  5.7 6.3 %all-to-all-start = ((bf16[8,2,128,128]{3,2,1,0:T(8,128)(2,1)}), bf16[8,2,128,128]{3,2,1,0:T(8,128)(2,1)S(1)}, u32[]{:S(2)}, u32[]{:S(2)}) async-start(bf16[8,2,128,128]{3,2,1,0:T(8,128)(2,1)} %get-tuple-element.35), calls=%async_computation | async-start | bytes 1048576 | tf_op jit(solution)/shard_map/all_to_all | solution.py:435
  12.2 6.7 %forward.1 = (bf16[256,2048]{1,0:T(8,128)(2,1)S(1)}, bf16[256,2048]{1,0:T(8,128)(2,1)S(1)}, f32[512,2048]{1,0:T(8,128)S(1)}, f32[512,2048]{1,0:T(8,128)S(1)}, f3...) custom-call(s32[1]{0:T(128)} %bitcast.9.meta, bf16[227,2048]{1,0:T(8,128)(2,1)S(1)} %bitcast.21, ...), custom_call_target="tpu_custom_call" | custom-call | flops 1549795328 | bytes 12582912 | tf_op jit(solution)/shard_map/forward/pallas_call | solution.py:90
  34.2 12.9 %all_gather.3 = s32[8,2,96]{2,1,0:T(2,128)S(1)} all-gather(s32[1,2,96]{2,1,0:T(2,128)S(1)} %add_bitcast_fusion), channel_id=1, replica_groups=mesh['parts'=2,'lat'=4,'fsdp'=2,'sub'=2] {'lat','sub'}, dimensions={0}, use_global_device_ids=true | all-gather | bytes 6912 | tf_op jit(solution)/shard_map/all_gather | solution.py:459
  51.6 11.8 %collective-permute-done.2.refs_4_.refs_5_.refs_17_ = bf16[8,2,128,128]{3,2,1,0:T(8,128)(2,1)S(1)} collective-permute-done((bf16[8,2,128,128]{3,2,1,0:T(8,128)(2,1)S(1)}, bf16[8,2,128,128]{3,2,1,0:T(8,128)(2,1)S(1)}, u32[]{:S(2)}, u32[]{:S(2)}) %collective-permute-start.2) | collective-permute-done | bytes 524320 | tf_op jit(solution)/shard_map/ppermute | solution.py:446
  64.4 9.3 %collective-permute-done.5.refs_7_.refs_8_.refs_20_ = bf16[8,2,128,128]{3,2,1,0:T(8,128)(2,1)S(1)} collective-permute-done((bf16[8,2,128,128]{3,2,1,0:T(8,128)(2,1)S(1)}, bf16[8,2,128,128]{3,2,1,0:T(8,128)(2,1)S(1)}, u32[]{:S(2)}, u32[]{:S(2)}) %collective-permute-start.5) | collective-permute-done | bytes 524320 | tf_op jit(solution)/shard_map/ppermute | solution.py:446
  95.8 4.4 %collective-permute-start.11 = (bf16[2,12,128,128]{3,2,1,0:T(8,128)(2,1)S(1)}, bf16[2,12,128,128]{3,2,1,0:T(8,128)(2,1)S(1)}, u32[]{:S(2)}, u32[]{:S(2)}) collective-permute-start(bf16[2,12,128,128]{3,2,1,0:T(8,128)(2,1)S(1)} %add.174), channel_id=1, source_target_pairs={{0,4},{4,8},{9,5},{13,9},{2,6},{6,10},{11,7},{15,11},{16,20},{20,2... | collective-permute-start | bytes 2359304 | tf_op jit(solution)/shard_map/ppermute | solution.py:370
  104.2 4.4 %collective-permute-start.23 = (bf16[2,12,128,128]{3,2,1,0:T(8,128)(2,1)S(1)}, bf16[2,12,128,128]{3,2,1,0:T(8,128)(2,1)S(1)}, u32[]{:S(2)}, u32[]{:S(2)}) collective-permute-start(bf16[2,12,128,128]{3,2,1,0:T(8,128)(2,1)S(1)} %add.180), channel_id=1, source_target_pairs={{0,4},{4,8},{9,5},{13,9},{2,6},{6,10},{11,7},{15,11},{16,20},{20,2... | collective-permute-start | bytes 2359304 | tf_op jit(solution)/shard_map/ppermute | solution.py:370
  108.7 6.8 %collective-permute-done.refs_3_.refs_1_ = bf16[256,2048]{1,0:T(8,128)(2,1)S(1)} collective-permute-done((bf16[256,2048]{1,0:T(8,128)(2,1)S(1)}, bf16[256,2048]{1,0:T(8,128)(2,1)S(1)}, u32[]{:S(2)}, u32[]{:S(2)}) %collective-permute-start) | collective-permute-done | bytes 1048608 | tf_op jit(solution)/shard_map/ppermute | solution.py:470
  121.1 4.4 %collective-permute-start.24 = (bf16[2,12,128,128]{3,2,1,0:T(8,128)(2,1)S(1)}, bf16[2,12,128,128]{3,2,1,0:T(8,128)(2,1)S(1)}, u32[]{:S(2)}, u32[]{:S(2)}) collective-permute-start(bf16[2,12,128,128]{3,2,1,0:T(8,128)(2,1)S(1)} %add.181), channel_id=1, source_target_pairs={{0,4},{4,8},{8,12},{5,1},{9,5},{13,9},{2,6},{6,10},{10,14},{7,3},{... | collective-permute-start | bytes 2359304 | tf_op jit(solution)/shard_map/ppermute | solution.py:370
  129.5 8.1 %collective-permute-done.24.refs_1_ = bf16[2,12,128,128]{3,2,1,0:T(8,128)(2,1)S(1)} collective-permute-done((bf16[2,12,128,128]{3,2,1,0:T(8,128)(2,1)S(1)}, bf16[2,12,128,128]{3,2,1,0:T(8,128)(2,1)S(1)}, u32[]{:S(2)}, u32[]{:S(2)}) %collective-permute-start.24) | collective-permute-done | bytes 786464 | tf_op jit(solution)/shard_map/ppermute | solution.py:370
  155.8 6.7 %collective-permute-start.49 = (bf16[2,12,128,128]{3,2,1,0:T(8,128)(2,1)S(1)}, bf16[2,12,128,128]{3,2,1,0:T(8,128)(2,1)S(1)}, u32[]{:S(2)}, u32[]{:S(2)}) collective-permute-start(bf16[2,12,128,128]{3,2,1,0:T(8,128)(2,1)S(1)} %add.178.refs_10_), channel_id=1, source_target_pairs={{0,4},{13,9},{2,6},{15,11},{16,20},{29,25},{18,22},{31,27}} | collective-permute-start | bytes 2359304 | tf_op jit(solution)/shard_map/ppermute | solution.py:370
  165.9 4.9 %collective-permute-start.27 = (bf16[2,12,128,128]{3,2,1,0:T(8,128)(2,1)S(1)}, bf16[2,12,128,128]{3,2,1,0:T(8,128)(2,1)S(1)}, u32[]{:S(2)}, u32[]{:S(2)}) collective-permute-start(bf16[2,12,128,128]{3,2,1,0:T(8,128)(2,1)S(1)} %add.184), channel_id=1, source_target_pairs={{0,4},{13,9},{2,6},{15,11},{16,20},{29,25},{18,22},{31,27}} | collective-permute-start | bytes 2359304 | tf_op jit(solution)/shard_map/ppermute | solution.py:370
  173.4 6.8 %collective-permute-done.27.refs_2_ = bf16[2,12,128,128]{3,2,1,0:T(8,128)(2,1)S(1)} collective-permute-done((bf16[2,12,128,128]{3,2,1,0:T(8,128)(2,1)S(1)}, bf16[2,12,128,128]{3,2,1,0:T(8,128)(2,1)S(1)}, u32[]{:S(2)}, u32[]{:S(2)}) %collective-permute-start.27) | collective-permute-done | bytes 786464 | tf_op jit(solution)/shard_map/ppermute | solution.py:370
  185.8 6.3 %collective-permute-start.29 = (bf16[2,12,128,128]{3,2,1,0:T(8,128)(2,1)S(1)}, bf16[2,12,128,128]{3,2,1,0:T(8,128)(2,1)S(1)}, u32[]{:S(2)}, u32[]{:S(2)}) collective-permute-start(bf16[2,12,128,128]{3,2,1,0:T(8,128)(2,1)S(1)} %add.185), channel_id=1, source_target_pairs={{0,4},{4,8},{9,5},{13,9},{2,6},{6,10},{11,7},{15,11},{16,20},{20,2... | collective-permute-start | bytes 2359304 | tf_op jit(solution)/shard_map/ppermute | solution.py:370
  192.7 8.2 %collective-permute-start.39 = (bf16[2,12,128,128]{3,2,1,0:T(8,128)(2,1)S(1)}, bf16[2,12,128,128]{3,2,1,0:T(8,128)(2,1)S(1)}, u32[]{:S(2)}, u32[]{:S(2)}) collective-permute-start(bf16[2,12,128,128]{3,2,1,0:T(8,128)(2,1)S(1)} %collective-permute-done.36.refs_10_.refs_3_), channel_id=1, source_target_pairs={{0,1},{1,0},{2,3},{3,2},{4,5},{5,4},{6,7},{7,6},{8,9},{9,8},{10,11... | collective-permute-start | bytes 2359304 | tf_op jit(solution)/shard_map/ppermute | solution.py:341
  203.2 6.3 %collective-permute-start.51 = (bf16[2,12,128,128]{3,2,1,0:T(8,128)(2,1)S(1)}, bf16[2,12,128,128]{3,2,1,0:T(8,128)(2,1)S(1)}, u32[]{:S(2)}, u32[]{:S(2)}) collective-permute-start(bf16[2,12,128,128]{3,2,1,0:T(8,128)(2,1)S(1)} %add.190), channel_id=1, source_target_pairs={{0,4},{4,8},{8,12},{5,1},{9,5},{13,9},{2,6},{6,10},{10,14},{7,3},{... | collective-permute-start | bytes 2359304 | tf_op jit(solution)/shard_map/ppermute | solution.py:370
  216.7 5.1 %decode.2 = (bf16[256,2048]{1,0:T(8,128)(2,1)S(1)}, bf16[256,2048]{1,0:T(8,128)(2,1)S(1)}) custom-call(s32[8,16]{1,0:T(8,128)S(1)} %get-tuple-element.74.tab_j, s32[8,16]{1,0:T(8,128)S(1)} %get-tuple-element.75.tab_m, s32[3]{0:T(128)S(1)} %pad_add_fusion.1.meta, bf16[2,12,128,128]{3,2,1,0:T(8,128)(2,1)S(1)} %add.183.refs_0_, ...), custom_call_target="tpu_custom_call" | custom-call | flops 4294967296 | bytes 12582912 | tf_op jit(solution)/shard_map/decode/pallas_call | solution.py:312
  222.3 5.2 %collective-permute-done.31.refs_1_ = bf16[2,12,128,128]{3,2,1,0:T(8,128)(2,1)S(1)} collective-permute-done((bf16[2,12,128,128]{3,2,1,0:T(8,128)(2,1)S(1)}, bf16[2,12,128,128]{3,2,1,0:T(8,128)(2,1)S(1)}, u32[]{:S(2)}, u32[]{:S(2)}) %collective-permute-start.31) | collective-permute-done | bytes 786464 | tf_op jit(solution)/shard_map/ppermute | solution.py:370
  229.6 4.4 %collective-permute-start.53 = (bf16[2,12,128,128]{3,2,1,0:T(8,128)(2,1)S(1)}, bf16[2,12,128,128]{3,2,1,0:T(8,128)(2,1)S(1)}, u32[]{:S(2)}, u32[]{:S(2)}) collective-permute-start(bf16[2,12,128,128]{3,2,1,0:T(8,128)(2,1)S(1)} %add.192.refs_7_), channel_id=1, source_target_pairs={{0,4},{4,8},{8,12},{5,1},{9,5},{13,9},{2,6},{6,10},{10,14},{7,3},{... | collective-permute-start | bytes 2359304 | tf_op jit(solution)/shard_map/ppermute | solution.py:370
  238.8 14.6 %collective-permute-done.54.refs_1_ = bf16[256,2048]{1,0:T(8,128)(2,1)S(1)} collective-permute-done((bf16[256,2048]{1,0:T(8,128)(2,1)S(1)}, bf16[256,2048]{1,0:T(8,128)(2,1)S(1)}, u32[]{:S(2)}, u32[]{:S(2)}) %collective-permute-start.54) | collective-permute-done | bytes 1048608 | tf_op jit(solution)/shard_map/ppermute | solution.py:470
  254.9 6.1 %backward.1 = (f32[16,512]{1,0:T(8,128)S(1)}, f32[16,227]{1,0:T(8,128)S(1)}) custom-call(s32[2]{0:T(128)S(1)} %fusion.6.offs, bf16[256,2048]{1,0:T(8,128)(2,1)S(1)} %get-tuple-element.56.refs_2_.refs_0_, bf16[256,2048]{1,0:T(8,128)(2,1)S(1)} %collective-permute-done.54.refs_1_, f32[512,2048]{1,0:T(8,128)S(1)} %copy-done.3, f32[512,2048]{1,0:T(8,128)S(1)} %copy-done.5, ...), custom_call_target="tpu_custom_call" | custom-call | flops 1073741824 | bytes 10485760 | tf_op jit(solution)/shard_map/backward/pallas_call | solution.py:161
  268.4 11.3 %collective-permute-start.62 = (f32[16,739]{1,0:T(8,128)S(1)}, f32[16,739]{1,0:T(8,128)S(1)}, u32[]{:S(2)}, u32[]{:S(2)}) collective-permute-start(f32[16,739]{1,0:T(8,128)S(1)} %add.135), channel_id=1, source_target_pairs={{0,4},{4,0},{8,12},{12,8},{1,5},{5,1},{9,13},{13,9},{2,6},{6,2},{1... | collective-permute-start | bytes 141896 | tf_op jit(solution)/shard_map/ppermute | solution.py:387
  282.3 18.7 %collective-permute-start.63 = (f32[16,739]{1,0:T(8,128)S(1)}, f32[16,739]{1,0:T(8,128)S(1)}, u32[]{:S(2)}, u32[]{:S(2)}) collective-permute-start(f32[16,739]{1,0:T(8,128)S(1)} %add.136), channel_id=1, source_target_pairs={{0,8},{4,12},{8,0},{12,4},{1,9},{5,13},{9,1},{13,5},{2,10},{6,14},... | collective-permute-start | bytes 141896 | tf_op jit(solution)/shard_map/ppermute | solution.py:387
  308.7 6.4 %decode.3 = bf16[256,4096]{1,0:T(8,128)(2,1)} custom-call(s32[8,16]{1,0:T(8,128)S(1)} %get-tuple-element.74.tab_j, s32[8,16]{1,0:T(8,128)S(1)} %get-tuple-element.75.tab_m, s32[3]{0:T(128)S(1)} %pad_add_fusion.1.meta, bf16[2,12,128,128]{3,2,1,0:T(8,128)(2,1)S(1)} %add.188.refs_0_, bf16[2,12,128,128]{3,2,1,0:T(8,128)(2,1)S(1)} %collective-permute-done.41.refs_1_, ...), custom_call_target="tpu_custom_call" | custom-call | flops 4294967296 | bytes 12582912 | tf_op jit(solution)/shard_map/decode/pallas_call | solution.py:312
  (213 shorter events, 127.3 us)
Async XLA Ops:
  5.7 21.7 %all-to-all-start = ((bf16[8,2,128,128]{3,2,1,0:T(8,128)(2,1)}), bf16[8,2,128,128]{3,2,1,0:T(8,128)(2,1)S(1)}, u32[]{:S(2)}, u32[]{:S(2)}) async-start(bf16[8,2,128,128]{3,2,1,0:T(8,128)(2,1)} %get-tuple-element.35), calls=%async_computation | async-start | bytes 1048576 | tf_op jit(solution)/shard_map/all_to_all | solution.py:435
  27.3 19.7 %all-to-all-start.1 = ((bf16[8,2,128,128]{3,2,1,0:T(8,128)(2,1)}), bf16[8,2,128,128]{3,2,1,0:T(8,128)(2,1)S(1)}, u32[]{:S(2)}, u32[]{:S(2)}) async-start(bf16[8,2,128,128]{3,2,1,0:T(8,128)(2,1)} %get-tuple-element.41), calls=%async_computation.1 | async-start | bytes 1048576 | tf_op jit(solution)/shard_map/all_to_all | solution.py:435
  31.1 19.9 %collective-permute-start.3 = (bf16[8,2,128,128]{3,2,1,0:T(8,128)(2,1)S(1)}, bf16[8,2,128,128]{3,2,1,0:T(8,128)(2,1)S(1)}, u32[]{:S(2)}, u32[]{:S(2)}) collective-permute-start(bf16[8,2,128,128]{3,2,1,0:T(8,128)(2,1)S(1)} %all-to-all-done.refs_1_.refs_2_.refs_14_), channel_id=1, source_target_pairs={{0,16},{16,0},{1,17},{17,1},{2,18},{18,2},{3,19},{19,3},{4,20},{20... | collective-permute-start | bytes 1572872 | tf_op jit(solution)/shard_map/ppermute | solution.py:447
  32.7 31.7 %collective-permute-start.1 = (bf16[8,2,128,128]{3,2,1,0:T(8,128)(2,1)S(1)}, bf16[8,2,128,128]{3,2,1,0:T(8,128)(2,1)S(1)}, u32[]{:S(2)}, u32[]{:S(2)}) collective-permute-start(bf16[8,2,128,128]{3,2,1,0:T(8,128)(2,1)S(1)} %all-to-all-done.refs_1_.refs_2_.refs_14_), channel_id=1, source_target_pairs={{0,2},{2,0},{1,3},{3,1},{4,6},{6,4},{5,7},{7,5},{8,10},{10,8},{9,1... | collective-permute-start | bytes 1572872 | tf_op jit(solution)/shard_map/ppermute | solution.py:446
  51.0 22.7 %collective-permute-start.5 = (bf16[8,2,128,128]{3,2,1,0:T(8,128)(2,1)S(1)}, bf16[8,2,128,128]{3,2,1,0:T(8,128)(2,1)S(1)}, u32[]{:S(2)}, u32[]{:S(2)}) collective-permute-start(bf16[8,2,128,128]{3,2,1,0:T(8,128)(2,1)S(1)} %collective-permute-done.3.refs_5_.refs_6_.refs_18_), channel_id=1, source_target_pairs={{0,2},{2,0},{1,3},{3,1},{4,6},{6,4},{5,7},{7,5},{8,10},{10,8},{9,1... | collective-permute-start | bytes 1572872 | tf_op jit(solution)/shard_map/ppermute | solution.py:446
  89.9 25.6 %collective-permute-start = (bf16[256,2048]{1,0:T(8,128)(2,1)S(1)}, bf16[256,2048]{1,0:T(8,128)(2,1)S(1)}, u32[]{:S(2)}, u32[]{:S(2)}) collective-permute-start(bf16[256,2048]{1,0:T(8,128)(2,1)S(1)} %copy-done.13), channel_id=1, source_target_pairs={{0,2},{2,0},{1,3},{3,1},{4,6},{6,4},{5,7},{7,5},{8,10},{10,8},{9,1... | collective-permute-start | bytes 3145736 | tf_op jit(solution)/shard_map/ppermute | solution.py:470
  95.4 20.0 %collective-permute-start.7 = (bf16[2,12,128,128]{3,2,1,0:T(8,128)(2,1)S(1)}, bf16[2,12,128,128]{3,2,1,0:T(8,128)(2,1)S(1)}, u32[]{:S(2)}, u32[]{:S(2)}) collective-permute-start(bf16[2,12,128,128]{3,2,1,0:T(8,128)(2,1)S(1)} %get-tuple-element.43.refs_0_), channel_id=1, source_target_pairs={{0,1},{1,0},{2,3},{3,2},{4,5},{5,4},{6,7},{7,6},{8,9},{9,8},{10,11... | collective-permute-start | bytes 2359304 | tf_op jit(solution)/shard_map/ppermute | solution.py:341
  95.8 19.6 %collective-permute-start.11 = (bf16[2,12,128,128]{3,2,1,0:T(8,128)(2,1)S(1)}, bf16[2,12,128,128]{3,2,1,0:T(8,128)(2,1)S(1)}, u32[]{:S(2)}, u32[]{:S(2)}) collective-permute-start(bf16[2,12,128,128]{3,2,1,0:T(8,128)(2,1)S(1)} %add.174), channel_id=1, source_target_pairs={{0,4},{4,8},{9,5},{13,9},{2,6},{6,10},{11,7},{15,11},{16,20},{20,2... | collective-permute-start | bytes 2359304 | tf_op jit(solution)/shard_map/ppermute | solution.py:370
  145.8 19.0 %collective-permute-start.26 = (bf16[2,12,128,128]{3,2,1,0:T(8,128)(2,1)S(1)}, bf16[2,12,128,128]{3,2,1,0:T(8,128)(2,1)S(1)}, u32[]{:S(2)}, u32[]{:S(2)}) collective-permute-start(bf16[2,12,128,128]{3,2,1,0:T(8,128)(2,1)S(1)} %add.183.refs_0_), channel_id=1, source_target_pairs={{0,4},{4,8},{8,12},{5,1},{9,5},{13,9},{2,6},{6,10},{10,14},{7,3},{... | collective-permute-start | bytes 2359304 | tf_op jit(solution)/shard_map/ppermute | solution.py:370
  171.8 20.3 %collective-permute-start.32 = (bf16[2,12,128,128]{3,2,1,0:T(8,128)(2,1)S(1)}, bf16[2,12,128,128]{3,2,1,0:T(8,128)(2,1)S(1)}, u32[]{:S(2)}, u32[]{:S(2)}) collective-permute-start(bf16[2,12,128,128]{3,2,1,0:T(8,128)(2,1)S(1)} %collective-permute-done.26.refs_2_.refs_1_), channel_id=1, source_target_pairs={{0,1},{1,0},{2,3},{3,2},{4,5},{5,4},{6,7},{7,6},{8,9},{9,8},{10,11... | collective-permute-start | bytes 2359304 | tf_op jit(solution)/shard_map/ppermute | solution.py:341
  172.7 19.5 %collective-permute-start.36 = (bf16[2,12,128,128]{3,2,1,0:T(8,128)(2,1)S(1)}, bf16[2,12,128,128]{3,2,1,0:T(8,128)(2,1)S(1)}, u32[]{:S(2)}, u32[]{:S(2)}) collective-permute-start(bf16[2,12,128,128]{3,2,1,0:T(8,128)(2,1)S(1)} %collective-permute-done.35.refs_9_.refs_3_), channel_id=1, source_target_pairs={{8,12},{5,1},{10,14},{7,3},{24,28},{21,17},{26,30},{23,19}} | collective-permute-start | bytes 2359304 | tf_op jit(solution)/shard_map/ppermute | solution.py:370
  180.9 19.9 %collective-permute-start.50 = (bf16[2,12,128,128]{3,2,1,0:T(8,128)(2,1)S(1)}, bf16[2,12,128,128]{3,2,1,0:T(8,128)(2,1)S(1)}, u32[]{:S(2)}, u32[]{:S(2)}) collective-permute-start(bf16[2,12,128,128]{3,2,1,0:T(8,128)(2,1)S(1)} %add.189), channel_id=1, source_target_pairs={{0,4},{4,8},{9,5},{13,9},{2,6},{6,10},{11,7},{15,11},{16,20},{20,2... | collective-permute-start | bytes 2359304 | tf_op jit(solution)/shard_map/ppermute | solution.py:370
  185.8 17.4 %collective-permute-start.29 = (bf16[2,12,128,128]{3,2,1,0:T(8,128)(2,1)S(1)}, bf16[2,12,128,128]{3,2,1,0:T(8,128)(2,1)S(1)}, u32[]{:S(2)}, u32[]{:S(2)}) collective-permute-start(bf16[2,12,128,128]{3,2,1,0:T(8,128)(2,1)S(1)} %add.185), channel_id=1, source_target_pairs={{0,4},{4,8},{9,5},{13,9},{2,6},{6,10},{11,7},{15,11},{16,20},{20,2... | collective-permute-start | bytes 2359304 | tf_op jit(solution)/shard_map/ppermute | solution.py:370
  192.1 17.9 %collective-permute-start.38 = (bf16[2,12,128,128]{3,2,1,0:T(8,128)(2,1)S(1)}, bf16[2,12,128,128]{3,2,1,0:T(8,128)(2,1)S(1)}, u32[]{:S(2)}, u32[]{:S(2)}) collective-permute-start(bf16[2,12,128,128]{3,2,1,0:T(8,128)(2,1)S(1)} %collective-permute-done.35.refs_9_.refs_3_), channel_id=1, source_target_pairs={{0,1},{1,0},{2,3},{3,2},{4,5},{5,4},{6,7},{7,6},{8,9},{9,8},{10,11... | collective-permute-start | bytes 2359304 | tf_op jit(solution)/shard_map/ppermute | solution.py:341
  192.2 24.5 %collective-permute-start.33 = (bf16[2,12,128,128]{3,2,1,0:T(8,128)(2,1)S(1)}, bf16[2,12,128,128]{3,2,1,0:T(8,128)(2,1)S(1)}, u32[]{:S(2)}, u32[]{:S(2)}) collective-permute-start(bf16[2,12,128,128]{3,2,1,0:T(8,128)(2,1)S(1)} %collective-permute-done.28.refs_3_.refs_2_), channel_id=1, source_target_pairs={{0,1},{1,0},{2,3},{3,2},{4,5},{5,4},{6,7},{7,6},{8,9},{9,8},{10,11... | collective-permute-start | bytes 2359304 | tf_op jit(solution)/shard_map/ppermute | solution.py:341
  192.7 24.0 %collective-permute-start.39 = (bf16[2,12,128,128]{3,2,1,0:T(8,128)(2,1)S(1)}, bf16[2,12,128,128]{3,2,1,0:T(8,128)(2,1)S(1)}, u32[]{:S(2)}, u32[]{:S(2)}) collective-permute-start(bf16[2,12,128,128]{3,2,1,0:T(8,128)(2,1)S(1)} %collective-permute-done.36.refs_10_.refs_3_), channel_id=1, source_target_pairs={{0,1},{1,0},{2,3},{3,2},{4,5},{5,4},{6,7},{7,6},{8,9},{9,8},{10,11... | collective-permute-start | bytes 2359304 | tf_op jit(solution)/shard_map/ppermute | solution.py:341
  203.2 18.6 %collective-permute-start.51 = (bf16[2,12,128,128]{3,2,1,0:T(8,128)(2,1)S(1)}, bf16[2,12,128,128]{3,2,1,0:T(8,128)(2,1)S(1)}, u32[]{:S(2)}, u32[]{:S(2)}) collective-permute-start(bf16[2,12,128,128]{3,2,1,0:T(8,128)(2,1)S(1)} %add.190), channel_id=1, source_target_pairs={{0,4},{4,8},{8,12},{5,1},{9,5},{13,9},{2,6},{6,10},{10,14},{7,3},{... | collective-permute-start | bytes 2359304 | tf_op jit(solution)/shard_map/ppermute | solution.py:370
  227.8 25.6 %collective-permute-start.54 = (bf16[256,2048]{1,0:T(8,128)(2,1)S(1)}, bf16[256,2048]{1,0:T(8,128)(2,1)S(1)}, u32[]{:S(2)}, u32[]{:S(2)}) collective-permute-start(bf16[256,2048]{1,0:T(8,128)(2,1)S(1)} %get-tuple-element.59), channel_id=1, source_target_pairs={{0,2},{2,0},{1,3},{3,1},{4,6},{6,4},{5,7},{7,5},{8,10},{10,8},{9,1... | collective-permute-start | bytes 3145736 | tf_op jit(solution)/shard_map/ppermute | solution.py:470
  229.6 23.7 %collective-permute-start.53 = (bf16[2,12,128,128]{3,2,1,0:T(8,128)(2,1)S(1)}, bf16[2,12,128,128]{3,2,1,0:T(8,128)(2,1)S(1)}, u32[]{:S(2)}, u32[]{:S(2)}) collective-permute-start(bf16[2,12,128,128]{3,2,1,0:T(8,128)(2,1)S(1)} %add.192.refs_7_), channel_id=1, source_target_pairs={{0,4},{4,8},{8,12},{5,1},{9,5},{13,9},{2,6},{6,10},{10,14},{7,3},{... | collective-permute-start | bytes 2359304 | tf_op jit(solution)/shard_map/ppermute | solution.py:370
  234.4 19.7 %collective-permute-start.41 = (bf16[2,12,128,128]{3,2,1,0:T(8,128)(2,1)S(1)}, bf16[2,12,128,128]{3,2,1,0:T(8,128)(2,1)S(1)}, u32[]{:S(2)}, u32[]{:S(2)}) collective-permute-start(bf16[2,12,128,128]{3,2,1,0:T(8,128)(2,1)S(1)} %add.188.refs_0_), channel_id=1, source_target_pairs={{0,4},{4,8},{8,12},{5,1},{9,5},{13,9},{2,6},{6,10},{10,14},{7,3},{... | collective-permute-start | bytes 2359304 | tf_op jit(solution)/shard_map/ppermute | solution.py:370
  266.9 36.2 %collective-permute-start.44 = (bf16[2,12,128,128]{3,2,1,0:T(8,128)(2,1)S(1)}, bf16[2,12,128,128]{3,2,1,0:T(8,128)(2,1)S(1)}, u32[]{:S(2)}, u32[]{:S(2)}) collective-permute-start(bf16[2,12,128,128]{3,2,1,0:T(8,128)(2,1)S(1)} %collective-permute-done.41.refs_1_), channel_id=1, source_target_pairs={{0,1},{1,0},{2,3},{3,2},{4,5},{5,4},{6,7},{7,6},{8,9},{9,8},{10,11... | collective-permute-start | bytes 2359304 | tf_op jit(solution)/shard_map/ppermute | solution.py:341
  267.0 36.6 %collective-permute-start.43 = (bf16[2,12,128,128]{3,2,1,0:T(8,128)(2,1)S(1)}, bf16[2,12,128,128]{3,2,1,0:T(8,128)(2,1)S(1)}, u32[]{:S(2)}, u32[]{:S(2)}) collective-permute-start(bf16[2,12,128,128]{3,2,1,0:T(8,128)(2,1)S(1)} %collective-permute-done.42.refs_2_), channel_id=1, source_target_pairs={{8,12},{5,1},{10,14},{7,3},{24,28},{21,17},{26,30},{23,19}} | collective-permute-start | bytes 2359304 | tf_op jit(solution)/shard_map/ppermute | solution.py:370
  267.7 36.0 %collective-permute-start.58 = (bf16[2,12,128,128]{3,2,1,0:T(8,128)(2,1)S(1)}, bf16[2,12,128,128]{3,2,1,0:T(8,128)(2,1)S(1)}, u32[]{:S(2)}, u32[]{:S(2)}) collective-permute-start(bf16[2,12,128,128]{3,2,1,0:T(8,128)(2,1)S(1)} %collective-permute-done.55.refs_9_), channel_id=1, source_target_pairs={{8,12},{5,1},{10,14},{7,3},{24,28},{21,17},{26,30},{23,19}} | collective-permute-start | bytes 2359304 | tf_op jit(solution)/shard_map/ppermute | solution.py:370
  282.3 20.7 %collective-permute-start.63 = (f32[16,739]{1,0:T(8,128)S(1)}, f32[16,739]{1,0:T(8,128)S(1)}, u32[]{:S(2)}, u32[]{:S(2)}) collective-permute-start(f32[16,739]{1,0:T(8,128)S(1)} %add.136), channel_id=1, source_target_pairs={{0,8},{4,12},{8,0},{12,4},{1,9},{5,13},{9,1},{13,5},{2,10},{6,14},... | collective-permute-start | bytes 141896 | tf_op jit(solution)/shard_map/ppermute | solution.py:387
  (61 other events, 718.9 us)

commit v4 on v3

--- a/solution.py
+++ b/solution.py
@@ -521,14 +521,14 @@
                         behind = [] if grad else [passes[0]["out"][0]]
                         half = add([st["sums", 0], st["now"]], behind)
                         st["mesh"] = st["now"] = add([half, swap_sub(half)], [])
-                    if not grad and t > 1 and h == chunks - 1:
+                    if not grad and t == n - 1 and h == chunks - 1:
                         if t == n - 1:
                             sums = backward(
                                 offs, grads, normed, slope, inv, mid, x,
                                 frozen_output_weight, adapter_up_weight,
                             )
-                            sums = add_all(jnp.concatenate(sums, axis=1), ("sub", "fsdp"))
-                        done = [sums] if t == n - 1 else grads
+                            sums = add_all(jnp.concatenate(sums, axis=1), ("sub", "fsdp", "lat"))
+                        done = [sums]
                         st["now"], *_ = lax.optimization_barrier((st["now"], *done))
                     st["now"] = st["came", t] = spread_step(t, st["now"])
                     st["theirs", t] = swap_sub(st["now"])
@@ -548,7 +548,6 @@
                     offs = (((f - turns + nf) % nf) * chans).astype(jnp.int32)
     decoded = passes[1]["out"][0]
 
-    sums = add_all(sums, ("lat",))
     up_gradient, grad_down = sums[:, :width], sums[:, width:].T
     return (decoded.reshape(1, 1, chans, grid_rows), grad_down, up_gradient)
 

time: 316 us -> 312 us (0.987)
    ppermute x4, starting transfers between devices: 32.3 us -> 9.62 us  [add_all(): lax.ppermute(value, axis, [(i, i ^ step) for i in range(size)])]
    ppermute x28, starting transfers between devices: 13.1 us -> 32.3 us  [swap_sub(): return lax.ppermute(a, 'sub', [(i, (i + 1) % ns) for i in range(ns)])]
    ppermute x24, waiting for transfers between devices: 38.7 us -> 49.6 us  [along(): return lax.ppermute(value, ('lat', 'sub'), pairs)]
    ppermute x2, waiting for transfers between devices: 21.3 us -> 12.3 us  [body(): lax.ppermute(v, 'fsdp', [(i, (i + r) % nf) for i in range(nf)])]
where the time goes in v4:
time: 312 us; the launch traced here: 311 us
  starting transfers between devices  137 us (44%)
  waiting for transfers between devices  97.4 us (31%)
  Pallas kernels  49.5 us (16%)
  blocking collectives  12.9 us (4%)
  local copies, waits for them, and re-layouts  9.98 us (3%)
    ppermute x24, starting transfers between devices, along(): return lax.ppermute(value, ('lat', 'sub'), pairs)  74.7 us
    ppermute x24, waiting for transfers between devices, along(): return lax.ppermute(value, ('lat', 'sub'), pairs)  49.6 us
    ppermute x28, starting transfers between devices, swap_sub(): return lax.ppermute(a, 'sub', [(i, (i + 1) % ns) for i in range(ns)])  32.3 us
    ppermute x3, waiting for transfers between devices, body(): over_x = lambda v: lax.ppermute(v, 'fsdp', flip)  21.2 us
    pallas_call x8, Pallas kernels, encode(): pl.pallas_call(functools.partial(encode_kernel, panels=panels, weights=le...  16.9 us
    all_gather x1, blocking collectives, body(): both = lax.all_gather(pattern, ('lat', 'sub'), tiled=True)  12.9 us
    ppermute x2, waiting for transfers between devices, body(): lax.ppermute(v, 'fsdp', [(i, (i + r) % nf) for i in range(nf)])  12.3 us
    pallas_call x2, Pallas kernels, decode(): pl.pallas_call(functools.partial(decode_kernel, n=n, ns=ns, weights=len(w...  11.6 us
  transfers between devices with their start and end apart: 66, of which 23 were waited for; matrix products, arithmetic and copies ran while one was open for 1% of the time, Pallas kernels for 13%

profile of v4, /device:TPU:0, one launch (start us, length us, event | category | flops | bytes accessed | tf_op | source)
XLA Modules:
  0.0 311.4 jit_solution(579523228311134073)
XLA Ops:
  5.7 6.3 %all-to-all-start = ((bf16[8,2,128,128]{3,2,1,0:T(8,128)(2,1)}), bf16[8,2,128,128]{3,2,1,0:T(8,128)(2,1)S(1)}, u32[]{:S(2)}, u32[]{:S(2)}) async-start(bf16[8,2,128,128]{3,2,1,0:T(8,128)(2,1)} %get-tuple-element.34), calls=%async_computation | async-start | bytes 1048576 | tf_op jit(solution)/shard_map/all_to_all | solution.py:435
  12.2 6.7 %forward.1 = (bf16[256,2048]{1,0:T(8,128)(2,1)S(1)}, bf16[256,2048]{1,0:T(8,128)(2,1)S(1)}, f32[512,2048]{1,0:T(8,128)S(1)}, f32[512,2048]{1,0:T(8,128)S(1)}, f3...) custom-call(s32[1]{0:T(128)} %bitcast.9.meta, bf16[227,2048]{1,0:T(8,128)(2,1)S(1)} %bitcast.21, ...), custom_call_target="tpu_custom_call" | custom-call | flops 1549795328 | bytes 12582912 | tf_op jit(solution)/shard_map/forward/pallas_call | solution.py:90
  34.2 12.9 %all_gather.3 = s32[8,2,96]{2,1,0:T(2,128)S(1)} all-gather(s32[1,2,96]{2,1,0:T(2,128)S(1)} %add_bitcast_fusion), channel_id=1, replica_groups=mesh['parts'=2,'lat'=4,'fsdp'=2,'sub'=2] {'lat','sub'}, dimensions={0}, use_global_device_ids=true | all-gather | bytes 6912 | tf_op jit(solution)/shard_map/all_gather | solution.py:459
  51.6 11.8 %collective-permute-done.2.refs_4_.refs_5_.refs_17_ = bf16[8,2,128,128]{3,2,1,0:T(8,128)(2,1)S(1)} collective-permute-done((bf16[8,2,128,128]{3,2,1,0:T(8,128)(2,1)S(1)}, bf16[8,2,128,128]{3,2,1,0:T(8,128)(2,1)S(1)}, u32[]{:S(2)}, u32[]{:S(2)}) %collective-permute-start.2) | collective-permute-done | bytes 524320 | tf_op jit(solution)/shard_map/ppermute | solution.py:446
  64.4 9.3 %collective-permute-done.5.refs_7_.refs_8_.refs_20_ = bf16[8,2,128,128]{3,2,1,0:T(8,128)(2,1)S(1)} collective-permute-done((bf16[8,2,128,128]{3,2,1,0:T(8,128)(2,1)S(1)}, bf16[8,2,128,128]{3,2,1,0:T(8,128)(2,1)S(1)}, u32[]{:S(2)}, u32[]{:S(2)}) %collective-permute-start.5) | collective-permute-done | bytes 524320 | tf_op jit(solution)/shard_map/ppermute | solution.py:446
  108.7 6.8 %collective-permute-done.refs_3_.refs_1_ = bf16[256,2048]{1,0:T(8,128)(2,1)S(1)} collective-permute-done((bf16[256,2048]{1,0:T(8,128)(2,1)S(1)}, bf16[256,2048]{1,0:T(8,128)(2,1)S(1)}, u32[]{:S(2)}, u32[]{:S(2)}) %collective-permute-start) | collective-permute-done | bytes 1048608 | tf_op jit(solution)/shard_map/ppermute | solution.py:470
  121.1 4.4 %collective-permute-start.24 = (bf16[2,12,128,128]{3,2,1,0:T(8,128)(2,1)S(1)}, bf16[2,12,128,128]{3,2,1,0:T(8,128)(2,1)S(1)}, u32[]{:S(2)}, u32[]{:S(2)}) collective-permute-start(bf16[2,12,128,128]{3,2,1,0:T(8,128)(2,1)S(1)} %add.181), channel_id=1, source_target_pairs={{0,4},{4,8},{8,12},{5,1},{9,5},{13,9},{2,6},{6,10},{10,14},{7,3},{... | collective-permute-start | bytes 2359304 | tf_op jit(solution)/shard_map/ppermute | solution.py:370
  129.5 8.1 %collective-permute-done.24.refs_1_ = bf16[2,12,128,128]{3,2,1,0:T(8,128)(2,1)S(1)} collective-permute-done((bf16[2,12,128,128]{3,2,1,0:T(8,128)(2,1)S(1)}, bf16[2,12,128,128]{3,2,1,0:T(8,128)(2,1)S(1)}, u32[]{:S(2)}, u32[]{:S(2)}) %collective-permute-start.24) | collective-permute-done | bytes 786464 | tf_op jit(solution)/shard_map/ppermute | solution.py:370
  155.8 6.7 %collective-permute-start.49 = (bf16[2,12,128,128]{3,2,1,0:T(8,128)(2,1)S(1)}, bf16[2,12,128,128]{3,2,1,0:T(8,128)(2,1)S(1)}, u32[]{:S(2)}, u32[]{:S(2)}) collective-permute-start(bf16[2,12,128,128]{3,2,1,0:T(8,128)(2,1)S(1)} %add.178.refs_10_), channel_id=1, source_target_pairs={{0,4},{13,9},{2,6},{15,11},{16,20},{29,25},{18,22},{31,27}} | collective-permute-start | bytes 2359304 | tf_op jit(solution)/shard_map/ppermute | solution.py:370
  165.9 4.9 %collective-permute-start.27 = (bf16[2,12,128,128]{3,2,1,0:T(8,128)(2,1)S(1)}, bf16[2,12,128,128]{3,2,1,0:T(8,128)(2,1)S(1)}, u32[]{:S(2)}, u32[]{:S(2)}) collective-permute-start(bf16[2,12,128,128]{3,2,1,0:T(8,128)(2,1)S(1)} %add.184), channel_id=1, source_target_pairs={{0,4},{13,9},{2,6},{15,11},{16,20},{29,25},{18,22},{31,27}} | collective-permute-start | bytes 2359304 | tf_op jit(solution)/shard_map/ppermute | solution.py:370
  173.4 6.8 %collective-permute-done.27.refs_2_ = bf16[2,12,128,128]{3,2,1,0:T(8,128)(2,1)S(1)} collective-permute-done((bf16[2,12,128,128]{3,2,1,0:T(8,128)(2,1)S(1)}, bf16[2,12,128,128]{3,2,1,0:T(8,128)(2,1)S(1)}, u32[]{:S(2)}, u32[]{:S(2)}) %collective-permute-start.27) | collective-permute-done | bytes 786464 | tf_op jit(solution)/shard_map/ppermute | solution.py:370
  185.8 6.3 %collective-permute-start.29 = (bf16[2,12,128,128]{3,2,1,0:T(8,128)(2,1)S(1)}, bf16[2,12,128,128]{3,2,1,0:T(8,128)(2,1)S(1)}, u32[]{:S(2)}, u32[]{:S(2)}) collective-permute-start(bf16[2,12,128,128]{3,2,1,0:T(8,128)(2,1)S(1)} %add.185), channel_id=1, source_target_pairs={{0,4},{4,8},{9,5},{13,9},{2,6},{6,10},{11,7},{15,11},{16,20},{20,2... | collective-permute-start | bytes 2359304 | tf_op jit(solution)/shard_map/ppermute | solution.py:370
  192.7 8.2 %collective-permute-start.39 = (bf16[2,12,128,128]{3,2,1,0:T(8,128)(2,1)S(1)}, bf16[2,12,128,128]{3,2,1,0:T(8,128)(2,1)S(1)}, u32[]{:S(2)}, u32[]{:S(2)}) collective-permute-start(bf16[2,12,128,128]{3,2,1,0:T(8,128)(2,1)S(1)} %collective-permute-done.36.refs_10_.refs_3_), channel_id=1, source_target_pairs={{0,1},{1,0},{2,3},{3,2},{4,5},{5,4},{6,7},{7,6},{8,9},{9,8},{10,11... | collective-permute-start | bytes 2359304 | tf_op jit(solution)/shard_map/ppermute | solution.py:341
  203.3 6.3 %collective-permute-start.51 = (bf16[2,12,128,128]{3,2,1,0:T(8,128)(2,1)S(1)}, bf16[2,12,128,128]{3,2,1,0:T(8,128)(2,1)S(1)}, u32[]{:S(2)}, u32[]{:S(2)}) collective-permute-start(bf16[2,12,128,128]{3,2,1,0:T(8,128)(2,1)S(1)} %add.190), channel_id=1, source_target_pairs={{0,4},{4,8},{8,12},{5,1},{9,5},{13,9},{2,6},{6,10},{10,14},{7,3},{... | collective-permute-start | bytes 2359304 | tf_op jit(solution)/shard_map/ppermute | solution.py:370
  216.7 5.1 %decode.2 = (bf16[256,2048]{1,0:T(8,128)(2,1)S(1)}, bf16[256,2048]{1,0:T(8,128)(2,1)S(1)}) custom-call(s32[8,16]{1,0:T(8,128)S(1)} %get-tuple-element.72.tab_j, s32[8,16]{1,0:T(8,128)S(1)} %get-tuple-element.73.tab_m, s32[3]{0:T(128)S(1)} %pad_add_fusion.1.meta, bf16[2,12,128,128]{3,2,1,0:T(8,128)(2,1)S(1)} %add.183.refs_0_, ...), custom_call_target="tpu_custom_call" | custom-call | flops 4294967296 | bytes 12582912 | tf_op jit(solution)/shard_map/decode/pallas_call | solution.py:312
  222.3 5.2 %collective-permute-done.31.refs_1_ = bf16[2,12,128,128]{3,2,1,0:T(8,128)(2,1)S(1)} collective-permute-done((bf16[2,12,128,128]{3,2,1,0:T(8,128)(2,1)S(1)}, bf16[2,12,128,128]{3,2,1,0:T(8,128)(2,1)S(1)}, u32[]{:S(2)}, u32[]{:S(2)}) %collective-permute-start.31) | collective-permute-done | bytes 786464 | tf_op jit(solution)/shard_map/ppermute | solution.py:370
  228.1 4.7 %collective-permute-start.53 = (bf16[2,12,128,128]{3,2,1,0:T(8,128)(2,1)S(1)}, bf16[2,12,128,128]{3,2,1,0:T(8,128)(2,1)S(1)}, u32[]{:S(2)}, u32[]{:S(2)}) collective-permute-start(bf16[2,12,128,128]{3,2,1,0:T(8,128)(2,1)S(1)} %add.192.refs_7_), channel_id=1, source_target_pairs={{0,4},{4,8},{8,12},{5,1},{9,5},{13,9},{2,6},{6,10},{10,14},{7,3},{... | collective-permute-start | bytes 2359304 | tf_op jit(solution)/shard_map/ppermute | solution.py:370
  243.0 7.7 %collective-permute-done.41.refs_1_ = bf16[2,12,128,128]{3,2,1,0:T(8,128)(2,1)S(1)} collective-permute-done((bf16[2,12,128,128]{3,2,1,0:T(8,128)(2,1)S(1)}, bf16[2,12,128,128]{3,2,1,0:T(8,128)(2,1)S(1)}, u32[]{:S(2)}, u32[]{:S(2)}) %collective-permute-start.41) | collective-permute-done | bytes 786464 | tf_op jit(solution)/shard_map/ppermute | solution.py:370
  251.4 5.5 %collective-permute-done.55.refs_1_ = bf16[256,2048]{1,0:T(8,128)(2,1)S(1)} collective-permute-done((bf16[256,2048]{1,0:T(8,128)(2,1)S(1)}, bf16[256,2048]{1,0:T(8,128)(2,1)S(1)}, u32[]{:S(2)}, u32[]{:S(2)}) %collective-permute-start.55) | collective-permute-done | bytes 1048608 | tf_op jit(solution)/shard_map/ppermute | solution.py:470
  257.0 6.1 %backward.1 = (f32[16,512]{1,0:T(8,128)S(1)}, f32[16,227]{1,0:T(8,128)S(1)}) custom-call(s32[2]{0:T(128)S(1)} %fusion.6.offs, bf16[256,2048]{1,0:T(8,128)(2,1)S(1)} %get-tuple-element.55.refs_2_.refs_0_, bf16[256,2048]{1,0:T(8,128)(2,1)S(1)} %collective-permute-done.55.refs_1_, f32[512,2048]{1,0:T(8,128)S(1)} %copy-done.3, f32[512,2048]{1,0:T(8,128)S(1)} %copy-done.5, ...), custom_call_target="tpu_custom_call" | custom-call | flops 1073741824 | bytes 10485760 | tf_op jit(solution)/shard_map/backward/pallas_call | solution.py:161
  274.1 4.5 %collective-permute-start.59 = (f32[16,739]{1,0:T(8,128)S(1)}, f32[16,739]{1,0:T(8,128)S(1)}, u32[]{:S(2)}, u32[]{:S(2)}) collective-permute-start(f32[16,739]{1,0:T(8,128)S(1)} %add.136), channel_id=1, source_target_pairs={{0,8},{4,12},{8,0},{12,4},{1,9},{5,13},{9,1},{13,5},{2,10},{6,14},... | collective-permute-start | bytes 141896 | tf_op jit(solution)/shard_map/ppermute | solution.py:387
  284.9 9.6 %collective-permute-start.46 = (bf16[2,12,128,128]{3,2,1,0:T(8,128)(2,1)S(1)}, bf16[2,12,128,128]{3,2,1,0:T(8,128)(2,1)S(1)}, u32[]{:S(2)}, u32[]{:S(2)}) collective-permute-start(bf16[2,12,128,128]{3,2,1,0:T(8,128)(2,1)S(1)} %collective-permute-done.43.refs_3_), channel_id=1, source_target_pairs={{0,1},{1,0},{2,3},{3,2},{4,5},{5,4},{6,7},{7,6},{8,9},{9,8},{10,11... | collective-permute-start | bytes 2359304 | tf_op jit(solution)/shard_map/ppermute | solution.py:341
  294.5 8.4 %collective-permute-start.63 = (bf16[2,12,128,128]{3,2,1,0:T(8,128)(2,1)S(1)}, bf16[2,12,128,128]{3,2,1,0:T(8,128)(2,1)S(1)}, u32[]{:S(2)}, u32[]{:S(2)}) collective-permute-start(bf16[2,12,128,128]{3,2,1,0:T(8,128)(2,1)S(1)} %collective-permute-done.60.refs_10_), channel_id=1, source_target_pairs={{0,1},{1,0},{2,3},{3,2},{4,5},{5,4},{6,7},{7,6},{8,9},{9,8},{10,11... | collective-permute-start | bytes 2359304 | tf_op jit(solution)/shard_map/ppermute | solution.py:341
  304.8 6.4 %decode.3 = bf16[256,4096]{1,0:T(8,128)(2,1)} custom-call(s32[8,16]{1,0:T(8,128)S(1)} %get-tuple-element.72.tab_j, s32[8,16]{1,0:T(8,128)S(1)} %get-tuple-element.73.tab_m, s32[3]{0:T(128)S(1)} %pad_add_fusion.1.meta, bf16[2,12,128,128]{3,2,1,0:T(8,128)(2,1)S(1)} %add.188.refs_0_, bf16[2,12,128,128]{3,2,1,0:T(8,128)(2,1)S(1)} %collective-permute-done.41.refs_1_, ...), custom_call_target="tpu_custom_call" | custom-call | flops 4294967296 | bytes 12582912 | tf_op jit(solution)/shard_map/decode/pallas_call | solution.py:312
  (213 shorter events, 140.8 us)
Async XLA Ops:
  5.7 21.7 %all-to-all-start = ((bf16[8,2,128,128]{3,2,1,0:T(8,128)(2,1)}), bf16[8,2,128,128]{3,2,1,0:T(8,128)(2,1)S(1)}, u32[]{:S(2)}, u32[]{:S(2)}) async-start(bf16[8,2,128,128]{3,2,1,0:T(8,128)(2,1)} %get-tuple-element.34), calls=%async_computation | async-start | bytes 1048576 | tf_op jit(solution)/shard_map/all_to_all | solution.py:435
  27.3 19.7 %all-to-all-start.1 = ((bf16[8,2,128,128]{3,2,1,0:T(8,128)(2,1)}), bf16[8,2,128,128]{3,2,1,0:T(8,128)(2,1)S(1)}, u32[]{:S(2)}, u32[]{:S(2)}) async-start(bf16[8,2,128,128]{3,2,1,0:T(8,128)(2,1)} %get-tuple-element.40), calls=%async_computation.1 | async-start | bytes 1048576 | tf_op jit(solution)/shard_map/all_to_all | solution.py:435
  31.1 19.9 %collective-permute-start.3 = (bf16[8,2,128,128]{3,2,1,0:T(8,128)(2,1)S(1)}, bf16[8,2,128,128]{3,2,1,0:T(8,128)(2,1)S(1)}, u32[]{:S(2)}, u32[]{:S(2)}) collective-permute-start(bf16[8,2,128,128]{3,2,1,0:T(8,128)(2,1)S(1)} %all-to-all-done.refs_1_.refs_2_.refs_14_), channel_id=1, source_target_pairs={{0,16},{16,0},{1,17},{17,1},{2,18},{18,2},{3,19},{19,3},{4,20},{20... | collective-permute-start | bytes 1572872 | tf_op jit(solution)/shard_map/ppermute | solution.py:447
  32.7 31.7 %collective-permute-start.1 = (bf16[8,2,128,128]{3,2,1,0:T(8,128)(2,1)S(1)}, bf16[8,2,128,128]{3,2,1,0:T(8,128)(2,1)S(1)}, u32[]{:S(2)}, u32[]{:S(2)}) collective-permute-start(bf16[8,2,128,128]{3,2,1,0:T(8,128)(2,1)S(1)} %all-to-all-done.refs_1_.refs_2_.refs_14_), channel_id=1, source_target_pairs={{0,2},{2,0},{1,3},{3,1},{4,6},{6,4},{5,7},{7,5},{8,10},{10,8},{9,1... | collective-permute-start | bytes 1572872 | tf_op jit(solution)/shard_map/ppermute | solution.py:446
  51.0 22.7 %collective-permute-start.5 = (bf16[8,2,128,128]{3,2,1,0:T(8,128)(2,1)S(1)}, bf16[8,2,128,128]{3,2,1,0:T(8,128)(2,1)S(1)}, u32[]{:S(2)}, u32[]{:S(2)}) collective-permute-start(bf16[8,2,128,128]{3,2,1,0:T(8,128)(2,1)S(1)} %collective-permute-done.3.refs_5_.refs_6_.refs_18_), channel_id=1, source_target_pairs={{0,2},{2,0},{1,3},{3,1},{4,6},{6,4},{5,7},{7,5},{8,10},{10,8},{9,1... | collective-permute-start | bytes 1572872 | tf_op jit(solution)/shard_map/ppermute | solution.py:446
  89.9 25.6 %collective-permute-start = (bf16[256,2048]{1,0:T(8,128)(2,1)S(1)}, bf16[256,2048]{1,0:T(8,128)(2,1)S(1)}, u32[]{:S(2)}, u32[]{:S(2)}) collective-permute-start(bf16[256,2048]{1,0:T(8,128)(2,1)S(1)} %copy-done.13), channel_id=1, source_target_pairs={{0,2},{2,0},{1,3},{3,1},{4,6},{6,4},{5,7},{7,5},{8,10},{10,8},{9,1... | collective-permute-start | bytes 3145736 | tf_op jit(solution)/shard_map/ppermute | solution.py:470
  95.4 20.0 %collective-permute-start.7 = (bf16[2,12,128,128]{3,2,1,0:T(8,128)(2,1)S(1)}, bf16[2,12,128,128]{3,2,1,0:T(8,128)(2,1)S(1)}, u32[]{:S(2)}, u32[]{:S(2)}) collective-permute-start(bf16[2,12,128,128]{3,2,1,0:T(8,128)(2,1)S(1)} %get-tuple-element.42.refs_0_), channel_id=1, source_target_pairs={{0,1},{1,0},{2,3},{3,2},{4,5},{5,4},{6,7},{7,6},{8,9},{9,8},{10,11... | collective-permute-start | bytes 2359304 | tf_op jit(solution)/shard_map/ppermute | solution.py:341
  95.8 19.6 %collective-permute-start.11 = (bf16[2,12,128,128]{3,2,1,0:T(8,128)(2,1)S(1)}, bf16[2,12,128,128]{3,2,1,0:T(8,128)(2,1)S(1)}, u32[]{:S(2)}, u32[]{:S(2)}) collective-permute-start(bf16[2,12,128,128]{3,2,1,0:T(8,128)(2,1)S(1)} %add.174), channel_id=1, source_target_pairs={{0,4},{4,8},{9,5},{13,9},{2,6},{6,10},{11,7},{15,11},{16,20},{20,2... | collective-permute-start | bytes 2359304 | tf_op jit(solution)/shard_map/ppermute | solution.py:370
  145.8 19.0 %collective-permute-start.26 = (bf16[2,12,128,128]{3,2,1,0:T(8,128)(2,1)S(1)}, bf16[2,12,128,128]{3,2,1,0:T(8,128)(2,1)S(1)}, u32[]{:S(2)}, u32[]{:S(2)}) collective-permute-start(bf16[2,12,128,128]{3,2,1,0:T(8,128)(2,1)S(1)} %add.183.refs_0_), channel_id=1, source_target_pairs={{0,4},{4,8},{8,12},{5,1},{9,5},{13,9},{2,6},{6,10},{10,14},{7,3},{... | collective-permute-start | bytes 2359304 | tf_op jit(solution)/shard_map/ppermute | solution.py:370
  171.8 20.3 %collective-permute-start.32 = (bf16[2,12,128,128]{3,2,1,0:T(8,128)(2,1)S(1)}, bf16[2,12,128,128]{3,2,1,0:T(8,128)(2,1)S(1)}, u32[]{:S(2)}, u32[]{:S(2)}) collective-permute-start(bf16[2,12,128,128]{3,2,1,0:T(8,128)(2,1)S(1)} %collective-permute-done.26.refs_2_.refs_1_), channel_id=1, source_target_pairs={{0,1},{1,0},{2,3},{3,2},{4,5},{5,4},{6,7},{7,6},{8,9},{9,8},{10,11... | collective-permute-start | bytes 2359304 | tf_op jit(solution)/shard_map/ppermute | solution.py:341
  172.7 19.5 %collective-permute-start.36 = (bf16[2,12,128,128]{3,2,1,0:T(8,128)(2,1)S(1)}, bf16[2,12,128,128]{3,2,1,0:T(8,128)(2,1)S(1)}, u32[]{:S(2)}, u32[]{:S(2)}) collective-permute-start(bf16[2,12,128,128]{3,2,1,0:T(8,128)(2,1)S(1)} %collective-permute-done.35.refs_9_.refs_3_), channel_id=1, source_target_pairs={{8,12},{5,1},{10,14},{7,3},{24,28},{21,17},{26,30},{23,19}} | collective-permute-start | bytes 2359304 | tf_op jit(solution)/shard_map/ppermute | solution.py:370
  180.9 20.0 %collective-permute-start.50 = (bf16[2,12,128,128]{3,2,1,0:T(8,128)(2,1)S(1)}, bf16[2,12,128,128]{3,2,1,0:T(8,128)(2,1)S(1)}, u32[]{:S(2)}, u32[]{:S(2)}) collective-permute-start(bf16[2,12,128,128]{3,2,1,0:T(8,128)(2,1)S(1)} %add.189), channel_id=1, source_target_pairs={{0,4},{4,8},{9,5},{13,9},{2,6},{6,10},{11,7},{15,11},{16,20},{20,2... | collective-permute-start | bytes 2359304 | tf_op jit(solution)/shard_map/ppermute | solution.py:370
  192.1 17.9 %collective-permute-start.38 = (bf16[2,12,128,128]{3,2,1,0:T(8,128)(2,1)S(1)}, bf16[2,12,128,128]{3,2,1,0:T(8,128)(2,1)S(1)}, u32[]{:S(2)}, u32[]{:S(2)}) collective-permute-start(bf16[2,12,128,128]{3,2,1,0:T(8,128)(2,1)S(1)} %collective-permute-done.35.refs_9_.refs_3_), channel_id=1, source_target_pairs={{0,1},{1,0},{2,3},{3,2},{4,5},{5,4},{6,7},{7,6},{8,9},{9,8},{10,11... | collective-permute-start | bytes 2359304 | tf_op jit(solution)/shard_map/ppermute | solution.py:341
  192.2 24.5 %collective-permute-start.33 = (bf16[2,12,128,128]{3,2,1,0:T(8,128)(2,1)S(1)}, bf16[2,12,128,128]{3,2,1,0:T(8,128)(2,1)S(1)}, u32[]{:S(2)}, u32[]{:S(2)}) collective-permute-start(bf16[2,12,128,128]{3,2,1,0:T(8,128)(2,1)S(1)} %collective-permute-done.28.refs_3_.refs_2_), channel_id=1, source_target_pairs={{0,1},{1,0},{2,3},{3,2},{4,5},{5,4},{6,7},{7,6},{8,9},{9,8},{10,11... | collective-permute-start | bytes 2359304 | tf_op jit(solution)/shard_map/ppermute | solution.py:341
  192.7 24.0 %collective-permute-start.39 = (bf16[2,12,128,128]{3,2,1,0:T(8,128)(2,1)S(1)}, bf16[2,12,128,128]{3,2,1,0:T(8,128)(2,1)S(1)}, u32[]{:S(2)}, u32[]{:S(2)}) collective-permute-start(bf16[2,12,128,128]{3,2,1,0:T(8,128)(2,1)S(1)} %collective-permute-done.36.refs_10_.refs_3_), channel_id=1, source_target_pairs={{0,1},{1,0},{2,3},{3,2},{4,5},{5,4},{6,7},{7,6},{8,9},{9,8},{10,11... | collective-permute-start | bytes 2359304 | tf_op jit(solution)/shard_map/ppermute | solution.py:341
  203.3 18.6 %collective-permute-start.51 = (bf16[2,12,128,128]{3,2,1,0:T(8,128)(2,1)S(1)}, bf16[2,12,128,128]{3,2,1,0:T(8,128)(2,1)S(1)}, u32[]{:S(2)}, u32[]{:S(2)}) collective-permute-start(bf16[2,12,128,128]{3,2,1,0:T(8,128)(2,1)S(1)} %add.190), channel_id=1, source_target_pairs={{0,4},{4,8},{8,12},{5,1},{9,5},{13,9},{2,6},{6,10},{10,14},{7,3},{... | collective-permute-start | bytes 2359304 | tf_op jit(solution)/shard_map/ppermute | solution.py:370
  233.2 17.5 %collective-permute-start.41 = (bf16[2,12,128,128]{3,2,1,0:T(8,128)(2,1)S(1)}, bf16[2,12,128,128]{3,2,1,0:T(8,128)(2,1)S(1)}, u32[]{:S(2)}, u32[]{:S(2)}) collective-permute-start(bf16[2,12,128,128]{3,2,1,0:T(8,128)(2,1)S(1)} %add.188.refs_0_), channel_id=1, source_target_pairs={{0,4},{4,8},{8,12},{5,1},{9,5},{13,9},{2,6},{6,10},{10,14},{7,3},{... | collective-permute-start | bytes 2359304 | tf_op jit(solution)/shard_map/ppermute | solution.py:370
  237.6 19.4 %collective-permute-start.55 = (bf16[256,2048]{1,0:T(8,128)(2,1)S(1)}, bf16[256,2048]{1,0:T(8,128)(2,1)S(1)}, u32[]{:S(2)}, u32[]{:S(2)}) collective-permute-start(bf16[256,2048]{1,0:T(8,128)(2,1)S(1)} %get-tuple-element.58), channel_id=1, source_target_pairs={{0,2},{2,0},{1,3},{3,1},{4,6},{6,4},{5,7},{7,5},{8,10},{10,8},{9,1... | collective-permute-start | bytes 3145736 | tf_op jit(solution)/shard_map/ppermute | solution.py:470
  242.3 39.0 %collective-permute-start.54 = (bf16[2,12,128,128]{3,2,1,0:T(8,128)(2,1)S(1)}, bf16[2,12,128,128]{3,2,1,0:T(8,128)(2,1)S(1)}, u32[]{:S(2)}, u32[]{:S(2)}) collective-permute-start(bf16[2,12,128,128]{3,2,1,0:T(8,128)(2,1)S(1)} %collective-permute-done.53.refs_8_), channel_id=1, source_target_pairs={{4,8},{8,12},{5,1},{9,5},{6,10},{10,14},{7,3},{11,7},{20,24},{24,2... | collective-permute-start | bytes 2359304 | tf_op jit(solution)/shard_map/ppermute | solution.py:370
  250.7 30.5 %collective-permute-start.42 = (bf16[2,12,128,128]{3,2,1,0:T(8,128)(2,1)S(1)}, bf16[2,12,128,128]{3,2,1,0:T(8,128)(2,1)S(1)}, u32[]{:S(2)}, u32[]{:S(2)}) collective-permute-start(bf16[2,12,128,128]{3,2,1,0:T(8,128)(2,1)S(1)} %collective-permute-done.41.refs_1_), channel_id=1, source_target_pairs={{4,8},{8,12},{5,1},{9,5},{6,10},{10,14},{7,3},{11,7},{20,24},{24,2... | collective-permute-start | bytes 2359304 | tf_op jit(solution)/shard_map/ppermute | solution.py:370
  282.7 21.4 %collective-permute-start.61 = (bf16[2,12,128,128]{3,2,1,0:T(8,128)(2,1)S(1)}, bf16[2,12,128,128]{3,2,1,0:T(8,128)(2,1)S(1)}, u32[]{:S(2)}, u32[]{:S(2)}) collective-permute-start(bf16[2,12,128,128]{3,2,1,0:T(8,128)(2,1)S(1)} %collective-permute-done.53.refs_8_), channel_id=1, source_target_pairs={{0,1},{1,0},{2,3},{3,2},{4,5},{5,4},{6,7},{7,6},{8,9},{9,8},{10,11... | collective-permute-start | bytes 2359304 | tf_op jit(solution)/shard_map/ppermute | solution.py:341
  284.4 19.7 %collective-permute-start.45 = (bf16[2,12,128,128]{3,2,1,0:T(8,128)(2,1)S(1)}, bf16[2,12,128,128]{3,2,1,0:T(8,128)(2,1)S(1)}, u32[]{:S(2)}, u32[]{:S(2)}) collective-permute-start(bf16[2,12,128,128]{3,2,1,0:T(8,128)(2,1)S(1)} %collective-permute-done.42.refs_2_), channel_id=1, source_target_pairs={{0,1},{1,0},{2,3},{3,2},{4,5},{5,4},{6,7},{7,6},{8,9},{9,8},{10,11... | collective-permute-start | bytes 2359304 | tf_op jit(solution)/shard_map/ppermute | solution.py:341
  284.5 19.6 %collective-permute-start.62 = (bf16[2,12,128,128]{3,2,1,0:T(8,128)(2,1)S(1)}, bf16[2,12,128,128]{3,2,1,0:T(8,128)(2,1)S(1)}, u32[]{:S(2)}, u32[]{:S(2)}) collective-permute-start(bf16[2,12,128,128]{3,2,1,0:T(8,128)(2,1)S(1)} %collective-permute-done.54.refs_9_), channel_id=1, source_target_pairs={{0,1},{1,0},{2,3},{3,2},{4,5},{5,4},{6,7},{7,6},{8,9},{9,8},{10,11... | collective-permute-start | bytes 2359304 | tf_op jit(solution)/shard_map/ppermute | solution.py:341
  284.9 19.2 %collective-permute-start.46 = (bf16[2,12,128,128]{3,2,1,0:T(8,128)(2,1)S(1)}, bf16[2,12,128,128]{3,2,1,0:T(8,128)(2,1)S(1)}, u32[]{:S(2)}, u32[]{:S(2)}) collective-permute-start(bf16[2,12,128,128]{3,2,1,0:T(8,128)(2,1)S(1)} %collective-permute-done.43.refs_3_), channel_id=1, source_target_pairs={{0,1},{1,0},{2,3},{3,2},{4,5},{5,4},{6,7},{7,6},{8,9},{9,8},{10,11... | collective-permute-start | bytes 2359304 | tf_op jit(solution)/shard_map/ppermute | solution.py:341
  (61 other events, 738.6 us)

commit v5 on v4

--- a/solution.py
+++ b/solution.py
@@ -445,8 +445,10 @@
         flip = [(0, 1), (1, 0)]
         over_x = lambda v: lax.ppermute(v, "fsdp", flip)
         over_y = lambda v: lax.ppermute(v, "parts", flip)
+        cut = cs // 4
+        corner = lambda a, b: (over_x(b[:, :cut]), over_y(a[:, cut:]))
         x1, y1, x2, y2 = over_x(first), over_y(first), over_x(second), over_y(second)
-        weights = [first, second, x1, x2, y1, y2, over_x(y1), over_y(x2)]
+        weights = [first, second, x1, x2, y1, y2, *corner(x1, y1), *corner(x2, y2)]
         half = jnp.arange(cs, dtype=jnp.int32)
         slot_ranks = jnp.concatenate([(r0 ^ k) * cs + half for k in range(4)])
     else:

time: 312 us -> 309 us (level)
  waiting for transfers between devices: 97.4 us -> 92.5 us
    ppermute x3 -> x4, waiting for transfers between devices: 21.2 us -> 8.4 us  [body(): over_x = lambda v: lax.ppermute(v, 'fsdp', flip)]
    ppermute x3 -> x4, waiting for transfers between devices: 1.8 us -> 9.84 us  [body(): over_y = lambda v: lax.ppermute(v, 'parts', flip)]
    unnamed x40 -> x38, local copies, waits for them, and re-layouts: 8.66 us -> 7.08 us
  transfers between devices with their start and end apart: 66 -> 68, of which waited for: 23 -> 23; matrix products, arithmetic and copies ran while one was open for 1% -> 1% of each run, Pallas kernels for 13% -> 13%
where the time goes in v5:
time: 309 us; the launch traced here: 308 us
  starting transfers between devices  140 us (45%)
  waiting for transfers between devices  92.5 us (30%)
  Pallas kernels  49.6 us (16%)
  blocking collectives  12.9 us (4%)
  local copies, waits for them, and re-layouts  8.47 us (3%)
    ppermute x24, starting transfers between devices, along(): return lax.ppermute(value, ('lat', 'sub'), pairs)  74.6 us
    ppermute x24, waiting for transfers between devices, along(): return lax.ppermute(value, ('lat', 'sub'), pairs)  49.5 us
    ppermute x28, starting transfers between devices, swap_sub(): return lax.ppermute(a, 'sub', [(i, (i + 1) % ns) for i in range(ns)])  32.4 us
    pallas_call x8, Pallas kernels, encode(): pl.pallas_call(functools.partial(encode_kernel, panels=panels, weights=le...  17 us
    all_gather x1, blocking collectives, body(): both = lax.all_gather(pattern, ('lat', 'sub'), tiled=True)  12.9 us
    ppermute x2, waiting for transfers between devices, body(): lax.ppermute(v, 'fsdp', [(i, (i + r) % nf) for i in range(nf)])  12.3 us
    pallas_call x2, Pallas kernels, decode(): pl.pallas_call(functools.partial(decode_kernel, n=n, ns=ns, weights=len(w...  11.5 us
    ppermute x4, waiting for transfers between devices, body(): over_y = lambda v: lax.ppermute(v, 'parts', flip)  9.84 us
  transfers between devices with their start and end apart: 68, of which 23 were waited for; matrix products, arithmetic and copies ran while one was open for 1% of the time, Pallas kernels for 13%

profile of v5, /device:TPU:0, one launch (start us, length us, event | category | flops | bytes accessed | tf_op | source)
XLA Modules:
  0.0 308.4 jit_solution(11447334313488892622)
XLA Ops:
  5.7 6.3 %all-to-all-start = ((bf16[8,2,128,128]{3,2,1,0:T(8,128)(2,1)}), bf16[8,2,128,128]{3,2,1,0:T(8,128)(2,1)S(1)}, u32[]{:S(2)}, u32[]{:S(2)}) async-start(bf16[8,2,128,128]{3,2,1,0:T(8,128)(2,1)} %get-tuple-element.34), calls=%async_computation | async-start | bytes 1048576 | tf_op jit(solution)/shard_map/all_to_all | solution.py:435
  12.2 6.7 %forward.1 = (bf16[256,2048]{1,0:T(8,128)(2,1)S(1)}, bf16[256,2048]{1,0:T(8,128)(2,1)S(1)}, f32[512,2048]{1,0:T(8,128)S(1)}, f32[512,2048]{1,0:T(8,128)S(1)}, f3...) custom-call(s32[1]{0:T(128)} %bitcast.9.meta, bf16[227,2048]{1,0:T(8,128)(2,1)S(1)} %bitcast.21, ...), custom_call_target="tpu_custom_call" | custom-call | flops 1549795328 | bytes 12582912 | tf_op jit(solution)/shard_map/forward/pallas_call | solution.py:90
  34.1 12.9 %all_gather.3 = s32[8,2,96]{2,1,0:T(2,128)S(1)} all-gather(s32[1,2,96]{2,1,0:T(2,128)S(1)} %add_bitcast_fusion), channel_id=1, replica_groups=mesh['parts'=2,'lat'=4,'fsdp'=2,'sub'=2] {'lat','sub'}, dimensions={0}, use_global_device_ids=true | all-gather | bytes 6912 | tf_op jit(solution)/shard_map/all_gather | solution.py:461
  52.4 9.8 %collective-permute-done.4.refs_6_.refs_7_.refs_19_ = bf16[8,2,128,128]{3,2,1,0:T(8,128)(2,1)S(1)} collective-permute-done((bf16[8,2,128,128]{3,2,1,0:T(8,128)(2,1)S(1)}, bf16[8,2,128,128]{3,2,1,0:T(8,128)(2,1)S(1)}, u32[]{:S(2)}, u32[]{:S(2)}) %collective-permute-start.4) | collective-permute-done | bytes 524320 | tf_op jit(solution)/shard_map/ppermute | solution.py:447
  69.4 4.7 %collective-permute-done.7.refs_9_.refs_10_.refs_22_ = bf16[8,1,128,128]{3,2,1,0:T(8,128)(2,1)S(1)} collective-permute-done((bf16[8,1,128,128]{3,2,1,0:T(8,128)(2,1)S(1)}, bf16[8,1,128,128]{3,2,1,0:T(8,128)(2,1)S(1)}, u32[]{:S(2)}, u32[]{:S(2)}) %collective-permute-start.7) | collective-permute-done | bytes 262176 | tf_op jit(solution)/shard_map/ppermute | solution.py:446
  105.7 6.8 %collective-permute-done.refs_3_.refs_1_ = bf16[256,2048]{1,0:T(8,128)(2,1)S(1)} collective-permute-done((bf16[256,2048]{1,0:T(8,128)(2,1)S(1)}, bf16[256,2048]{1,0:T(8,128)(2,1)S(1)}, u32[]{:S(2)}, u32[]{:S(2)}) %collective-permute-start) | collective-permute-done | bytes 1048608 | tf_op jit(solution)/shard_map/ppermute | solution.py:472
  126.5 8.1 %collective-permute-done.26.refs_1_ = bf16[2,12,128,128]{3,2,1,0:T(8,128)(2,1)S(1)} collective-permute-done((bf16[2,12,128,128]{3,2,1,0:T(8,128)(2,1)S(1)}, bf16[2,12,128,128]{3,2,1,0:T(8,128)(2,1)S(1)}, u32[]{:S(2)}, u32[]{:S(2)}) %collective-permute-start.26) | collective-permute-done | bytes 786464 | tf_op jit(solution)/shard_map/ppermute | solution.py:370
  138.0 4.4 %collective-permute-start.17 = (bf16[2,12,128,128]{3,2,1,0:T(8,128)(2,1)S(1)}, bf16[2,12,128,128]{3,2,1,0:T(8,128)(2,1)S(1)}, u32[]{:S(2)}, u32[]{:S(2)}) collective-permute-start(bf16[2,12,128,128]{3,2,1,0:T(8,128)(2,1)S(1)} %add.177.refs_7_), channel_id=1, source_target_pairs={{0,4},{4,8},{8,12},{5,1},{9,5},{13,9},{2,6},{6,10},{10,14},{7,3},{... | collective-permute-start | bytes 2359304 | tf_op jit(solution)/shard_map/ppermute | solution.py:370
  152.9 6.7 %collective-permute-start.51 = (bf16[2,12,128,128]{3,2,1,0:T(8,128)(2,1)S(1)}, bf16[2,12,128,128]{3,2,1,0:T(8,128)(2,1)S(1)}, u32[]{:S(2)}, u32[]{:S(2)}) collective-permute-start(bf16[2,12,128,128]{3,2,1,0:T(8,128)(2,1)S(1)} %add.178.refs_12_), channel_id=1, source_target_pairs={{0,4},{13,9},{2,6},{15,11},{16,20},{29,25},{18,22},{31,27}} | collective-permute-start | bytes 2359304 | tf_op jit(solution)/shard_map/ppermute | solution.py:370
  162.9 4.9 %collective-permute-start.29 = (bf16[2,12,128,128]{3,2,1,0:T(8,128)(2,1)S(1)}, bf16[2,12,128,128]{3,2,1,0:T(8,128)(2,1)S(1)}, u32[]{:S(2)}, u32[]{:S(2)}) collective-permute-start(bf16[2,12,128,128]{3,2,1,0:T(8,128)(2,1)S(1)} %add.184), channel_id=1, source_target_pairs={{0,4},{13,9},{2,6},{15,11},{16,20},{29,25},{18,22},{31,27}} | collective-permute-start | bytes 2359304 | tf_op jit(solution)/shard_map/ppermute | solution.py:370
  170.4 6.8 %collective-permute-done.29.refs_2_ = bf16[2,12,128,128]{3,2,1,0:T(8,128)(2,1)S(1)} collective-permute-done((bf16[2,12,128,128]{3,2,1,0:T(8,128)(2,1)S(1)}, bf16[2,12,128,128]{3,2,1,0:T(8,128)(2,1)S(1)}, u32[]{:S(2)}, u32[]{:S(2)}) %collective-permute-start.29) | collective-permute-done | bytes 786464 | tf_op jit(solution)/shard_map/ppermute | solution.py:370
  182.8 6.3 %collective-permute-start.31 = (bf16[2,12,128,128]{3,2,1,0:T(8,128)(2,1)S(1)}, bf16[2,12,128,128]{3,2,1,0:T(8,128)(2,1)S(1)}, u32[]{:S(2)}, u32[]{:S(2)}) collective-permute-start(bf16[2,12,128,128]{3,2,1,0:T(8,128)(2,1)S(1)} %add.185), channel_id=1, source_target_pairs={{0,4},{4,8},{9,5},{13,9},{2,6},{6,10},{11,7},{15,11},{16,20},{20,2... | collective-permute-start | bytes 2359304 | tf_op jit(solution)/shard_map/ppermute | solution.py:370
  189.7 8.2 %collective-permute-start.41 = (bf16[2,12,128,128]{3,2,1,0:T(8,128)(2,1)S(1)}, bf16[2,12,128,128]{3,2,1,0:T(8,128)(2,1)S(1)}, u32[]{:S(2)}, u32[]{:S(2)}) collective-permute-start(bf16[2,12,128,128]{3,2,1,0:T(8,128)(2,1)S(1)} %collective-permute-done.38.refs_10_.refs_3_), channel_id=1, source_target_pairs={{0,1},{1,0},{2,3},{3,2},{4,5},{5,4},{6,7},{7,6},{8,9},{9,8},{10,11... | collective-permute-start | bytes 2359304 | tf_op jit(solution)/shard_map/ppermute | solution.py:341
  200.3 6.3 %collective-permute-start.53 = (bf16[2,12,128,128]{3,2,1,0:T(8,128)(2,1)S(1)}, bf16[2,12,128,128]{3,2,1,0:T(8,128)(2,1)S(1)}, u32[]{:S(2)}, u32[]{:S(2)}) collective-permute-start(bf16[2,12,128,128]{3,2,1,0:T(8,128)(2,1)S(1)} %add.190), channel_id=1, source_target_pairs={{0,4},{4,8},{8,12},{5,1},{9,5},{13,9},{2,6},{6,10},{10,14},{7,3},{... | collective-permute-start | bytes 2359304 | tf_op jit(solution)/shard_map/ppermute | solution.py:370
  213.7 5.1 %decode.2 = (bf16[256,2048]{1,0:T(8,128)(2,1)S(1)}, bf16[256,2048]{1,0:T(8,128)(2,1)S(1)}) custom-call(s32[8,16]{1,0:T(8,128)S(1)} %get-tuple-element.72.tab_j, s32[8,16]{1,0:T(8,128)S(1)} %get-tuple-element.73.tab_m, s32[3]{0:T(128)S(1)} %pad_add_fusion.1.meta, bf16[2,12,128,128]{3,2,1,0:T(8,128)(2,1)S(1)} %add.183.refs_0_, ...), custom_call_target="tpu_custom_call" | custom-call | flops 4294967296 | bytes 12582912 | tf_op jit(solution)/shard_map/decode/pallas_call | solution.py:312
  219.3 5.2 %collective-permute-done.33.refs_1_ = bf16[2,12,128,128]{3,2,1,0:T(8,128)(2,1)S(1)} collective-permute-done((bf16[2,12,128,128]{3,2,1,0:T(8,128)(2,1)S(1)}, bf16[2,12,128,128]{3,2,1,0:T(8,128)(2,1)S(1)}, u32[]{:S(2)}, u32[]{:S(2)}) %collective-permute-start.33) | collective-permute-done | bytes 786464 | tf_op jit(solution)/shard_map/ppermute | solution.py:370
  225.2 4.7 %collective-permute-start.55 = (bf16[2,12,128,128]{3,2,1,0:T(8,128)(2,1)S(1)}, bf16[2,12,128,128]{3,2,1,0:T(8,128)(2,1)S(1)}, u32[]{:S(2)}, u32[]{:S(2)}) collective-permute-start(bf16[2,12,128,128]{3,2,1,0:T(8,128)(2,1)S(1)} %add.192.refs_7_), channel_id=1, source_target_pairs={{0,4},{4,8},{8,12},{5,1},{9,5},{13,9},{2,6},{6,10},{10,14},{7,3},{... | collective-permute-start | bytes 2359304 | tf_op jit(solution)/shard_map/ppermute | solution.py:370
  240.0 7.7 %collective-permute-done.43.refs_1_ = bf16[2,12,128,128]{3,2,1,0:T(8,128)(2,1)S(1)} collective-permute-done((bf16[2,12,128,128]{3,2,1,0:T(8,128)(2,1)S(1)}, bf16[2,12,128,128]{3,2,1,0:T(8,128)(2,1)S(1)}, u32[]{:S(2)}, u32[]{:S(2)}) %collective-permute-start.43) | collective-permute-done | bytes 786464 | tf_op jit(solution)/shard_map/ppermute | solution.py:370
  248.5 5.5 %collective-permute-done.57.refs_1_ = bf16[256,2048]{1,0:T(8,128)(2,1)S(1)} collective-permute-done((bf16[256,2048]{1,0:T(8,128)(2,1)S(1)}, bf16[256,2048]{1,0:T(8,128)(2,1)S(1)}, u32[]{:S(2)}, u32[]{:S(2)}) %collective-permute-start.57) | collective-permute-done | bytes 1048608 | tf_op jit(solution)/shard_map/ppermute | solution.py:472
  254.0 6.1 %backward.1 = (f32[16,512]{1,0:T(8,128)S(1)}, f32[16,227]{1,0:T(8,128)S(1)}) custom-call(s32[2]{0:T(128)S(1)} %fusion.6.offs, bf16[256,2048]{1,0:T(8,128)(2,1)S(1)} %get-tuple-element.55.refs_2_.refs_0_, bf16[256,2048]{1,0:T(8,128)(2,1)S(1)} %collective-permute-done.57.refs_1_, f32[512,2048]{1,0:T(8,128)S(1)} %copy-done.2, f32[512,2048]{1,0:T(8,128)S(1)} %copy-done.4, ...), custom_call_target="tpu_custom_call" | custom-call | flops 1073741824 | bytes 10485760 | tf_op jit(solution)/shard_map/backward/pallas_call | solution.py:161
  271.2 4.5 %collective-permute-start.61 = (f32[16,739]{1,0:T(8,128)S(1)}, f32[16,739]{1,0:T(8,128)S(1)}, u32[]{:S(2)}, u32[]{:S(2)}) collective-permute-start(f32[16,739]{1,0:T(8,128)S(1)} %add.136), channel_id=1, source_target_pairs={{0,8},{4,12},{8,0},{12,4},{1,9},{5,13},{9,1},{13,5},{2,10},{6,14},... | collective-permute-start | bytes 141896 | tf_op jit(solution)/shard_map/ppermute | solution.py:387
  281.9 9.6 %collective-permute-start.48 = (bf16[2,12,128,128]{3,2,1,0:T(8,128)(2,1)S(1)}, bf16[2,12,128,128]{3,2,1,0:T(8,128)(2,1)S(1)}, u32[]{:S(2)}, u32[]{:S(2)}) collective-permute-start(bf16[2,12,128,128]{3,2,1,0:T(8,128)(2,1)S(1)} %collective-permute-done.45.refs_3_), channel_id=1, source_target_pairs={{0,1},{1,0},{2,3},{3,2},{4,5},{5,4},{6,7},{7,6},{8,9},{9,8},{10,11... | collective-permute-start | bytes 2359304 | tf_op jit(solution)/shard_map/ppermute | solution.py:341
  291.5 8.4 %collective-permute-start.65 = (bf16[2,12,128,128]{3,2,1,0:T(8,128)(2,1)S(1)}, bf16[2,12,128,128]{3,2,1,0:T(8,128)(2,1)S(1)}, u32[]{:S(2)}, u32[]{:S(2)}) collective-permute-start(bf16[2,12,128,128]{3,2,1,0:T(8,128)(2,1)S(1)} %collective-permute-done.62.refs_10_), channel_id=1, source_target_pairs={{0,1},{1,0},{2,3},{3,2},{4,5},{5,4},{6,7},{7,6},{8,9},{9,8},{10,11... | collective-permute-start | bytes 2359304 | tf_op jit(solution)/shard_map/ppermute | solution.py:341
  301.8 6.4 %decode.3 = bf16[256,4096]{1,0:T(8,128)(2,1)} custom-call(s32[8,16]{1,0:T(8,128)S(1)} %get-tuple-element.72.tab_j, s32[8,16]{1,0:T(8,128)S(1)} %get-tuple-element.73.tab_m, s32[3]{0:T(128)S(1)} %pad_add_fusion.1.meta, bf16[2,12,128,128]{3,2,1,0:T(8,128)(2,1)S(1)} %add.188.refs_0_, bf16[2,12,128,128]{3,2,1,0:T(8,128)(2,1)S(1)} %collective-permute-done.43.refs_1_, ...), custom_call_target="tpu_custom_call" | custom-call | flops 4294967296 | bytes 12582912 | tf_op jit(solution)/shard_map/decode/pallas_call | solution.py:312
  (219 shorter events, 144.4 us)
Async XLA Ops:
  5.7 21.7 %all-to-all-start = ((bf16[8,2,128,128]{3,2,1,0:T(8,128)(2,1)}), bf16[8,2,128,128]{3,2,1,0:T(8,128)(2,1)S(1)}, u32[]{:S(2)}, u32[]{:S(2)}) async-start(bf16[8,2,128,128]{3,2,1,0:T(8,128)(2,1)} %get-tuple-element.34), calls=%async_computation | async-start | bytes 1048576 | tf_op jit(solution)/shard_map/all_to_all | solution.py:435
  27.4 20.1 %all-to-all-start.1 = ((bf16[8,2,128,128]{3,2,1,0:T(8,128)(2,1)}), bf16[8,2,128,128]{3,2,1,0:T(8,128)(2,1)S(1)}, u32[]{:S(2)}, u32[]{:S(2)}) async-start(bf16[8,2,128,128]{3,2,1,0:T(8,128)(2,1)} %get-tuple-element.40), calls=%async_computation.1 | async-start | bytes 1048576 | tf_op jit(solution)/shard_map/all_to_all | solution.py:435
  31.0 20.1 %collective-permute-start.3 = (bf16[8,2,128,128]{3,2,1,0:T(8,128)(2,1)S(1)}, bf16[8,2,128,128]{3,2,1,0:T(8,128)(2,1)S(1)}, u32[]{:S(2)}, u32[]{:S(2)}) collective-permute-start(bf16[8,2,128,128]{3,2,1,0:T(8,128)(2,1)S(1)} %all-to-all-done.refs_1_.refs_2_.refs_14_), channel_id=1, source_target_pairs={{0,16},{16,0},{1,17},{17,1},{2,18},{18,2},{3,19},{19,3},{4,20},{20... | collective-permute-start | bytes 1572872 | tf_op jit(solution)/shard_map/ppermute | solution.py:447
  32.6 19.2 %collective-permute-start.1 = (bf16[8,2,128,128]{3,2,1,0:T(8,128)(2,1)S(1)}, bf16[8,2,128,128]{3,2,1,0:T(8,128)(2,1)S(1)}, u32[]{:S(2)}, u32[]{:S(2)}) collective-permute-start(bf16[8,2,128,128]{3,2,1,0:T(8,128)(2,1)S(1)} %all-to-all-done.refs_1_.refs_2_.refs_14_), channel_id=1, source_target_pairs={{0,2},{2,0},{1,3},{3,1},{4,6},{6,4},{5,7},{7,5},{8,10},{10,8},{9,1... | collective-permute-start | bytes 1572872 | tf_op jit(solution)/shard_map/ppermute | solution.py:446
  51.2 18.2 %collective-permute-start.5 = (bf16[8,1,128,128]{3,2,1,0:T(8,128)(2,1)S(1)}, bf16[8,1,128,128]{3,2,1,0:T(8,128)(2,1)S(1)}, u32[]{:S(2)}, u32[]{:S(2)}) collective-permute-start(bf16[8,1,128,128]{3,2,1,0:T(8,128)(2,1)S(1)} %slice.34), channel_id=1, source_target_pairs={{0,2},{2,0},{1,3},{3,1},{4,6},{6,4},{5,7},{7,5},{8,10},{10,8},{9,1... | collective-permute-start | bytes 786440 | tf_op jit(solution)/shard_map/ppermute | solution.py:446
  51.9 17.6 %collective-permute-start.6 = (bf16[8,1,128,128]{3,2,1,0:T(8,128)(2,1)S(1)}, bf16[8,1,128,128]{3,2,1,0:T(8,128)(2,1)S(1)}, u32[]{:S(2)}, u32[]{:S(2)}) collective-permute-start(bf16[8,1,128,128]{3,2,1,0:T(8,128)(2,1)S(1)} %slice.35), channel_id=1, source_target_pairs={{0,16},{16,0},{1,17},{17,1},{2,18},{18,2},{3,19},{19,3},{4,20},{20... | collective-permute-start | bytes 786440 | tf_op jit(solution)/shard_map/ppermute | solution.py:447
  86.9 25.6 %collective-permute-start = (bf16[256,2048]{1,0:T(8,128)(2,1)S(1)}, bf16[256,2048]{1,0:T(8,128)(2,1)S(1)}, u32[]{:S(2)}, u32[]{:S(2)}) collective-permute-start(bf16[256,2048]{1,0:T(8,128)(2,1)S(1)} %copy-done.12), channel_id=1, source_target_pairs={{0,2},{2,0},{1,3},{3,1},{4,6},{6,4},{5,7},{7,5},{8,10},{10,8},{9,1... | collective-permute-start | bytes 3145736 | tf_op jit(solution)/shard_map/ppermute | solution.py:472
  92.4 20.0 %collective-permute-start.9 = (bf16[2,12,128,128]{3,2,1,0:T(8,128)(2,1)S(1)}, bf16[2,12,128,128]{3,2,1,0:T(8,128)(2,1)S(1)}, u32[]{:S(2)}, u32[]{:S(2)}) collective-permute-start(bf16[2,12,128,128]{3,2,1,0:T(8,128)(2,1)S(1)} %get-tuple-element.42.refs_0_), channel_id=1, source_target_pairs={{0,1},{1,0},{2,3},{3,2},{4,5},{5,4},{6,7},{7,6},{8,9},{9,8},{10,11... | collective-permute-start | bytes 2359304 | tf_op jit(solution)/shard_map/ppermute | solution.py:341
  92.8 19.6 %collective-permute-start.13 = (bf16[2,12,128,128]{3,2,1,0:T(8,128)(2,1)S(1)}, bf16[2,12,128,128]{3,2,1,0:T(8,128)(2,1)S(1)}, u32[]{:S(2)}, u32[]{:S(2)}) collective-permute-start(bf16[2,12,128,128]{3,2,1,0:T(8,128)(2,1)S(1)} %add.174), channel_id=1, source_target_pairs={{0,4},{4,8},{9,5},{13,9},{2,6},{6,10},{11,7},{15,11},{16,20},{20,2... | collective-permute-start | bytes 2359304 | tf_op jit(solution)/shard_map/ppermute | solution.py:370
  142.8 18.9 %collective-permute-start.28 = (bf16[2,12,128,128]{3,2,1,0:T(8,128)(2,1)S(1)}, bf16[2,12,128,128]{3,2,1,0:T(8,128)(2,1)S(1)}, u32[]{:S(2)}, u32[]{:S(2)}) collective-permute-start(bf16[2,12,128,128]{3,2,1,0:T(8,128)(2,1)S(1)} %add.183.refs_0_), channel_id=1, source_target_pairs={{0,4},{4,8},{8,12},{5,1},{9,5},{13,9},{2,6},{6,10},{10,14},{7,3},{... | collective-permute-start | bytes 2359304 | tf_op jit(solution)/shard_map/ppermute | solution.py:370
  168.8 20.3 %collective-permute-start.34 = (bf16[2,12,128,128]{3,2,1,0:T(8,128)(2,1)S(1)}, bf16[2,12,128,128]{3,2,1,0:T(8,128)(2,1)S(1)}, u32[]{:S(2)}, u32[]{:S(2)}) collective-permute-start(bf16[2,12,128,128]{3,2,1,0:T(8,128)(2,1)S(1)} %collective-permute-done.28.refs_2_.refs_1_), channel_id=1, source_target_pairs={{0,1},{1,0},{2,3},{3,2},{4,5},{5,4},{6,7},{7,6},{8,9},{9,8},{10,11... | collective-permute-start | bytes 2359304 | tf_op jit(solution)/shard_map/ppermute | solution.py:341
  169.7 19.5 %collective-permute-start.38 = (bf16[2,12,128,128]{3,2,1,0:T(8,128)(2,1)S(1)}, bf16[2,12,128,128]{3,2,1,0:T(8,128)(2,1)S(1)}, u32[]{:S(2)}, u32[]{:S(2)}) collective-permute-start(bf16[2,12,128,128]{3,2,1,0:T(8,128)(2,1)S(1)} %collective-permute-done.37.refs_9_.refs_3_), channel_id=1, source_target_pairs={{8,12},{5,1},{10,14},{7,3},{24,28},{21,17},{26,30},{23,19}} | collective-permute-start | bytes 2359304 | tf_op jit(solution)/shard_map/ppermute | solution.py:370
  178.0 20.0 %collective-permute-start.52 = (bf16[2,12,128,128]{3,2,1,0:T(8,128)(2,1)S(1)}, bf16[2,12,128,128]{3,2,1,0:T(8,128)(2,1)S(1)}, u32[]{:S(2)}, u32[]{:S(2)}) collective-permute-start(bf16[2,12,128,128]{3,2,1,0:T(8,128)(2,1)S(1)} %add.189), channel_id=1, source_target_pairs={{0,4},{4,8},{9,5},{13,9},{2,6},{6,10},{11,7},{15,11},{16,20},{20,2... | collective-permute-start | bytes 2359304 | tf_op jit(solution)/shard_map/ppermute | solution.py:370
  189.1 17.9 %collective-permute-start.40 = (bf16[2,12,128,128]{3,2,1,0:T(8,128)(2,1)S(1)}, bf16[2,12,128,128]{3,2,1,0:T(8,128)(2,1)S(1)}, u32[]{:S(2)}, u32[]{:S(2)}) collective-permute-start(bf16[2,12,128,128]{3,2,1,0:T(8,128)(2,1)S(1)} %collective-permute-done.37.refs_9_.refs_3_), channel_id=1, source_target_pairs={{0,1},{1,0},{2,3},{3,2},{4,5},{5,4},{6,7},{7,6},{8,9},{9,8},{10,11... | collective-permute-start | bytes 2359304 | tf_op jit(solution)/shard_map/ppermute | solution.py:341
  189.2 24.5 %collective-permute-start.35 = (bf16[2,12,128,128]{3,2,1,0:T(8,128)(2,1)S(1)}, bf16[2,12,128,128]{3,2,1,0:T(8,128)(2,1)S(1)}, u32[]{:S(2)}, u32[]{:S(2)}) collective-permute-start(bf16[2,12,128,128]{3,2,1,0:T(8,128)(2,1)S(1)} %collective-permute-done.30.refs_3_.refs_2_), channel_id=1, source_target_pairs={{0,1},{1,0},{2,3},{3,2},{4,5},{5,4},{6,7},{7,6},{8,9},{9,8},{10,11... | collective-permute-start | bytes 2359304 | tf_op jit(solution)/shard_map/ppermute | solution.py:341
  189.7 24.0 %collective-permute-start.41 = (bf16[2,12,128,128]{3,2,1,0:T(8,128)(2,1)S(1)}, bf16[2,12,128,128]{3,2,1,0:T(8,128)(2,1)S(1)}, u32[]{:S(2)}, u32[]{:S(2)}) collective-permute-start(bf16[2,12,128,128]{3,2,1,0:T(8,128)(2,1)S(1)} %collective-permute-done.38.refs_10_.refs_3_), channel_id=1, source_target_pairs={{0,1},{1,0},{2,3},{3,2},{4,5},{5,4},{6,7},{7,6},{8,9},{9,8},{10,11... | collective-permute-start | bytes 2359304 | tf_op jit(solution)/shard_map/ppermute | solution.py:341
  200.3 18.6 %collective-permute-start.53 = (bf16[2,12,128,128]{3,2,1,0:T(8,128)(2,1)S(1)}, bf16[2,12,128,128]{3,2,1,0:T(8,128)(2,1)S(1)}, u32[]{:S(2)}, u32[]{:S(2)}) collective-permute-start(bf16[2,12,128,128]{3,2,1,0:T(8,128)(2,1)S(1)} %add.190), channel_id=1, source_target_pairs={{0,4},{4,8},{8,12},{5,1},{9,5},{13,9},{2,6},{6,10},{10,14},{7,3},{... | collective-permute-start | bytes 2359304 | tf_op jit(solution)/shard_map/ppermute | solution.py:370
  234.6 19.4 %collective-permute-start.57 = (bf16[256,2048]{1,0:T(8,128)(2,1)S(1)}, bf16[256,2048]{1,0:T(8,128)(2,1)S(1)}, u32[]{:S(2)}, u32[]{:S(2)}) collective-permute-start(bf16[256,2048]{1,0:T(8,128)(2,1)S(1)} %get-tuple-element.58), channel_id=1, source_target_pairs={{0,2},{2,0},{1,3},{3,1},{4,6},{6,4},{5,7},{7,5},{8,10},{10,8},{9,1... | collective-permute-start | bytes 3145736 | tf_op jit(solution)/shard_map/ppermute | solution.py:472
  239.3 39.0 %collective-permute-start.56 = (bf16[2,12,128,128]{3,2,1,0:T(8,128)(2,1)S(1)}, bf16[2,12,128,128]{3,2,1,0:T(8,128)(2,1)S(1)}, u32[]{:S(2)}, u32[]{:S(2)}) collective-permute-start(bf16[2,12,128,128]{3,2,1,0:T(8,128)(2,1)S(1)} %collective-permute-done.55.refs_8_), channel_id=1, source_target_pairs={{4,8},{8,12},{5,1},{9,5},{6,10},{10,14},{7,3},{11,7},{20,24},{24,2... | collective-permute-start | bytes 2359304 | tf_op jit(solution)/shard_map/ppermute | solution.py:370
  247.7 30.5 %collective-permute-start.44 = (bf16[2,12,128,128]{3,2,1,0:T(8,128)(2,1)S(1)}, bf16[2,12,128,128]{3,2,1,0:T(8,128)(2,1)S(1)}, u32[]{:S(2)}, u32[]{:S(2)}) collective-permute-start(bf16[2,12,128,128]{3,2,1,0:T(8,128)(2,1)S(1)} %collective-permute-done.43.refs_1_), channel_id=1, source_target_pairs={{4,8},{8,12},{5,1},{9,5},{6,10},{10,14},{7,3},{11,7},{20,24},{24,2... | collective-permute-start | bytes 2359304 | tf_op jit(solution)/shard_map/ppermute | solution.py:370
  279.7 21.4 %collective-permute-start.63 = (bf16[2,12,128,128]{3,2,1,0:T(8,128)(2,1)S(1)}, bf16[2,12,128,128]{3,2,1,0:T(8,128)(2,1)S(1)}, u32[]{:S(2)}, u32[]{:S(2)}) collective-permute-start(bf16[2,12,128,128]{3,2,1,0:T(8,128)(2,1)S(1)} %collective-permute-done.55.refs_8_), channel_id=1, source_target_pairs={{0,1},{1,0},{2,3},{3,2},{4,5},{5,4},{6,7},{7,6},{8,9},{9,8},{10,11... | collective-permute-start | bytes 2359304 | tf_op jit(solution)/shard_map/ppermute | solution.py:341
  281.4 19.7 %collective-permute-start.47 = (bf16[2,12,128,128]{3,2,1,0:T(8,128)(2,1)S(1)}, bf16[2,12,128,128]{3,2,1,0:T(8,128)(2,1)S(1)}, u32[]{:S(2)}, u32[]{:S(2)}) collective-permute-start(bf16[2,12,128,128]{3,2,1,0:T(8,128)(2,1)S(1)} %collective-permute-done.44.refs_2_), channel_id=1, source_target_pairs={{0,1},{1,0},{2,3},{3,2},{4,5},{5,4},{6,7},{7,6},{8,9},{9,8},{10,11... | collective-permute-start | bytes 2359304 | tf_op jit(solution)/shard_map/ppermute | solution.py:341
  281.5 19.6 %collective-permute-start.64 = (bf16[2,12,128,128]{3,2,1,0:T(8,128)(2,1)S(1)}, bf16[2,12,128,128]{3,2,1,0:T(8,128)(2,1)S(1)}, u32[]{:S(2)}, u32[]{:S(2)}) collective-permute-start(bf16[2,12,128,128]{3,2,1,0:T(8,128)(2,1)S(1)} %collective-permute-done.56.refs_9_), channel_id=1, source_target_pairs={{0,1},{1,0},{2,3},{3,2},{4,5},{5,4},{6,7},{7,6},{8,9},{9,8},{10,11... | collective-permute-start | bytes 2359304 | tf_op jit(solution)/shard_map/ppermute | solution.py:341
  281.9 19.2 %collective-permute-start.48 = (bf16[2,12,128,128]{3,2,1,0:T(8,128)(2,1)S(1)}, bf16[2,12,128,128]{3,2,1,0:T(8,128)(2,1)S(1)}, u32[]{:S(2)}, u32[]{:S(2)}) collective-permute-start(bf16[2,12,128,128]{3,2,1,0:T(8,128)(2,1)S(1)} %collective-permute-done.45.refs_3_), channel_id=1, source_target_pairs={{0,1},{1,0},{2,3},{3,2},{4,5},{5,4},{6,7},{7,6},{8,9},{9,8},{10,11... | collective-permute-start | bytes 2359304 | tf_op jit(solution)/shard_map/ppermute | solution.py:341
  (62 other events, 779.0 us)

commit v6 on v5

--- a/solution.py
+++ b/solution.py
@@ -84,7 +84,7 @@
 def forward(meta, x, w_in, a_down, a_up, w_out, nf, deps):
     width, rows = w_out.shape[0], x.shape[1]
     rank = a_down.shape[1]
-    step = min(512, rows)
+    step = min(1024, rows)
     chans = width // nf
     full = lambda a: pl.BlockSpec(a.shape, lambda i, m: (0, 0))
     return pl.pallas_call(
@@ -155,7 +155,7 @@
 def backward(offs, pieces, normed, slope, inv, mid, x, w_out, a_up):
     width, rows = normed.shape
     rank = a_up.shape[0]
-    step = min(512, rows)
+    step = min(1024, rows)
     full = lambda a: pl.BlockSpec(a.shape, lambda i, m: (0, 0))
     tall = lambda a: pl.BlockSpec((a.shape[0], step), lambda i, m: (0, i))
     return pl.pallas_call(
@@ -350,7 +350,7 @@
 
 def add(terms, deps):
     shape = terms[0].shape
-    parts = 3 if shape[1] % 3 == 0 else 1
+    parts = 1
     spec = pl.BlockSpec((1, shape[1] // parts) + shape[2:], lambda i, j: (i, j, 0, 0))
     return pl.pallas_call(
         functools.partial(add_kernel, count=len(terms)),

time: 309 us -> 308 us (level)
  Pallas kernels: 49.6 us -> 46.5 us
  transfers between devices with their start and end apart: 68 -> 68, of which waited for: 23 -> 23; matrix products, arithmetic and copies ran while one was open for 1% -> 1% of each run, Pallas kernels for 13% -> 12%
where the time goes in v6:
time: 308 us; the launch traced here: 307 us
  starting transfers between devices  140 us (45%)
  waiting for transfers between devices  94 us (31%)
  Pallas kernels  46.5 us (15%)
  blocking collectives  12.9 us (4%)
  local copies, waits for them, and re-layouts  8.48 us (3%)
    ppermute x24, starting transfers between devices, along(): return lax.ppermute(value, ('lat', 'sub'), pairs)  75 us
    ppermute x24, waiting for transfers between devices, along(): return lax.ppermute(value, ('lat', 'sub'), pairs)  50 us
    ppermute x28, starting transfers between devices, swap_sub(): return lax.ppermute(a, 'sub', [(i, (i + 1) % ns) for i in range(ns)])  32.6 us
    pallas_call x8, Pallas kernels, encode(): pl.pallas_call(functools.partial(encode_kernel, panels=panels, weights=le...  17.1 us
    all_gather x1, blocking collectives, body(): both = lax.all_gather(pattern, ('lat', 'sub'), tiled=True)  12.9 us
    ppermute x2, waiting for transfers between devices, body(): lax.ppermute(v, 'fsdp', [(i, (i + r) % nf) for i in range(nf)])  12.1 us
    pallas_call x2, Pallas kernels, decode(): pl.pallas_call(functools.partial(decode_kernel, n=n, ns=ns, weights=len(w...  11.5 us
    ppermute x4, waiting for transfers between devices, body(): over_y = lambda v: lax.ppermute(v, 'parts', flip)  9.84 us
  transfers between devices with their start and end apart: 68, of which 23 were waited for; matrix products, arithmetic and copies ran while one was open for 1% of the time, Pallas kernels for 12%

profile of v6, /device:TPU:0, one launch (start us, length us, event | category | flops | bytes accessed | tf_op | source)
XLA Modules:
  0.0 307.2 jit_solution(14401249030739213055)
XLA Ops:
  5.7 6.3 %all-to-all-start = ((bf16[8,2,128,128]{3,2,1,0:T(8,128)(2,1)}), bf16[8,2,128,128]{3,2,1,0:T(8,128)(2,1)S(1)}, u32[]{:S(2)}, u32[]{:S(2)}) async-start(bf16[8,2,128,128]{3,2,1,0:T(8,128)(2,1)} %get-tuple-element.34), calls=%async_computation | async-start | bytes 1048576 | tf_op jit(solution)/shard_map/all_to_all | solution.py:435
  12.2 5.6 %forward.1 = (bf16[256,2048]{1,0:T(8,128)(2,1)S(1)}, bf16[256,2048]{1,0:T(8,128)(2,1)S(1)}, f32[512,2048]{1,0:T(8,128)S(1)}, f32[512,2048]{1,0:T(8,128)S(1)}, f3...) custom-call(s32[1]{0:T(128)} %bitcast.9.meta, bf16[227,2048]{1,0:T(8,128)(2,1)S(1)} %bitcast.21, ...), custom_call_target="tpu_custom_call" | custom-call | flops 1549795328 | bytes 12582912 | tf_op jit(solution)/shard_map/forward/pallas_call | solution.py:90
  22.8 4.6 %all-to-all-done.refs_1_.refs_2_.refs_14_ = bf16[8,2,128,128]{3,2,1,0:T(8,128)(2,1)S(1)} async-done(((bf16[8,2,128,128]{3,2,1,0:T(8,128)(2,1)}), bf16[8,2,128,128]{3,2,1,0:T(8,128)(2,1)S(1)}, u32[]{:S(2)}, u32[]{:S(2)}) %all-to-all-start) | async-done | bytes 524320 | tf_op jit(solution)/shard_map/all_to_all | solution.py:435
  34.1 12.9 %all_gather.3 = s32[8,2,96]{2,1,0:T(2,128)S(1)} all-gather(s32[1,2,96]{2,1,0:T(2,128)S(1)} %add_bitcast_fusion), channel_id=1, replica_groups=mesh['parts'=2,'lat'=4,'fsdp'=2,'sub'=2] {'lat','sub'}, dimensions={0}, use_global_device_ids=true | all-gather | bytes 6912 | tf_op jit(solution)/shard_map/all_gather | solution.py:461
  52.4 9.8 %collective-permute-done.4.refs_6_.refs_7_.refs_19_ = bf16[8,2,128,128]{3,2,1,0:T(8,128)(2,1)S(1)} collective-permute-done((bf16[8,2,128,128]{3,2,1,0:T(8,128)(2,1)S(1)}, bf16[8,2,128,128]{3,2,1,0:T(8,128)(2,1)S(1)}, u32[]{:S(2)}, u32[]{:S(2)}) %collective-permute-start.4) | collective-permute-done | bytes 524320 | tf_op jit(solution)/shard_map/ppermute | solution.py:447
  69.4 4.7 %collective-permute-done.7.refs_9_.refs_10_.refs_22_ = bf16[8,1,128,128]{3,2,1,0:T(8,128)(2,1)S(1)} collective-permute-done((bf16[8,1,128,128]{3,2,1,0:T(8,128)(2,1)S(1)}, bf16[8,1,128,128]{3,2,1,0:T(8,128)(2,1)S(1)}, u32[]{:S(2)}, u32[]{:S(2)}) %collective-permute-start.7) | collective-permute-done | bytes 262176 | tf_op jit(solution)/shard_map/ppermute | solution.py:446
  105.6 6.8 %collective-permute-done.refs_3_.refs_1_ = bf16[256,2048]{1,0:T(8,128)(2,1)S(1)} collective-permute-done((bf16[256,2048]{1,0:T(8,128)(2,1)S(1)}, bf16[256,2048]{1,0:T(8,128)(2,1)S(1)}, u32[]{:S(2)}, u32[]{:S(2)}) %collective-permute-start) | collective-permute-done | bytes 1048608 | tf_op jit(solution)/shard_map/ppermute | solution.py:472
  126.4 8.1 %collective-permute-done.26.refs_1_ = bf16[2,12,128,128]{3,2,1,0:T(8,128)(2,1)S(1)} collective-permute-done((bf16[2,12,128,128]{3,2,1,0:T(8,128)(2,1)S(1)}, bf16[2,12,128,128]{3,2,1,0:T(8,128)(2,1)S(1)}, u32[]{:S(2)}, u32[]{:S(2)}) %collective-permute-start.26) | collective-permute-done | bytes 786464 | tf_op jit(solution)/shard_map/ppermute | solution.py:370
  152.6 6.5 %collective-permute-start.51 = (bf16[2,12,128,128]{3,2,1,0:T(8,128)(2,1)S(1)}, bf16[2,12,128,128]{3,2,1,0:T(8,128)(2,1)S(1)}, u32[]{:S(2)}, u32[]{:S(2)}) collective-permute-start(bf16[2,12,128,128]{3,2,1,0:T(8,128)(2,1)S(1)} %add.178.refs_12_), channel_id=1, source_target_pairs={{0,4},{13,9},{2,6},{15,11},{16,20},{29,25},{18,22},{31,27}} | collective-permute-start | bytes 2359304 | tf_op jit(solution)/shard_map/ppermute | solution.py:370
  162.4 5.1 %collective-permute-start.29 = (bf16[2,12,128,128]{3,2,1,0:T(8,128)(2,1)S(1)}, bf16[2,12,128,128]{3,2,1,0:T(8,128)(2,1)S(1)}, u32[]{:S(2)}, u32[]{:S(2)}) collective-permute-start(bf16[2,12,128,128]{3,2,1,0:T(8,128)(2,1)S(1)} %add.184), channel_id=1, source_target_pairs={{0,4},{13,9},{2,6},{15,11},{16,20},{29,25},{18,22},{31,27}} | collective-permute-start | bytes 2359304 | tf_op jit(solution)/shard_map/ppermute | solution.py:370
  170.1 6.9 %collective-permute-done.29.refs_2_ = bf16[2,12,128,128]{3,2,1,0:T(8,128)(2,1)S(1)} collective-permute-done((bf16[2,12,128,128]{3,2,1,0:T(8,128)(2,1)S(1)}, bf16[2,12,128,128]{3,2,1,0:T(8,128)(2,1)S(1)}, u32[]{:S(2)}, u32[]{:S(2)}) %collective-permute-start.29) | collective-permute-done | bytes 786464 | tf_op jit(solution)/shard_map/ppermute | solution.py:370
  182.5 6.2 %collective-permute-start.31 = (bf16[2,12,128,128]{3,2,1,0:T(8,128)(2,1)S(1)}, bf16[2,12,128,128]{3,2,1,0:T(8,128)(2,1)S(1)}, u32[]{:S(2)}, u32[]{:S(2)}) collective-permute-start(bf16[2,12,128,128]{3,2,1,0:T(8,128)(2,1)S(1)} %add.185), channel_id=1, source_target_pairs={{0,4},{4,8},{9,5},{13,9},{2,6},{6,10},{11,7},{15,11},{16,20},{20,2... | collective-permute-start | bytes 2359304 | tf_op jit(solution)/shard_map/ppermute | solution.py:370
  189.3 8.4 %collective-permute-start.41 = (bf16[2,12,128,128]{3,2,1,0:T(8,128)(2,1)S(1)}, bf16[2,12,128,128]{3,2,1,0:T(8,128)(2,1)S(1)}, u32[]{:S(2)}, u32[]{:S(2)}) collective-permute-start(bf16[2,12,128,128]{3,2,1,0:T(8,128)(2,1)S(1)} %collective-permute-done.38.refs_10_.refs_3_), channel_id=1, source_target_pairs={{0,1},{1,0},{2,3},{3,2},{4,5},{5,4},{6,7},{7,6},{8,9},{9,8},{10,11... | collective-permute-start | bytes 2359304 | tf_op jit(solution)/shard_map/ppermute | solution.py:341
  200.0 6.2 %collective-permute-start.53 = (bf16[2,12,128,128]{3,2,1,0:T(8,128)(2,1)S(1)}, bf16[2,12,128,128]{3,2,1,0:T(8,128)(2,1)S(1)}, u32[]{:S(2)}, u32[]{:S(2)}) collective-permute-start(bf16[2,12,128,128]{3,2,1,0:T(8,128)(2,1)S(1)} %add.190), channel_id=1, source_target_pairs={{0,4},{4,8},{8,12},{5,1},{9,5},{13,9},{2,6},{6,10},{10,14},{7,3},{... | collective-permute-start | bytes 2359304 | tf_op jit(solution)/shard_map/ppermute | solution.py:370
  213.3 5.1 %decode.2 = (bf16[256,2048]{1,0:T(8,128)(2,1)S(1)}, bf16[256,2048]{1,0:T(8,128)(2,1)S(1)}) custom-call(s32[8,16]{1,0:T(8,128)S(1)} %get-tuple-element.72.tab_j, s32[8,16]{1,0:T(8,128)S(1)} %get-tuple-element.73.tab_m, s32[3]{0:T(128)S(1)} %pad_add_fusion.1.meta, bf16[2,12,128,128]{3,2,1,0:T(8,128)(2,1)S(1)} %add.183.refs_0_, ...), custom_call_target="tpu_custom_call" | custom-call | flops 4294967296 | bytes 12582912 | tf_op jit(solution)/shard_map/decode/pallas_call | solution.py:312
  218.8 5.3 %collective-permute-done.33.refs_1_ = bf16[2,12,128,128]{3,2,1,0:T(8,128)(2,1)S(1)} collective-permute-done((bf16[2,12,128,128]{3,2,1,0:T(8,128)(2,1)S(1)}, bf16[2,12,128,128]{3,2,1,0:T(8,128)(2,1)S(1)}, u32[]{:S(2)}, u32[]{:S(2)}) %collective-permute-start.33) | collective-permute-done | bytes 786464 | tf_op jit(solution)/shard_map/ppermute | solution.py:370
  224.7 4.7 %collective-permute-start.55 = (bf16[2,12,128,128]{3,2,1,0:T(8,128)(2,1)S(1)}, bf16[2,12,128,128]{3,2,1,0:T(8,128)(2,1)S(1)}, u32[]{:S(2)}, u32[]{:S(2)}) collective-permute-start(bf16[2,12,128,128]{3,2,1,0:T(8,128)(2,1)S(1)} %add.192.refs_7_), channel_id=1, source_target_pairs={{0,4},{4,8},{8,12},{5,1},{9,5},{13,9},{2,6},{6,10},{10,14},{7,3},{... | collective-permute-start | bytes 2359304 | tf_op jit(solution)/shard_map/ppermute | solution.py:370
  239.6 7.7 %collective-permute-done.43.refs_1_ = bf16[2,12,128,128]{3,2,1,0:T(8,128)(2,1)S(1)} collective-permute-done((bf16[2,12,128,128]{3,2,1,0:T(8,128)(2,1)S(1)}, bf16[2,12,128,128]{3,2,1,0:T(8,128)(2,1)S(1)}, u32[]{:S(2)}, u32[]{:S(2)}) %collective-permute-start.43) | collective-permute-done | bytes 786464 | tf_op jit(solution)/shard_map/ppermute | solution.py:370
  248.2 5.3 %collective-permute-done.57.refs_1_ = bf16[256,2048]{1,0:T(8,128)(2,1)S(1)} collective-permute-done((bf16[256,2048]{1,0:T(8,128)(2,1)S(1)}, bf16[256,2048]{1,0:T(8,128)(2,1)S(1)}, u32[]{:S(2)}, u32[]{:S(2)}) %collective-permute-start.57) | collective-permute-done | bytes 1048608 | tf_op jit(solution)/shard_map/ppermute | solution.py:472
  253.5 5.3 %backward.1 = (f32[16,512]{1,0:T(8,128)S(1)}, f32[16,227]{1,0:T(8,128)S(1)}) custom-call(s32[2]{0:T(128)S(1)} %fusion.6.offs, bf16[256,2048]{1,0:T(8,128)(2,1)S(1)} %get-tuple-element.55.refs_2_.refs_0_, bf16[256,2048]{1,0:T(8,128)(2,1)S(1)} %collective-permute-done.57.refs_1_, f32[512,2048]{1,0:T(8,128)S(1)} %copy-done.2, f32[512,2048]{1,0:T(8,128)S(1)} %copy-done.4, ...), custom_call_target="tpu_custom_call" | custom-call | flops 1073741824 | bytes 10485760 | tf_op jit(solution)/shard_map/backward/pallas_call | solution.py:161
  269.9 4.5 %collective-permute-start.61 = (f32[16,739]{1,0:T(8,128)S(1)}, f32[16,739]{1,0:T(8,128)S(1)}, u32[]{:S(2)}, u32[]{:S(2)}) collective-permute-start(f32[16,739]{1,0:T(8,128)S(1)} %add.136), channel_id=1, source_target_pairs={{0,8},{4,12},{8,0},{12,4},{1,9},{5,13},{9,1},{13,5},{2,10},{6,14},... | collective-permute-start | bytes 141896 | tf_op jit(solution)/shard_map/ppermute | solution.py:387
  280.7 9.6 %collective-permute-start.48 = (bf16[2,12,128,128]{3,2,1,0:T(8,128)(2,1)S(1)}, bf16[2,12,128,128]{3,2,1,0:T(8,128)(2,1)S(1)}, u32[]{:S(2)}, u32[]{:S(2)}) collective-permute-start(bf16[2,12,128,128]{3,2,1,0:T(8,128)(2,1)S(1)} %collective-permute-done.45.refs_3_), channel_id=1, source_target_pairs={{0,1},{1,0},{2,3},{3,2},{4,5},{5,4},{6,7},{7,6},{8,9},{9,8},{10,11... | collective-permute-start | bytes 2359304 | tf_op jit(solution)/shard_map/ppermute | solution.py:341
  290.3 8.4 %collective-permute-start.65 = (bf16[2,12,128,128]{3,2,1,0:T(8,128)(2,1)S(1)}, bf16[2,12,128,128]{3,2,1,0:T(8,128)(2,1)S(1)}, u32[]{:S(2)}, u32[]{:S(2)}) collective-permute-start(bf16[2,12,128,128]{3,2,1,0:T(8,128)(2,1)S(1)} %collective-permute-done.62.refs_10_), channel_id=1, source_target_pairs={{0,1},{1,0},{2,3},{3,2},{4,5},{5,4},{6,7},{7,6},{8,9},{9,8},{10,11... | collective-permute-start | bytes 2359304 | tf_op jit(solution)/shard_map/ppermute | solution.py:341
  300.6 6.4 %decode.3 = bf16[256,4096]{1,0:T(8,128)(2,1)} custom-call(s32[8,16]{1,0:T(8,128)S(1)} %get-tuple-element.72.tab_j, s32[8,16]{1,0:T(8,128)S(1)} %get-tuple-element.73.tab_m, s32[3]{0:T(128)S(1)} %pad_add_fusion.1.meta, bf16[2,12,128,128]{3,2,1,0:T(8,128)(2,1)S(1)} %add.188.refs_0_, bf16[2,12,128,128]{3,2,1,0:T(8,128)(2,1)S(1)} %collective-permute-done.43.refs_1_, ...), custom_call_target="tpu_custom_call" | custom-call | flops 4294967296 | bytes 12582912 | tf_op jit(solution)/shard_map/decode/pallas_call | solution.py:312
  (219 shorter events, 144.7 us)
Async XLA Ops:
  5.7 21.7 %all-to-all-start = ((bf16[8,2,128,128]{3,2,1,0:T(8,128)(2,1)}), bf16[8,2,128,128]{3,2,1,0:T(8,128)(2,1)S(1)}, u32[]{:S(2)}, u32[]{:S(2)}) async-start(bf16[8,2,128,128]{3,2,1,0:T(8,128)(2,1)} %get-tuple-element.34), calls=%async_computation | async-start | bytes 1048576 | tf_op jit(solution)/shard_map/all_to_all | solution.py:435
  27.4 20.1 %all-to-all-start.1 = ((bf16[8,2,128,128]{3,2,1,0:T(8,128)(2,1)}), bf16[8,2,128,128]{3,2,1,0:T(8,128)(2,1)S(1)}, u32[]{:S(2)}, u32[]{:S(2)}) async-start(bf16[8,2,128,128]{3,2,1,0:T(8,128)(2,1)} %get-tuple-element.40), calls=%async_computation.1 | async-start | bytes 1048576 | tf_op jit(solution)/shard_map/all_to_all | solution.py:435
  31.0 20.1 %collective-permute-start.3 = (bf16[8,2,128,128]{3,2,1,0:T(8,128)(2,1)S(1)}, bf16[8,2,128,128]{3,2,1,0:T(8,128)(2,1)S(1)}, u32[]{:S(2)}, u32[]{:S(2)}) collective-permute-start(bf16[8,2,128,128]{3,2,1,0:T(8,128)(2,1)S(1)} %all-to-all-done.refs_1_.refs_2_.refs_14_), channel_id=1, source_target_pairs={{0,16},{16,0},{1,17},{17,1},{2,18},{18,2},{3,19},{19,3},{4,20},{20... | collective-permute-start | bytes 1572872 | tf_op jit(solution)/shard_map/ppermute | solution.py:447
  32.6 19.2 %collective-permute-start.1 = (bf16[8,2,128,128]{3,2,1,0:T(8,128)(2,1)S(1)}, bf16[8,2,128,128]{3,2,1,0:T(8,128)(2,1)S(1)}, u32[]{:S(2)}, u32[]{:S(2)}) collective-permute-start(bf16[8,2,128,128]{3,2,1,0:T(8,128)(2,1)S(1)} %all-to-all-done.refs_1_.refs_2_.refs_14_), channel_id=1, source_target_pairs={{0,2},{2,0},{1,3},{3,1},{4,6},{6,4},{5,7},{7,5},{8,10},{10,8},{9,1... | collective-permute-start | bytes 1572872 | tf_op jit(solution)/shard_map/ppermute | solution.py:446
  51.2 18.2 %collective-permute-start.5 = (bf16[8,1,128,128]{3,2,1,0:T(8,128)(2,1)S(1)}, bf16[8,1,128,128]{3,2,1,0:T(8,128)(2,1)S(1)}, u32[]{:S(2)}, u32[]{:S(2)}) collective-permute-start(bf16[8,1,128,128]{3,2,1,0:T(8,128)(2,1)S(1)} %slice.34), channel_id=1, source_target_pairs={{0,2},{2,0},{1,3},{3,1},{4,6},{6,4},{5,7},{7,5},{8,10},{10,8},{9,1... | collective-permute-start | bytes 786440 | tf_op jit(solution)/shard_map/ppermute | solution.py:446
  86.8 25.6 %collective-permute-start = (bf16[256,2048]{1,0:T(8,128)(2,1)S(1)}, bf16[256,2048]{1,0:T(8,128)(2,1)S(1)}, u32[]{:S(2)}, u32[]{:S(2)}) collective-permute-start(bf16[256,2048]{1,0:T(8,128)(2,1)S(1)} %copy-done.12), channel_id=1, source_target_pairs={{0,2},{2,0},{1,3},{3,1},{4,6},{6,4},{5,7},{7,5},{8,10},{10,8},{9,1... | collective-permute-start | bytes 3145736 | tf_op jit(solution)/shard_map/ppermute | solution.py:472
  92.4 20.0 %collective-permute-start.9 = (bf16[2,12,128,128]{3,2,1,0:T(8,128)(2,1)S(1)}, bf16[2,12,128,128]{3,2,1,0:T(8,128)(2,1)S(1)}, u32[]{:S(2)}, u32[]{:S(2)}) collective-permute-start(bf16[2,12,128,128]{3,2,1,0:T(8,128)(2,1)S(1)} %get-tuple-element.42.refs_0_), channel_id=1, source_target_pairs={{0,1},{1,0},{2,3},{3,2},{4,5},{5,4},{6,7},{7,6},{8,9},{9,8},{10,11... | collective-permute-start | bytes 2359304 | tf_op jit(solution)/shard_map/ppermute | solution.py:341
  92.7 19.7 %collective-permute-start.13 = (bf16[2,12,128,128]{3,2,1,0:T(8,128)(2,1)S(1)}, bf16[2,12,128,128]{3,2,1,0:T(8,128)(2,1)S(1)}, u32[]{:S(2)}, u32[]{:S(2)}) collective-permute-start(bf16[2,12,128,128]{3,2,1,0:T(8,128)(2,1)S(1)} %add.174), channel_id=1, source_target_pairs={{0,4},{4,8},{9,5},{13,9},{2,6},{6,10},{11,7},{15,11},{16,20},{20,2... | collective-permute-start | bytes 2359304 | tf_op jit(solution)/shard_map/ppermute | solution.py:370
  142.5 18.8 %collective-permute-start.28 = (bf16[2,12,128,128]{3,2,1,0:T(8,128)(2,1)S(1)}, bf16[2,12,128,128]{3,2,1,0:T(8,128)(2,1)S(1)}, u32[]{:S(2)}, u32[]{:S(2)}) collective-permute-start(bf16[2,12,128,128]{3,2,1,0:T(8,128)(2,1)S(1)} %add.183.refs_0_), channel_id=1, source_target_pairs={{0,4},{4,8},{8,12},{5,1},{9,5},{13,9},{2,6},{6,10},{10,14},{7,3},{... | collective-permute-start | bytes 2359304 | tf_op jit(solution)/shard_map/ppermute | solution.py:370
  168.5 20.2 %collective-permute-start.34 = (bf16[2,12,128,128]{3,2,1,0:T(8,128)(2,1)S(1)}, bf16[2,12,128,128]{3,2,1,0:T(8,128)(2,1)S(1)}, u32[]{:S(2)}, u32[]{:S(2)}) collective-permute-start(bf16[2,12,128,128]{3,2,1,0:T(8,128)(2,1)S(1)} %collective-permute-done.28.refs_2_.refs_1_), channel_id=1, source_target_pairs={{0,1},{1,0},{2,3},{3,2},{4,5},{5,4},{6,7},{7,6},{8,9},{9,8},{10,11... | collective-permute-start | bytes 2359304 | tf_op jit(solution)/shard_map/ppermute | solution.py:341
  169.4 19.4 %collective-permute-start.38 = (bf16[2,12,128,128]{3,2,1,0:T(8,128)(2,1)S(1)}, bf16[2,12,128,128]{3,2,1,0:T(8,128)(2,1)S(1)}, u32[]{:S(2)}, u32[]{:S(2)}) collective-permute-start(bf16[2,12,128,128]{3,2,1,0:T(8,128)(2,1)S(1)} %collective-permute-done.37.refs_9_.refs_3_), channel_id=1, source_target_pairs={{8,12},{5,1},{10,14},{7,3},{24,28},{21,17},{26,30},{23,19}} | collective-permute-start | bytes 2359304 | tf_op jit(solution)/shard_map/ppermute | solution.py:370
  177.7 20.0 %collective-permute-start.52 = (bf16[2,12,128,128]{3,2,1,0:T(8,128)(2,1)S(1)}, bf16[2,12,128,128]{3,2,1,0:T(8,128)(2,1)S(1)}, u32[]{:S(2)}, u32[]{:S(2)}) collective-permute-start(bf16[2,12,128,128]{3,2,1,0:T(8,128)(2,1)S(1)} %add.189), channel_id=1, source_target_pairs={{0,4},{4,8},{9,5},{13,9},{2,6},{6,10},{11,7},{15,11},{16,20},{20,2... | collective-permute-start | bytes 2359304 | tf_op jit(solution)/shard_map/ppermute | solution.py:370
  188.7 17.9 %collective-permute-start.40 = (bf16[2,12,128,128]{3,2,1,0:T(8,128)(2,1)S(1)}, bf16[2,12,128,128]{3,2,1,0:T(8,128)(2,1)S(1)}, u32[]{:S(2)}, u32[]{:S(2)}) collective-permute-start(bf16[2,12,128,128]{3,2,1,0:T(8,128)(2,1)S(1)} %collective-permute-done.37.refs_9_.refs_3_), channel_id=1, source_target_pairs={{0,1},{1,0},{2,3},{3,2},{4,5},{5,4},{6,7},{7,6},{8,9},{9,8},{10,11... | collective-permute-start | bytes 2359304 | tf_op jit(solution)/shard_map/ppermute | solution.py:341
  188.8 24.5 %collective-permute-start.35 = (bf16[2,12,128,128]{3,2,1,0:T(8,128)(2,1)S(1)}, bf16[2,12,128,128]{3,2,1,0:T(8,128)(2,1)S(1)}, u32[]{:S(2)}, u32[]{:S(2)}) collective-permute-start(bf16[2,12,128,128]{3,2,1,0:T(8,128)(2,1)S(1)} %collective-permute-done.30.refs_3_.refs_2_), channel_id=1, source_target_pairs={{0,1},{1,0},{2,3},{3,2},{4,5},{5,4},{6,7},{7,6},{8,9},{9,8},{10,11... | collective-permute-start | bytes 2359304 | tf_op jit(solution)/shard_map/ppermute | solution.py:341
  189.3 24.0 %collective-permute-start.41 = (bf16[2,12,128,128]{3,2,1,0:T(8,128)(2,1)S(1)}, bf16[2,12,128,128]{3,2,1,0:T(8,128)(2,1)S(1)}, u32[]{:S(2)}, u32[]{:S(2)}) collective-permute-start(bf16[2,12,128,128]{3,2,1,0:T(8,128)(2,1)S(1)} %collective-permute-done.38.refs_10_.refs_3_), channel_id=1, source_target_pairs={{0,1},{1,0},{2,3},{3,2},{4,5},{5,4},{6,7},{7,6},{8,9},{9,8},{10,11... | collective-permute-start | bytes 2359304 | tf_op jit(solution)/shard_map/ppermute | solution.py:341
  200.0 18.5 %collective-permute-start.53 = (bf16[2,12,128,128]{3,2,1,0:T(8,128)(2,1)S(1)}, bf16[2,12,128,128]{3,2,1,0:T(8,128)(2,1)S(1)}, u32[]{:S(2)}, u32[]{:S(2)}) collective-permute-start(bf16[2,12,128,128]{3,2,1,0:T(8,128)(2,1)S(1)} %add.190), channel_id=1, source_target_pairs={{0,4},{4,8},{8,12},{5,1},{9,5},{13,9},{2,6},{6,10},{10,14},{7,3},{... | collective-permute-start | bytes 2359304 | tf_op jit(solution)/shard_map/ppermute | solution.py:370
  229.7 17.6 %collective-permute-start.43 = (bf16[2,12,128,128]{3,2,1,0:T(8,128)(2,1)S(1)}, bf16[2,12,128,128]{3,2,1,0:T(8,128)(2,1)S(1)}, u32[]{:S(2)}, u32[]{:S(2)}) collective-permute-start(bf16[2,12,128,128]{3,2,1,0:T(8,128)(2,1)S(1)} %add.188.refs_0_), channel_id=1, source_target_pairs={{0,4},{4,8},{8,12},{5,1},{9,5},{13,9},{2,6},{6,10},{10,14},{7,3},{... | collective-permute-start | bytes 2359304 | tf_op jit(solution)/shard_map/ppermute | solution.py:370
  234.1 19.4 %collective-permute-start.57 = (bf16[256,2048]{1,0:T(8,128)(2,1)S(1)}, bf16[256,2048]{1,0:T(8,128)(2,1)S(1)}, u32[]{:S(2)}, u32[]{:S(2)}) collective-permute-start(bf16[256,2048]{1,0:T(8,128)(2,1)S(1)} %get-tuple-element.58), channel_id=1, source_target_pairs={{0,2},{2,0},{1,3},{3,1},{4,6},{6,4},{5,7},{7,5},{8,10},{10,8},{9,1... | collective-permute-start | bytes 3145736 | tf_op jit(solution)/shard_map/ppermute | solution.py:472
  238.8 38.2 %collective-permute-start.56 = (bf16[2,12,128,128]{3,2,1,0:T(8,128)(2,1)S(1)}, bf16[2,12,128,128]{3,2,1,0:T(8,128)(2,1)S(1)}, u32[]{:S(2)}, u32[]{:S(2)}) collective-permute-start(bf16[2,12,128,128]{3,2,1,0:T(8,128)(2,1)S(1)} %collective-permute-done.55.refs_8_), channel_id=1, source_target_pairs={{4,8},{8,12},{5,1},{9,5},{6,10},{10,14},{7,3},{11,7},{20,24},{24,2... | collective-permute-start | bytes 2359304 | tf_op jit(solution)/shard_map/ppermute | solution.py:370
  247.3 29.8 %collective-permute-start.44 = (bf16[2,12,128,128]{3,2,1,0:T(8,128)(2,1)S(1)}, bf16[2,12,128,128]{3,2,1,0:T(8,128)(2,1)S(1)}, u32[]{:S(2)}, u32[]{:S(2)}) collective-permute-start(bf16[2,12,128,128]{3,2,1,0:T(8,128)(2,1)S(1)} %collective-permute-done.43.refs_1_), channel_id=1, source_target_pairs={{4,8},{8,12},{5,1},{9,5},{6,10},{10,14},{7,3},{11,7},{20,24},{24,2... | collective-permute-start | bytes 2359304 | tf_op jit(solution)/shard_map/ppermute | solution.py:370
  278.5 21.4 %collective-permute-start.63 = (bf16[2,12,128,128]{3,2,1,0:T(8,128)(2,1)S(1)}, bf16[2,12,128,128]{3,2,1,0:T(8,128)(2,1)S(1)}, u32[]{:S(2)}, u32[]{:S(2)}) collective-permute-start(bf16[2,12,128,128]{3,2,1,0:T(8,128)(2,1)S(1)} %collective-permute-done.55.refs_8_), channel_id=1, source_target_pairs={{0,1},{1,0},{2,3},{3,2},{4,5},{5,4},{6,7},{7,6},{8,9},{9,8},{10,11... | collective-permute-start | bytes 2359304 | tf_op jit(solution)/shard_map/ppermute | solution.py:341
  280.2 19.7 %collective-permute-start.47 = (bf16[2,12,128,128]{3,2,1,0:T(8,128)(2,1)S(1)}, bf16[2,12,128,128]{3,2,1,0:T(8,128)(2,1)S(1)}, u32[]{:S(2)}, u32[]{:S(2)}) collective-permute-start(bf16[2,12,128,128]{3,2,1,0:T(8,128)(2,1)S(1)} %collective-permute-done.44.refs_2_), channel_id=1, source_target_pairs={{0,1},{1,0},{2,3},{3,2},{4,5},{5,4},{6,7},{7,6},{8,9},{9,8},{10,11... | collective-permute-start | bytes 2359304 | tf_op jit(solution)/shard_map/ppermute | solution.py:341
  280.3 19.6 %collective-permute-start.64 = (bf16[2,12,128,128]{3,2,1,0:T(8,128)(2,1)S(1)}, bf16[2,12,128,128]{3,2,1,0:T(8,128)(2,1)S(1)}, u32[]{:S(2)}, u32[]{:S(2)}) collective-permute-start(bf16[2,12,128,128]{3,2,1,0:T(8,128)(2,1)S(1)} %collective-permute-done.56.refs_9_), channel_id=1, source_target_pairs={{0,1},{1,0},{2,3},{3,2},{4,5},{5,4},{6,7},{7,6},{8,9},{9,8},{10,11... | collective-permute-start | bytes 2359304 | tf_op jit(solution)/shard_map/ppermute | solution.py:341
  280.7 19.2 %collective-permute-start.48 = (bf16[2,12,128,128]{3,2,1,0:T(8,128)(2,1)S(1)}, bf16[2,12,128,128]{3,2,1,0:T(8,128)(2,1)S(1)}, u32[]{:S(2)}, u32[]{:S(2)}) collective-permute-start(bf16[2,12,128,128]{3,2,1,0:T(8,128)(2,1)S(1)} %collective-permute-done.45.refs_3_), channel_id=1, source_target_pairs={{0,1},{1,0},{2,3},{3,2},{4,5},{5,4},{6,7},{7,6},{8,9},{9,8},{10,11... | collective-permute-start | bytes 2359304 | tf_op jit(solution)/shard_map/ppermute | solution.py:341
  (62 other events, 778.0 us)
